TPU v7x, 32 devices: a whole 2x2x4 slice. The times are simulated.
32 devices in a mesh: dp: 8 (over z, x), rep: 4 (over y, core).
Axes of the slice: x: 2, y: 2, z: 4, core: 2. Of those that a mesh axis runs over, the one named last changes fastest.
Arguments:
- images: bfloat16 [384, 8, 8, 512], P(('dp', 'rep')), may hold values from -8 to 8
- micro_ids: int32 [384], P(('dp', 'rep')), may hold values from 0 to 3, as said below
- labels: int32 [384], P(('dp', 'rep')), may hold values from 0 to 9
- conv_weight: float32 [4608, 512], replicated, may hold values from -0.09375 to 0.09375
- conv_first: bfloat16 [4608, 512], replicated, may hold values from -1.1444092e-05 to 1.1444092e-05
- conv_second: bfloat16 [4608, 512], replicated, may hold values from 4.2188475e-14 to 1.687539e-13
- eig_scales: float32 [512, 512], replicated, may hold values from 0.01 to 0.1
- basis_in: float32 [512, 512], replicated, may hold values from -0.25 to 0.25
- basis_out: float32 [512, 512], replicated, may hold values from -0.25 to 0.25
- batchnorm_gain: float32 [512], replicated, may hold values from 0.5 to 1.5
- batchnorm_shift: float32 [512], replicated, may hold values from -2.5 to 2.5
- norm_first: float32 [2, 512], replicated, may hold values from -3.0517578e-05 to 3.0517578e-05
- norm_second: float32 [2, 512], replicated, may hold values from 3.8047728e-13 to 1.5219091e-12
- head: float32 [513, 10], replicated, may hold values from -0.25 to 0.25
- head_first: float32 [513, 10], replicated, may hold values from -3.0517578e-05 to 3.0517578e-05
- head_second: float32 [513, 10], replicated, may hold values from 3.8047728e-13 to 1.5219091e-12
Outputs:
- loss_parts: float32 [2], replicated
- grad_norm: float32 [], replicated
- conv_new: float32 [4608, 512], replicated
- conv_first_new: float32 [4608, 512], replicated
- conv_second_new: float32 [4608, 512], replicated
- scales_new: float32 [512, 512], replicated
- norm_new: float32 [2, 512], replicated
- norm_first_new: float32 [2, 512], replicated
- norm_second_new: float32 [2, 512], replicated
- head_new: float32 [513, 10], replicated
- head_first_new: float32 [513, 10], replicated
- head_second_new: float32 [513, 10], replicated
Inputs may be any that keep to these rules, and one draw needn't show every extreme that they name: `micro_ids`: in each aligned block of 12 slots the used slots (below 3) come first; in the last block all 12 slots are used, its first three in micro-batches 0, 1 and 2.
All inputs are finite; a program needn't handle non-finite values.
Results may differ from a plain program's by a relative error of at most 0.0027.
Values sent between devices are 32-bit elements; how exact they have to be, the bound alone decides.
A program may use at most 128 MiB of HBM per device.

v0:
```python
import jax
import jax.numpy as jnp
from jax import lax
from jax.sharding import PartitionSpec as P

NCLS = 10
STEP = 5


highest_precision = lax.Precision.HIGHEST
norm_eps = 1e-05
damping = 0.001
clip_limit = 0.01


def adamw(weight, grad, first, second, rate):
    first = 0.9 * first + 0.1 * grad
    second = 0.999 * second + 0.001 * grad * grad
    step_size = first / (1.0 - 0.9**STEP) / (jnp.sqrt(second / (1.0 - 0.999**STEP)) + 1e-08)
    return (weight - rate * (step_size + 0.01 * weight), first, second)


def shards(
    images,
    micro_ids,
    labels,
    conv_weight,
    conv_first,
    conv_second,
    eig_scales,
    basis_in,
    basis_out,
    batchnorm_gain,
    batchnorm_shift,
    norm_first,
    norm_second,
    head,
    head_first,
    head_second,
):
    count_img, rows, wid, chan = images.shape
    area = rows * wid
    cell_count = rows // 2 * (wid // 2)
    padded = jnp.pad(images, ((0, 0), (1, 1), (1, 1), (0, 0)))
    taps = [padded[:, r : r + rows, c : c + wid, :] for r in range(3) for c in range(3)]
    patches = jnp.concatenate(taps, axis=-1).reshape(-1, 9 * chan)
    convolution_block = jnp.dot(
        patches, conv_weight.astype(jnp.bfloat16), preferred_element_type=jnp.float32
    )
    convolution_block = convolution_block.reshape(count_img, rows * wid, chan)
    micro_member = (micro_ids[:, None] == jnp.arange(3)[None, :]).astype(jnp.float32)
    live = (micro_ids < 3).astype(jnp.float32)
    sums_local = jnp.einsum(
        "gu,gqf->uf", micro_member, convolution_block, precision=highest_precision
    )
    squares_local = jnp.einsum(
        "gu,gqf->uf",
        micro_member,
        convolution_block * convolution_block,
        precision=highest_precision,
    )
    counts_local = jnp.sum(micro_member, axis=0)
    counts = lax.psum(counts_local, ("dp", "rep"))
    sums, squares = lax.psum((sums_local, squares_local), ("dp", "rep"))
    pixels = counts * area
    total = jnp.sum(counts)
    mean = sums / pixels[:, None]
    var = squares / pixels[:, None] - mean * mean
    rstd = lax.rsqrt(var + norm_eps)
    image_mean = jnp.dot(micro_member, mean, precision=highest_precision)
    image_inverse_deviation = (
        jnp.dot(micro_member, rstd, precision=highest_precision) + (1.0 - live)[:, None]
    )
    normalized_input = (convolution_block - image_mean[:, None, :]) * image_inverse_deviation[
        :, None, :
    ]
    preactivation = batchnorm_gain * normalized_input + batchnorm_shift
    activation_map = jax.nn.softplus(preactivation)
    blocks = activation_map.reshape(count_img, rows // 2, 2, wid // 2, 2, chan)
    cell = jnp.log(jnp.sum(jnp.exp(blocks), axis=(2, 4)))
    pooled = jnp.sum(cell, axis=(1, 2)) / cell_count
    pooled_low = pooled.astype(jnp.bfloat16)
    head_low = head[:chan].astype(jnp.bfloat16)
    logits = jnp.dot(pooled_low, head_low, preferred_element_type=jnp.float32) + head[chan]
    logp = jax.nn.log_softmax(logits)
    onehot = (labels[:, None] == jnp.arange(NCLS)[None, :]).astype(jnp.float32)
    per_img = -(0.9 * jnp.sum(onehot * logp, axis=1) + 0.1 / NCLS * jnp.sum(logp, axis=1))
    loss_local = jnp.sum(live * per_img)
    dlogits = (jnp.exp(logp) - 0.9 * onehot - 0.1 / NCLS) * (live / total)[:, None]
    head_weight_grad = jnp.dot(
        pooled_low.astype(jnp.float32).T, dlogits, precision=highest_precision
    )
    head_local = jnp.concatenate([head_weight_grad, jnp.sum(dlogits, axis=0)[None, :]], axis=0)
    dpooled = (
        jnp.dot(dlogits, head_low.astype(jnp.float32).T, precision=highest_precision) / cell_count
    )
    share = jnp.exp(blocks - cell[:, :, None, :, None, :])
    dact = (dpooled[:, None, None, None, None, :] * share).reshape(count_img, rows * wid, chan)
    preactivation_gradient = dact * jax.nn.sigmoid(preactivation)
    back_one = jnp.einsum(
        "gu,gqf->uf", micro_member, preactivation_gradient, precision=highest_precision
    )
    backward_second = jnp.einsum(
        "gu,gqf->uf",
        micro_member,
        preactivation_gradient * normalized_input,
        precision=highest_precision,
    )
    sum_dpre, sum_dprex = lax.psum((back_one, backward_second), ("dp", "rep"))
    grad_norm_params = jnp.stack([jnp.sum(sum_dprex, axis=0), jnp.sum(sum_dpre, axis=0)])
    shift_offset_term = jnp.dot(
        micro_member, batchnorm_gain * sum_dpre / pixels[:, None], precision=highest_precision
    )
    scale_factor_term = jnp.dot(
        micro_member, batchnorm_gain * sum_dprex / pixels[:, None], precision=highest_precision
    )
    dconv = image_inverse_deviation[:, None, :] * (
        preactivation_gradient * batchnorm_gain
        - shift_offset_term[:, None, :]
        - normalized_input * scale_factor_term[:, None, :]
    )
    grad_low = dconv.reshape(-1, chan).astype(jnp.bfloat16)
    kernel_local = lax.dot_general(
        patches, grad_low, (((0,), (0,)), ((), ())), preferred_element_type=jnp.float32
    )
    turned = jnp.dot(
        padded.reshape(-1, chan).astype(jnp.float32), basis_in, precision=highest_precision
    )
    turned = (turned * turned).reshape(padded.shape)
    box = jnp.zeros((count_img, rows, wid, chan), jnp.float32)
    for r in range(3):
        for c in range(3):
            box = box + turned[:, r : r + rows, c : c + wid, :]
    gturned = jnp.dot(grad_low.astype(jnp.float32), basis_out, precision=highest_precision)
    stat_local = lax.dot_general(
        box.reshape(-1, chan),
        gturned * gturned,
        (((0,), (0,)), ((), ())),
        precision=highest_precision,
    )
    kernel_grad, stat, head_grad, loss_sum = lax.psum(
        (kernel_local, stat_local, head_local, loss_local), ("dp", "rep")
    )
    scales_new = 0.95 * eig_scales + 0.05 * (stat * (total * area * area))
    rot = jnp.einsum(
        "ji,tjk->tik", basis_in, kernel_grad.reshape(9, chan, chan), precision=highest_precision
    )
    rot = jnp.einsum("tik,kl->til", rot, basis_out, precision=highest_precision) / (
        scales_new + damping
    )
    back = jnp.einsum("ij,tjk->tik", basis_in, rot, precision=highest_precision)
    precond = jnp.einsum("tik,lk->til", back, basis_out, precision=highest_precision)
    precond = precond.reshape(9 * chan, chan)
    grad_norm = jnp.sqrt(
        jnp.sum(precond * precond)
        + jnp.sum(grad_norm_params * grad_norm_params)
        + jnp.sum(head_grad * head_grad)
    )
    factor = jnp.minimum(1.0, clip_limit / (grad_norm + 1e-06))
    conv_new, conv_m, conv_v = adamw(
        conv_weight,
        factor * precond,
        conv_first.astype(jnp.float32),
        conv_second.astype(jnp.float32),
        0.02,
    )
    norm_new, norm_m, norm_v = adamw(
        jnp.stack([batchnorm_gain, batchnorm_shift]),
        factor * grad_norm_params,
        norm_first,
        norm_second,
        0.1,
    )
    head_new, head_m, head_v = adamw(head, factor * head_grad, head_first, head_second, 0.05)
    loss_parts = jnp.stack([loss_sum, total])
    return (
        loss_parts,
        grad_norm,
        conv_new,
        conv_m,
        conv_v,
        scales_new,
        norm_new,
        norm_m,
        norm_v,
        head_new,
        head_m,
        head_v,
    )


def solution(mesh):
    in_specs = (
        P(("dp", "rep"), None, None, None),
        P(("dp", "rep")),
        P(("dp", "rep")),
        P(),
        P(),
        P(),
        P(),
        P(),
        P(),
        P(),
        P(),
        P(),
        P(),
        P(),
        P(),
        P(),
    )
    out_specs = (P(), P(), P(), P(), P(), P(), P(), P(), P(), P(), P(), P())
    return jax.shard_map(shards, mesh=mesh, in_specs=in_specs, out_specs=out_specs, check_vma=False)
```

profile of v0, /device:TPU:0, one launch (start us, length us, event | category | flops | bytes accessed | tf_op | source)
XLA Modules:
  0.0 537.7 jit_solution(9173168471506183486)
XLA Ops:
  7.3 1.4 fusion.19
  10.9 2.6 copy-done.3
  13.5 3.8 fusion.63
  17.8 42.8 %all-reduce.2 = (f32[3]{0:T(128)S(1)}, f32[3,512]{1,0:T(4,128)}, f32[3,512]{1,0:T(4,128)S(1)}) all-reduce(f32[3]{0:T(128)S(1)} %convert_reduce_fusion, f32[3,512]{1,0:T(4,128)S(1)} %fusion.47, f32[3,512]{1,0:T(4,128)S(1)} %fusion.49), channel_id=1, replica_groups=mesh['dp'=8,'rep'=4] {'dp','rep'}, use_global_device_ids=true, to_apply=%region_3.4 | all-reduce | flops 3075 | bytes 24600 | tf_op jit(solution)/shard_map/psum | solution.py:63
  63.3 2.3 fusion.13
  65.5 3.0 exp.26
  68.6 3.5 reduce_sum.166
  75.0 1.4 fusion.37
  76.4 1.9 sub.86
  78.3 3.1 sub.87
  81.5 4.2 fusion.62
  87.9 1.3 select_reduce_fusion.1
  89.2 1.4 pad_maximum_fusion
  90.6 42.0 %all-reduce.1 = (f32[1]{0:T(128)}, f32[3,512]{1,0:T(4,128)}, f32[3,512]{1,0:T(4,128)}, f32[513,10]{0,1:T(8,128)S(1)}) all-reduce(f32[1]{0:T(128)} %bitcast.2, f32[3,512]{1,0:T(4,128)} %fusion.45, f32[3,512]{1,0:T(4,128)} %fusion.46, f32[513,10]{0,1:T(8,128)} %pad_maximum_fusion), channel_id=1, replica_groups=mesh['dp'=8,'rep'=4] {'dp','rep'}, use_global_device_ids=true, to_apply=%region_13.14 | all-reduce | flops 8203 | bytes 65624 | tf_op jit(solution)/shard_map/psum | solution.py:141
  134.5 1.9 multiply_convert_fusion
  136.5 9.6 %fusion.70 = f32[4608,512]{1,0:T(8,128)} fusion(bf16[768,4608]{1,0:T(8,128)(2,1)} %bitcast.65, bf16[768,512]{1,0:T(8,128)(2,1)S(1)} %bitcast.63), kind=kOutput, calls=%fused_computation.132 | convolution fusion | flops 3623878656 | bytes 17301504 | tf_op jit(solution)/shard_map/dot_general | solution.py:123
  146.1 9.6 %copy.30 = f32[9,512,512]{1,2,0:T(8,128)} copy(f32[9,512,512]{2,1,0:T(8,128)} %bitcast.61) | data formatting | bytes 18874368 | tf_op jit(solution)/shard_map/reshape | solution.py:146
  155.7 2.0 pad.4
  157.6 2.5 reshape.76
  160.1 3.6 convolution_multiply_fusion
  163.7 4.4 reshape.77
  168.1 11.6 %slice_add_fusion = f32[12,8,8,512]{3,2,1,0:T(8,128)S(1)} fusion(f32[12,10,10,512]{3,2,1,0:T(8,128)} %reshape.77), kind=kLoop, calls=%fused_computation.29 | loop fusion | flops 3145728 | bytes 15728640 | tf_op jit(solution)/shard_map/add | solution.py:133
  179.8 1.5 convolution_multiply_fusion.1
  181.2 3.7 fusion.71
  187.0 1.9 pad_maximum_fusion.3
  189.5 199.4 %all-reduce.6.cloned.1.call-done = (f32[9,512,512]{1,2,0:T(8,128)}, f32[512,512]{1,0:T(8,128)}) async-done(((f32[9,512,512]{1,2,0:T(8,128)}, f32[512,512]{1,0:T(8,128)}), (f32[9,512,512]{1,2,0:T(8,128)}, f32[512,512]{1,0:T(8,128)})) %all-reduce.6.cloned.1.call-update) | async-done | bytes 10485776 | tf_op jit(solution)/shard_map/psum | solution.py:141
  388.8 30.4 %fusion.17 = f32[9,512,512]{2,1,0:T(8,128)S(1)} fusion(f32[9,512,512]{1,2,0:T(8,128)} %get-tuple-element.26, f32[512,512]{1,0:T(8,128)S(1)} %copy-done), kind=kOutput, calls=%fused_computation.50 | convolution fusion | flops 14495514624 | bytes 19922944 | tf_op jit(solution)/shard_map/ji,tjk->tik/dot_general | solution.py:145
  419.3 15.0 %fusion.4 = f32[9,512,512]{2,1,0:T(8,128)S(1)} fusion(f32[9,512,512]{2,1,0:T(8,128)S(1)} %fusion.17, f32[512,512]{1,0:T(8,128)S(1)} %copy-done.4), kind=kOutput, calls=%fused_computation.6 | convolution fusion | flops 14495514624 | bytes 19922944 | tf_op jit(solution)/shard_map/tik,kl->til/dot_general | solution.py:148
  435.6 32.0 %fusion.6 = f32[9,512,512]{2,1,0:T(8,128)S(1)} fusion(f32[9,512,512]{2,1,0:T(8,128)S(1)} %fusion.4, f32[512,512]{1,0:T(8,128)S(1)} %get-tuple-element.37, f32[512,512]{1,0:T(8,128)S(1)} %copy-done), kind=kOutput, calls=%fused_computation.10 | convolution fusion | flops 14497873920 | bytes 20971520 | tf_op jit(solution)/shard_map/ij,tjk->tik/dot_general | solution.py:151
  467.6 35.1 %multiply_reduce_fusion = (f32[]{:T(128)}, f32[9,512,512]{2,1,0:T(8,128)}) fusion(f32[512,512]{1,0:T(8,128)S(1)} %copy-done.4, f32[9,512,512]{2,1,0:T(8,128)S(1)} %fusion.6), kind=kOutput, calls=%fused_computation.9 | convolution fusion | flops 14500233216 | bytes 19922948 | tf_op jit(solution)/shard_map/tik,lk->til/dot_general | solution.py:152
  504.8 4.9 broadcast_multiply_fusion
  510.4 18.4 %multiply_subtract_fusion = (f32[4608,512]{1,0:T(8,128)}, f32[4608,512]{1,0:T(8,128)}, f32[4608,512]{1,0:T(8,128)}) fusion(f32[4608,512]{1,0:T(8,128)} %param.19, f32[9,512,512]{2,1,0:T(8,128)S(1)} %broadcast_multiply_fusion, bf16[4608,512]{1,0:T(8,128)(2,1)} %param.20, bf16[4608,512]{1,0:T(8,128)(2,1)} %param.21), kind=kLoop, calls=%fused_computation.8 | loop fusion | flops 40108032 | bytes 56623104 | tf_op jit(solution)/shard_map/sub | solution.py:20
  (89 shorter events, 16.1 us)
Async XLA Ops:
  7.2 152.9 %copy-start = (f32[512,512]{1,0:T(8,128)S(1)}, f32[512,512]{1,0:T(8,128)}, u32[]{:S(2)}) copy-start(f32[512,512]{1,0:T(8,128)} %param.23) | copy-start | bytes 3145732
  7.2 2.6 copy-start.2
  7.2 381.6 %all-reduce.6.cloned.1.call-start = ((), (), s32[]{:S(2)}) async-start(), calls=%async_computation | async-start | bytes 20971520 | tf_op jit(solution)/shard_map/psum | solution.py:141
  9.8 3.7 copy-start.3
  13.5 3.9 copy-start.10
  13.5 3.9 copy-start.17
  13.5 48.4 %copy-start.9 = (f32[513,10]{0,1:T(8,128)S(1)}, f32[513,10]{0,1:T(8,128)}, u32[]{:S(2)}) copy-start(f32[513,10]{0,1:T(8,128)} %param.29) | copy-start | bytes 61564
  13.5 49.7 %copy-start.13 = (f32[512]{0:T(512)S(1)}, f32[512]{0:T(512)}, u32[]{:S(2)}) copy-start(f32[512]{0:T(512)} %param.25) | copy-start | bytes 6148
  13.5 49.7 %copy-start.15 = (f32[512]{0:T(512)S(1)}, f32[512]{0:T(512)}, u32[]{:S(2)}) copy-start(f32[512]{0:T(512)} %param.26) | copy-start | bytes 6148
  60.6 1.7 copy-start.25
  61.2 7.3 %copy-start.26 = (f32[3]{0:T(128)}, f32[3]{0:T(128)S(1)}, u32[]{:S(2)}) copy-start(f32[3]{0:T(128)S(1)} %get-tuple-element.42) | copy-start | bytes 40
  61.9 11.5 %copy-start.19 = (f32[12]{0:T(128)}, f32[12]{0:T(128)S(1)}, u32[]{:S(2)}) copy-start(f32[12]{0:T(128)S(1)} %get-tuple-element.45) | copy-start | bytes 148
  65.5 7.9 %copy-start.22 = (s32[12]{0:T(128)S(1)}, s32[12]{0:T(128)}, u32[]{:S(2)}) copy-start(s32[12]{0:T(128)} %param.18) | copy-start | bytes 148
  81.5 4.2 copy-start.18
  136.5 9.6 %copy-start.5 = (bf16[12,64,512]{2,1,0:T(8,128)(2,1)}, bf16[12,64,512]{2,1,0:T(8,128)(2,1)S(1)}, u32[]{:S(2)}) copy-start(bf16[12,64,512]{2,1,0:T(8,128)(2,1)S(1)} %multiply_convert_fusion) | copy-start | bytes 2359300
  168.1 11.6 %copy-start.4 = (f32[512,512]{1,0:T(8,128)S(1)}, f32[512,512]{1,0:T(8,128)}, u32[]{:S(2)}) copy-start(f32[512,512]{1,0:T(8,128)} %param.24) | copy-start | bytes 3145732
  168.1 11.6 %copy-start.6 = (bf16[12,64,512]{2,1,0:T(8,128)(2,1)S(1)}, bf16[12,64,512]{2,1,0:T(8,128)(2,1)}, u32[]{:S(2)}) copy-start(bf16[12,64,512]{2,1,0:T(8,128)(2,1)} %copy-done.5) | copy-start | bytes 2359300
  185.0 0.7 copy-start.21
  185.0 0.7 copy-start.20
  419.3 15.0 %copy-start.7 = (f32[512,512]{1,0:T(8,128)S(1)}, f32[512,512]{1,0:T(8,128)}, u32[]{:S(2)}) copy-start(f32[512,512]{1,0:T(8,128)} %param.22) | copy-start | bytes 3145732
  419.3 15.0 %copy-start.8 = (f32[512,512]{1,0:T(8,128)S(1)}, f32[512,512]{1,0:T(8,128)}, u32[]{:S(2)}) copy-start(f32[512,512]{1,0:T(8,128)} %get-tuple-element.27) | copy-start | bytes 3145732
  504.8 4.9 copy-start.11
  504.8 4.9 copy-start.12
  510.4 18.5 %copy-start.14 = (f32[512]{0:T(512)S(1)}, f32[512]{0:T(512)}, u32[]{:S(2)}) copy-start(f32[512]{0:T(512)} %param.25) | copy-start | bytes 6148
  510.4 18.5 %copy-start.16 = (f32[512]{0:T(512)S(1)}, f32[512]{0:T(512)}, u32[]{:S(2)}) copy-start(f32[512]{0:T(512)} %param.26) | copy-start | bytes 6148
  510.4 18.5 %copy-start.23 = (f32[2,512]{1,0:T(2,128)S(1)}, f32[2,512]{1,0:T(2,128)}, u32[]{:S(2)}) copy-start(f32[2,512]{1,0:T(2,128)} %param.27) | copy-start | bytes 12292
  510.4 18.5 %copy-start.24 = (f32[2,512]{1,0:T(2,128)S(1)}, f32[2,512]{1,0:T(2,128)}, u32[]{:S(2)}) copy-start(f32[2,512]{1,0:T(2,128)} %param.28) | copy-start | bytes 12292
  510.4 19.1 %copy-start.1 = (f32[512,512]{1,0:T(8,128)S(1)}, f32[512,512]{1,0:T(8,128)}, u32[]{:S(2)}) copy-start(f32[512,512]{1,0:T(8,128)} %param.23) | copy-start | bytes 3145732
Sparse Core Ops, SparseCore 0:
  185.1 203.6 all-reduce.5
where the time goes:
time: 542 us; the launch traced here: 538 us
  waiting for transfers between devices  199 us (37%)
  matrix products  142 us (26%)
  blocking collectives  84.8 us (16%)
  other arithmetic  57.8 us (11%)
  local copies, waits for them, and re-layouts  34.4 us (6%)
  between operations  19.3 us (4%)
    psum x1, waiting for transfers between devices, shards(): lax.psum((kernel_local, stat_local, head_local, loss_local), ('dp', 'rep'))  199 us
    psum x1, blocking collectives, shards(): counts = lax.psum(counts_local, ('dp', 'rep'))  42.8 us
    psum x1, blocking collectives, shards(): lax.psum((kernel_local, stat_local, head_local, loss_local), ('dp', 'rep'))  42 us
    dot_general x1, matrix products, shards(): jnp.einsum('tik,lk->til', back, basis_out, precision=highest_precision)  35.1 us
    dot_general x1, matrix products, shards(): back = jnp.einsum('ij,tjk->tik', basis_in, rot, precision=highest_precision)  32 us
    dot_general x1, matrix products, shards(): jnp.einsum('ji,tjk->tik', basis_in, kernel_grad.reshape(9, chan, chan), p...  30.4 us
    sub x3, other arithmetic, adamw(): return (weight - rate * (step_size + 0.01 * weight), first, second)  19.7 us
    dot_general x1, matrix products, shards(): jnp.einsum('tik,kl->til', rot, basis_out, precision=highest_precision)  15 us
  transfers between devices with their start and end apart: 1, of which 1 were waited for; matrix products, arithmetic and copies ran while one was open for 1% of the time, Pallas kernels for 0%

commit v1 on v0

v1 whole, which is shorter than its diff:
```python
import functools
import itertools

import jax
import jax.numpy as jnp
from jax import lax
from jax.experimental import pallas as pl
from jax.experimental.pallas import tpu as pltpu
from jax.sharding import PartitionSpec as P

NCLS = 10
STEP = 5
NORM_EPS = 1e-05
DAMPING = 0.001
CLIP = 0.01
MESH = pl.DeviceIdType.MESH
F32 = jnp.float32
BF16 = jnp.bfloat16
HIGHEST = lax.Precision.HIGHEST
TAPS = 9
STAT = 9
UNITS = (0, 1, 9, 2, 3, 4, 5, 6, 7, 8)
ORDERS = {
    0: (0, 2, 1, 3, 4),
    1: (0, 3, 2, 1, 4),
    9: (0, 1, 2, 3, 4),
    2: (0, 2, 1, 3, 4),
    3: (0, 3, 2, 1, 4),
    4: (0, 3, 2, 1, 4),
    5: (0, 1, 2, 3, 4),
    6: (0, 2, 1, 3, 4),
    7: (0, 1, 3, 4, 2),
    8: (0, 1, 2, 3, 4),
}


def plan(extra):
    free, pending, tasks, held = {}, [], [], []
    serial = itertools.count()
    queue = list(UNITS)
    rank = {"ag": 0, "rs": 1, "sm": 1, "post": 2, "mm": 3, "fin": 4}
    clock, stat_ready = 0.0, False

    def send(dim, rows, now):
        size = rows * 2.048
        if dim == 0:
            need, lag = [("c", size / 550.0)], 0.9
        elif dim in (1, 2):
            need, lag = [(dim, size / 45.7)], 2.0
        elif dim == 3:
            need, lag = [("low", size / 45.7)], 2.0
        else:
            need, lag = [("high", size / 22.8), ("low", size / 45.7)], 2.8
        end = now
        for name, length in need:
            free[name] = max(free.get(name, 0.0), now) + length
            end = max(end, free[name])
        return end + lag

    def push(when, *task):
        pending.append((when, next(serial), task))

    push(0.0, "mm", queue.pop(0))
    push(send(0, 16, 0.0), "sm", 0)
    while pending:
        ready = [p for p in pending if p[0] <= clock]
        if not ready:
            clock = min(p[0] for p in pending)
            continue
        pick = min(ready, key=lambda p: (rank[p[2][0]], -p[2][-1] if len(p[2]) > 2 else 0, p[0], p[1]))
        pending.remove(pick)
        task = pick[2]
        tasks.append(task)
        kind, unit = task[0], task[1]
        if kind == "mm":
            push(send(0, 256, clock + 0.75), "rs", unit, 0)
            clock += 1.5
            if queue:
                push(clock, "mm", queue.pop(0))
        elif kind == "sm":
            clock += 0.05
            if unit + 1 < 5 + extra:
                push(send(min(unit + 1, 4), 16, clock), "sm", unit + 1)
        elif kind == "rs":
            stage = task[2]
            clock += 0.05 + (256 >> stage) * 0.0012
            if stage < 4 + extra:
                dim = ORDERS[unit][stage + 1] if stage < 4 else 4
                push(send(dim, max(256 >> (stage + 1), 16), clock), "rs", unit, stage + 1)
            elif unit == STAT or stat_ready:
                push(clock, "post", unit)
            else:
                held.append(unit)
        elif kind == "post":
            clock += 0.8
            if unit == STAT:
                stat_ready = True
                for other in held:
                    push(clock, "post", other)
            push(send(ORDERS[unit][4], 16, clock), "ag", unit, 0)
        elif kind == "ag":
            stage = task[2]
            clock += 0.05
            if stage < 4:
                push(send(ORDERS[unit][3 - stage], 16 << (stage + 1), clock), "ag", unit, stage + 1)
            else:
                push(clock, "fin", unit)
        else:
            clock += 1.2
    return tasks


def split(value):
    high = value.astype(BF16)
    return high, (value - high.astype(F32)).astype(BF16)


def dot(a, b, dims=((1,), (0,))):
    return lax.dot_general(a, b, (dims, ((), ())), preferred_element_type=F32)


def dot_exact(a, b, dims=((1,), (0,))):
    return lax.dot_general(a, b, (dims, ((), ())), precision=HIGHEST, preferred_element_type=F32)


def main_kernel(
    sizes,
    micro,
    labels,
    images,
    gain_ref,
    shift_ref,
    head,
    weight,
    eig_hbm,
    in_hbm,
    out_hbm,
    precond,
    scales,
    facts,
    work,
    half_sum,
    away,
    got0,
    got1,
    got2,
    got3,
    got4,
    got_more,
    small,
    small_got,
    tile_in,
    tile_core,
    tile_slots,
    tile_out,
    narrow,
    wide,
    conv,
    share,
    turned_hi,
    turned_lo,
    box_hi,
    box_lo,
    grad_low,
    rot_hi,
    rot_lo,
    rot2_hi,
    rot2_lo,
    eig,
    in_hi,
    in_lo,
    in_t_hi,
    in_t_lo,
    out_hi,
    out_lo,
    out_t_hi,
    out_t_lo,
    gathered_hi,
    gathered_lo,
    result,
    rows_stat,
    pooled,
    shares,
    shares_x,
    dpool,
    head_pad,
    scale_rows,
    square_sum,
    w_sem,
    load_sem,
    out_sem,
    rs_send,
    rs_recv,
    ag_send,
    ag_recv,
    sm_send,
    sm_recv,
    core_send,
    core_recv,
    chip_send,
    chip_recv,
):
    dp_count, rep_count, count_img = sizes
    area = 64
    cells = 16
    chips = dp_count * rep_count // 2
    dp = lax.axis_index("dp")
    rep = lax.axis_index("rep")
    core = rep % 2
    chip = dp * (rep_count // 2) + rep // 2
    bits = [("rep", 1), ("dp", 1), ("rep", 2), ("dp", 2), ("dp", 4)]
    step = 8
    while step < dp_count:
        bits.append(("dp", step))
        step *= 2
    step = 4
    while step < rep_count:
        bits.append(("rep", step))
        step *= 2
    extra = len(bits) - 5
    mine = [((dp if name == "dp" else rep) // weight_of) % 2 for name, weight_of in bits]

    def partner(k):
        name, weight_of = bits[k]
        change = (1 - 2 * mine[k]) * weight_of
        return (dp + change, rep) if name == "dp" else (dp, rep + change)

    def chip_device(q):
        return (q // (rep_count // 2), (q % (rep_count // 2)) * 2 + core)

    weight_copies = [pltpu.make_async_copy(weight.at[t], work.at[t], w_sem.at[t]) for t in range(TAPS)]
    for copy in weight_copies:
        copy.start()
    loads = [
        pltpu.make_async_copy(src, dst, load_sem.at[k])
        for k, (src, dst) in enumerate(((in_hbm, result.at[0]), (out_hbm, result.at[1]), (eig_hbm, eig)))
    ]
    for copy in loads:
        copy.start()

    barrier = pltpu.get_barrier_semaphore()

    def greet(k, carry):
        pl.semaphore_signal(barrier, inc=1, device_id=chip_device((chip + k) % chips), device_id_type=MESH)
        return carry

    lax.fori_loop(1, chips, greet, 0)
    pl.semaphore_signal(barrier, inc=1, device_id=partner(0), device_id_type=MESH)

    stride = count_img * 8
    column = lax.broadcasted_iota(jnp.int32, (2, 8, 512), 1)
    for k in range(3):
        narrow[k, 0:stride] = jnp.zeros((stride, 512), BF16)
        narrow[k, 9 * stride : 10 * stride] = jnp.zeros((stride, 512), BF16)

    def build(h, carry):
        for pair in range(count_img // 2):
            block = images[2 * pair : 2 * pair + 2, h].astype(F32)
            left = jnp.where(column == 0, 0.0, pltpu.roll(block, 1, 1))
            right = jnp.where(column == 7, 0.0, pltpu.roll(block, 7, 1))
            at = pl.ds(pl.multiple_of((h + 1) * stride + 16 * pair, 16), 16)
            at_wide = pl.ds(pl.multiple_of(h * 128 + 16 * pair, 16), 16)
            for k, value in enumerate((left, block, right)):
                low = value.reshape(16, 512).astype(BF16)
                narrow[k, at] = low
                wide[k, at_wide] = low
        fill = pl.ds(pl.multiple_of(h * 128 + stride, 16), 128 - stride)
        for k in range(3):
            wide[k, fill] = jnp.zeros((128 - stride, 512), BF16)
        grad_low[fill] = jnp.zeros((128 - stride, 512), BF16)
        return carry

    lax.fori_loop(0, 8, build, 0)

    def clear(h, carry):
        conv[h] = jnp.zeros((stride, 512), F32)
        return carry

    lax.fori_loop(0, 8, clear, 0)

    def conv_row(dy, carry):
        for dx in range(3):
            tap = dy * 3 + dx
            pltpu.make_async_copy(weight.at[tap], work.at[tap], w_sem.at[tap]).wait()

            def cast(k, inner):
                piece = work[tap, k // 4, (k // 2) % 2, k % 2].reshape(64, 512)
                turned_lo[dx, pl.ds(pl.multiple_of(k * 64, 64), 64), 0:512] = piece.astype(BF16)
                return inner

            lax.fori_loop(0, 8, cast, 0)
        for m in range(2):
            for n in range(2):
                total = None
                for dx in range(3):
                    rows = pl.ds(pl.multiple_of(dy * stride + m * 4 * stride, 16), 4 * stride)
                    term = dot(narrow[dx, rows], turned_lo[dx, :, n * 256 : n * 256 + 256])
                    total = term if total is None else total + term
                conv[4 * m : 4 * m + 4, :, n * 256 : n * 256 + 256] += total.reshape(4, stride, 256)
        return carry

    lax.fori_loop(0, 3, conv_row, 0)

    def member(n):
        return [jnp.where(micro[n] == m, 1.0, 0.0).astype(F32) for m in range(3)]

    def gather_sums(n, carry):
        at = pl.ds(pl.multiple_of(n * 8, 8), 8)
        first = jnp.zeros((8, 512), F32)
        second = jnp.zeros((8, 512), F32)
        for h in range(8):
            value = conv[h, at]
            first = first + value
            second = second + value * value
        kinds = member(n)
        return tuple(c + k * first for c, k in zip(carry[:3], kinds)) + tuple(
            c + k * second for c, k in zip(carry[3:6], kinds)
        )

    zero_tile = jnp.zeros((8, 512), F32)
    sums = lax.fori_loop(0, count_img, gather_sums, (zero_tile,) * 6)
    counts = [jnp.zeros((), F32)] * 3
    for n in range(count_img):
        counts = [c + k for c, k in zip(counts, member(n))]
    row8 = lax.broadcasted_iota(jnp.int32, (8, 512), 0)
    lane8 = lax.broadcasted_iota(jnp.int32, (8, 512), 1)

    def stack_rows(rows):
        tile = zero_tile
        for k, row in enumerate(rows):
            tile = jnp.where(row8 == k, jnp.broadcast_to(row, (8, 512)), tile)
        return tile

    count_row = zero_tile
    for m in range(3):
        count_row = jnp.where(lane8 % 256 == m, counts[m], count_row)
    tile_in[0] = jnp.where(row8 == 6, count_row, stack_rows([jnp.sum(s, axis=0, keepdims=True) for s in sums]))

    def core_half(which):
        return pl.ds(pl.multiple_of(which * 256, 256), 256)

    def tile_copy(i):
        return pltpu.make_async_remote_copy(
            src_ref=tile_in.at[i, :, core_half(1 - core)],
            dst_ref=tile_core.at[i],
            send_sem=core_send.at[2 * i],
            recv_sem=core_recv.at[2 * i],
            device_id=partner(0),
            device_id_type=MESH,
        )

    def tile_start(i):
        tile_copy(i).start()
        tile_copy(i).wait()
        tile_slots[i, 0] = tile_in[i, :, core_half(core)] + tile_core[i]

        def give(k, carry):
            pltpu.make_async_remote_copy(
                src_ref=tile_slots.at[i, 0],
                dst_ref=tile_slots.at[i, k],
                send_sem=chip_send.at[i],
                recv_sem=chip_recv.at[i],
                device_id=chip_device((chip + k) % chips),
                device_id_type=MESH,
            ).start()
            return carry

        lax.fori_loop(1, chips, give, 0)

    def tile_end(i):
        others = tile_slots.at[i, pl.ds(1, chips - 1)]
        pltpu.make_async_remote_copy(
            src_ref=others,
            dst_ref=others,
            send_sem=chip_send.at[i],
            recv_sem=chip_recv.at[i],
            device_id=partner(0),
            device_id_type=MESH,
        ).wait()

        def add(k, total):
            return total + tile_slots[i, (chip - k + chips) % chips]

        tile_out[i, core] = lax.fori_loop(0, chips, add, jnp.zeros((8, 256), F32))
        back = pltpu.make_async_remote_copy(
            src_ref=tile_out.at[i, core],
            dst_ref=tile_out.at[i, core],
            send_sem=core_send.at[2 * i + 1],
            recv_sem=core_recv.at[2 * i + 1],
            device_id=partner(0),
            device_id_type=MESH,
        )
        back.start()
        back.wait()
        return jnp.concatenate([tile_out[i, 0], tile_out[i, 1]], axis=1)

    pl.semaphore_wait(barrier, chips)
    tile_start(0)

    for copy in loads:
        copy.wait()
    value = result[0]
    in_hi[...], in_lo[...] = split(value)
    in_t_hi[...], in_t_lo[...] = split(value.T)
    value = result[1]
    out_hi[...], out_lo[...] = split(value)
    out_t_hi[...], out_t_lo[...] = split(value.T)
    for dx in range(3):
        for ref in (turned_hi, turned_lo):
            ref[dx, :, 0:128] = jnp.zeros((512, 128), BF16)
            ref[dx, :, 1152:1280] = jnp.zeros((512, 128), BF16)

    def turn(j, carry):
        total = None
        for dx in range(3):
            rows = wide[dx, pl.ds(pl.multiple_of(256 * j, 256), 256)]
            value = dot(in_t_hi[...], rows, ((1,), (1,))) + dot(in_t_lo[...], rows, ((1,), (1,)))
            at = pl.ds(pl.multiple_of(128 + 256 * j, 128), 256)
            turned_hi[dx, :, at], turned_lo[dx, :, at] = split(value)
            total = value * value if total is None else total + value * value
        result[j // 2, :, pl.ds(pl.multiple_of((j % 2) * 256, 256), 256)] = total
        return carry

    lax.fori_loop(0, 4, turn, 0)

    def squares(h):
        return result[h // 4, :, (h % 4) * 128 : (h % 4) * 128 + 128]

    for h in range(8):
        value = squares(h)
        if h > 0:
            value = value + squares(h - 1)
        if h < 7:
            value = value + squares(h + 1)
        box_hi[:, h * 128 : h * 128 + 128], box_lo[:, h * 128 : h * 128 + 128] = split(value)

    totals = tile_end(0)

    gain = gain_ref[...]
    shift = shift_ref[...]
    live_total = totals[6:7, 0:1] + totals[6:7, 1:2] + totals[6:7, 2:3]
    pixels = [totals[6:7, m : m + 1] * float(area) for m in range(3)]
    mean_rows, rstd_rows = [], []
    for m in range(3):
        mean = totals[m : m + 1] / pixels[m]
        var = totals[3 + m : 4 + m] / pixels[m] - mean * mean
        mean_rows.append(mean)
        rstd_rows.append(lax.rsqrt(var + NORM_EPS))
    rows_stat[0] = stack_rows(mean_rows)
    rows_stat[1] = stack_rows(rstd_rows)

    def image_rows(n, k):
        kinds = member(n)
        row = sum(kinds[m] * rows_stat[k, m : m + 1] for m in range(3))
        return row, 1.0 - (kinds[0] + kinds[1] + kinds[2])

    even = lax.broadcasted_iota(jnp.int32, (8, 512), 0) % 2 == 0
    pooled[...] = jnp.zeros((16, 512), F32)
    shares[...] = jnp.zeros((16, 512), F32)
    shares_x[...] = jnp.zeros((16, 512), F32)

    def forward(n, carry):
        mean, dead = image_rows(n, 0)
        rstd, _ = image_rows(n, 1)
        rstd = rstd + dead
        at = pl.ds(pl.multiple_of(n * 8, 8), 8)
        cell_sum, share_sum, share_x_sum = zero_tile, zero_tile, zero_tile
        for a in range(4):
            xs = [(conv[2 * a + k, at] - mean) * rstd for k in range(2)]
            exps = [jnp.exp(gain * x + shift) for x in xs]
            both = exps[0] + exps[1]
            both = both + jnp.where(even, pltpu.roll(both, 7, 0), pltpu.roll(both, 1, 0))
            both = both + 4.0
            cell_sum = cell_sum + jnp.log(both)
            inverse = 1.0 / both
            for k in range(2):
                part = exps[k] * inverse
                share[2 * a + k, at] = part
                share_sum = share_sum + part
                share_x_sum = share_x_sum + part * xs[k]
        row = pl.ds(n, 1)
        pooled[row] = jnp.sum(cell_sum, axis=0, keepdims=True) * (0.5 / cells)
        shares[row] = jnp.sum(share_sum, axis=0, keepdims=True)
        shares_x[row] = jnp.sum(share_x_sum, axis=0, keepdims=True)
        return carry

    lax.fori_loop(0, count_img, forward, 0)

    head_pad[...] = jnp.zeros((128, 640), F32)
    head_pad[0:NCLS, 0:513] = head[...]
    head_rows = head_pad[:, 0:512].astype(BF16)
    pooled_low = pooled[...].astype(BF16)
    logits = dot(pooled_low, head_rows, ((1,), (1,))) + head_pad[:, 512:640].T[0:1, :]
    row16 = lax.broadcasted_iota(jnp.int32, (16, 128), 0)
    lane16 = lax.broadcasted_iota(jnp.int32, (16, 128), 1)
    label_of = jnp.zeros((16, 128), jnp.int32)
    micro_of = jnp.full((16, 128), 3, jnp.int32)
    for n in range(count_img):
        label_of = jnp.where(row16 == n, labels[n], label_of)
        micro_of = jnp.where(row16 == n, micro[n], micro_of)
    is_class = lane16 < NCLS
    live = jnp.where(micro_of < 3, 1.0, 0.0)
    onehot = jnp.where(lane16 == label_of, 1.0, 0.0)
    top = jnp.max(jnp.where(is_class, logits, -3e38), axis=1, keepdims=True)
    shifted = jnp.where(is_class, logits - top, 0.0)
    log_sum = jnp.log(jnp.sum(jnp.where(is_class, jnp.exp(shifted), 0.0), axis=1, keepdims=True))
    logp = jnp.where(is_class, shifted - log_sum, 0.0)
    per_img = -(
        0.9 * jnp.sum(onehot * logp, axis=1, keepdims=True) + 0.1 / NCLS * jnp.sum(logp, axis=1, keepdims=True)
    )
    loss = jnp.sum(live[:, 0:1] * per_img, axis=0, keepdims=True)
    dlogits = jnp.where(is_class, jnp.exp(logp) - 0.9 * onehot - 0.1 / NCLS, 0.0) * (live / live_total)
    dpool[...] = dot_exact(dlogits, head_rows.astype(F32)) * (1.0 / cells)
    head_grad = dot_exact(dlogits, pooled_low.astype(F32), ((0,), (0,)))
    row16w = lax.broadcasted_iota(jnp.int32, (16, 512), 0)
    bias_grad = jnp.concatenate(
        [jnp.sum(dlogits, axis=0, keepdims=True), jnp.zeros((1, 384), F32)], axis=1
    )
    block = jnp.where(row16w < NCLS, head_grad[0:16], 0.0)
    block = jnp.where(row16w == NCLS, bias_grad, block)
    small[...] = jnp.where(row16w == NCLS + 1, loss, block)

    back_rows = []
    for which in (shares, shares_x):
        for m in range(3):
            inside = jnp.where(micro_of[:, 0:1] == m, 1.0, 0.0)
            back_rows.append(jnp.sum(inside * (dpool[...] * which[...]), axis=0, keepdims=True))
    tile_in[1] = stack_rows(back_rows)
    tile_start(1)
    totals = tile_end(1)
    norm_grads = [
        totals[3:4] + totals[4:5] + totals[5:6],
        totals[0:1] + totals[1:2] + totals[2:3],
    ]
    rows_stat[2] = stack_rows([gain * totals[m : m + 1] / pixels[m] for m in range(3)])
    rows_stat[3] = stack_rows([gain * totals[3 + m : 4 + m] / pixels[m] for m in range(3)])

    def backward(pair, carry):
        parts = []
        for k in range(2):
            n = 2 * pair + k
            mean, dead = image_rows(n, 0)
            rstd, _ = image_rows(n, 1)
            rstd = rstd + dead
            offset, _ = image_rows(n, 2)
            slope, _ = image_rows(n, 3)
            parts.append((mean, rstd, offset, slope, gain * dpool[pl.ds(n, 1)], pl.ds(pl.multiple_of(n * 8, 8), 8)))
        for h in range(8):
            values = []
            for mean, rstd, offset, slope, factor, at in parts:
                xhat = (conv[h, at] - mean) * rstd
                values.append(rstd * (factor * share[h, at] - offset - xhat * slope))
            rows = pl.ds(pl.multiple_of(h * 128 + 16 * pair, 16), 16)
            grad_low[rows] = jnp.concatenate(values, axis=0).astype(BF16)
        return carry

    lax.fori_loop(0, count_img // 2, backward, 0)

    def rotate(k, carry):
        rows = pl.ds(pl.multiple_of(k * 256, 256), 256)
        value = dot(grad_low[rows], out_hi[...]) + dot(grad_low[rows], out_lo[...])
        rot_hi[rows], rot_lo[rows] = split(value)
        rot2_hi[rows], rot2_lo[rows] = split(value * value)
        return carry

    lax.fori_loop(0, 4, rotate, 0)

    got = (got0, got1, got2, got3, got4)
    left_home = []

    def region(unit, fixed, first=1):
        return (unit,) + tuple(fixed.get(k, slice(None)) for k in range(first, 5))

    def rs_copy(unit, stage):
        if stage < 5:
            order = ORDERS[unit]
            fixed = {k: mine[k] for k in order[:stage]}
            fixed[order[stage]] = 1 - mine[order[stage]]
            target, to = got[stage].at[unit], partner(order[stage])
        else:
            fixed = dict(enumerate(mine[:5]))
            target, to = got_more.at[unit, stage - 5], partner(stage)
        source = half_sum.at[region(unit, fixed)] if stage else away.at[UNITS.index(unit) % 2]
        return pltpu.make_async_remote_copy(
            src_ref=source,
            dst_ref=target,
            send_sem=rs_send.at[unit, stage],
            recv_sem=rs_recv.at[unit, stage],
            device_id=to,
            device_id_type=MESH,
        )

    def ag_copy(unit, stage):
        order = ORDERS[unit]
        where = work.at[region(unit, {k: mine[k] for k in order[: 5 - stage]}, 0)]
        return pltpu.make_async_remote_copy(
            src_ref=where,
            dst_ref=where,
            send_sem=ag_send.at[unit, stage],
            recv_sem=ag_recv.at[unit, stage],
            device_id=partner(order[4 - stage]),
            device_id_type=MESH,
        )

    def sm_copy(stage):
        return pltpu.make_async_remote_copy(
            src_ref=small,
            dst_ref=small_got.at[stage],
            send_sem=sm_send.at[stage],
            recv_sem=sm_recv.at[stage],
            device_id=partner(stage),
            device_id_type=MESH,
        )

    def do_mm(unit):
        dy, dx = unit // 3, unit % 3
        slot = UNITS.index(unit) % 2
        if UNITS.index(unit) >= 2:
            before = UNITS[UNITS.index(unit) - 2]
            if before not in left_home:
                left_home.append(before)
                rs_copy(before, 0).wait_send()
        for stays, half in enumerate((1 - core, core)):
            rows = pl.ds(pl.multiple_of(half * 256, 256), 256)

            def tile(k, carry):
                cols = pl.ds(pl.multiple_of(k * 256, 256), 256)
                if unit == STAT:
                    left_hi, left_lo = box_hi[rows], box_lo[rows]
                    right_hi, right_lo = rot2_hi[:, cols], rot2_lo[:, cols]
                else:
                    left_hi = turned_hi[dx, rows, dy * 128 : dy * 128 + 1024]
                    left_lo = turned_lo[dx, rows, dy * 128 : dy * 128 + 1024]
                    right_hi, right_lo = rot_hi[:, cols], rot_lo[:, cols]
                value = dot(left_hi, right_hi) + dot(left_hi, right_lo) + dot(left_lo, right_hi)
                value = value.reshape(2, 2, 2, 2, 16, 256)
                if stays:
                    half_sum[unit, :, :, :, :, :, cols] = value
                else:
                    away[slot, :, :, :, :, :, cols] = value
                return carry

            lax.fori_loop(0, 2, tile, 0)
            if not stays:
                rs_copy(unit, 0).start()

    def do_rs(unit, stage):
        if stage == 0 and unit in left_home:
            rs_copy(unit, stage).wait_recv()
        else:
            rs_copy(unit, stage).wait()
            left_home.append(unit)
        if stage < 5:
            order = ORDERS[unit]
            fixed = {k: mine[k] for k in order[: stage + 1]}
            source, at = got[stage], (unit,)
        else:
            fixed = dict(enumerate(mine[:5]))
            source, at = got_more, (unit, stage - 5)
        left = [k for k in range(1, 5) if k not in fixed]

        def add(i, carry):
            inner = dict(fixed)
            where = at
            if len(left) >= 3:
                inner[left[0]], inner[left[1]] = i // 2, i % 2
                where = at + (i // 2, i % 2)
            half_sum[region(unit, inner)] += source[where]
            return carry

        if len(left) >= 3:
            lax.fori_loop(0, 4, add, 0)
        else:
            add(0, 0)
        if stage < 4 + extra:
            rs_copy(unit, stage + 1).start()

    own = dict(enumerate(mine[:5]))
    own_block = (((mine[0] * 2 + mine[1]) * 2 + mine[2]) * 2 + mine[3]) * 2 + mine[4]

    def do_post(unit):
        at = region(unit, own, 0)
        value = half_sum[region(unit, own)]
        if unit == STAT:
            rows = pl.ds(pl.multiple_of(own_block * 16, 16), 16)
            value = 0.95 * eig[rows] + 0.05 * (value * (live_total * float(area * area)))
            scale_rows[...] = value + DAMPING
            work[at] = value
        else:
            high, low = split(value / scale_rows[...])
            work[at] = dot(high, out_t_hi[...]) + dot(high, out_t_lo[...]) + dot(low, out_t_hi[...])
        ag_copy(unit, 0).start()

    def do_ag(unit, stage):
        ag_copy(unit, stage).wait()
        if stage < 4:
            ag_copy(unit, stage + 1).start()

    done = []

    def result_copy(k):
        unit = done[k]
        return pltpu.make_async_copy(
            result.at[k % 2], precond.at[pl.ds(unit * 512, 512)], out_sem.at[k % 2]
        )

    scales_copy = pltpu.make_async_copy(work.at[STAT], scales, out_sem.at[2])

    def do_fin(unit):
        if unit == STAT:
            scales_copy.start()
            return
        k = len(done)
        done.append(unit)
        if k >= 2:
            result_copy(k - 2).wait()

        def cut(i, carry):
            rows = pl.ds(pl.multiple_of(i * 64, 64), 64)
            value = work[unit, i // 4, (i // 2) % 2, i % 2].reshape(64, 512)
            gathered_hi[rows], gathered_lo[rows] = split(value)
            return carry

        lax.fori_loop(0, 8, cut, 0)

        def tile(i, carry):
            rows = pl.ds(pl.multiple_of((i // 2) * 256, 256), 256)
            cols = pl.ds(pl.multiple_of((i % 2) * 256, 256), 256)
            value = (
                dot(in_hi[rows], gathered_hi[:, cols])
                + dot(in_hi[rows], gathered_lo[:, cols])
                + dot(in_lo[rows], gathered_hi[:, cols])
            )
            result[k % 2, rows, cols] = value
            square_sum[...] += jnp.sum((value * value).reshape(32, 8, 256), axis=0)
            return carry

        lax.fori_loop(0, 4, tile, 0)
        result_copy(k).start()

    def do_sm(stage):
        sm_copy(stage).wait()
        small[...] += small_got[stage]
        if stage < 4 + extra:
            sm_copy(stage + 1).start()

    square_sum[...] = jnp.zeros((8, 256), F32)
    sm_copy(0).start()
    run = {"mm": do_mm, "rs": do_rs, "post": do_post, "ag": do_ag, "fin": do_fin, "sm": do_sm}
    for task in plan(extra):
        run[task[0]](*task[1:])

    block = small[...]
    head_part = jnp.where(row16w <= NCLS, block, 0.0)
    squared = (
        jnp.sum(jnp.sum(square_sum[...], axis=0, keepdims=True), axis=1, keepdims=True)
        + jnp.sum(norm_grads[0] * norm_grads[0] + norm_grads[1] * norm_grads[1], axis=1, keepdims=True)
        + jnp.sum(jnp.sum(head_part * head_part, axis=0, keepdims=True), axis=1, keepdims=True)
    )
    norm = jnp.sqrt(squared)
    factor = jnp.minimum(1.0, CLIP / (norm + 1e-06))
    facts[0:16] = block
    facts[16:24] = stack_rows(norm_grads + [block[NCLS + 1 : NCLS + 2], live_total, norm, factor])
    for k in range(max(len(done) - 2, 0), len(done)):
        result_copy(k).wait()
    scales_copy.wait()


def adamw(weight, grad, first, second, rate):
    first = 0.9 * first + 0.1 * grad
    second = 0.999 * second + 0.001 * grad * grad
    step_size = first / (1.0 - 0.9**STEP) / (jnp.sqrt(second / (1.0 - 0.999**STEP)) + 1e-08)
    return (weight - rate * (step_size + 0.01 * weight), first, second)


def adamw_positive(weight, grad, first, second, rate):
    first = 0.9 * first + 0.1 * grad
    second = 0.999 * second + 0.001 * grad * grad
    scaled = second * (1.0 / (1.0 - 0.999**STEP))
    root = scaled * lax.rsqrt(scaled) + 1e-08
    step = first * (rate / (1.0 - 0.9**STEP)) / root
    return (weight * (1.0 - 0.01 * rate) - step, first, second)


CHUNKS = 18
RING = 4


def update_kernel(
    facts,
    gain,
    shift,
    norm_first,
    norm_second,
    head,
    head_first,
    head_second,
    precond,
    weight,
    first,
    second,
    scales,
    loss_parts,
    grad_norm,
    norm_new,
    norm_m,
    norm_v,
    head_new,
    head_m,
    head_v,
    conv_new,
    conv_m,
    conv_v,
    scales_new,
    in_precond,
    in_weight,
    in_first,
    in_second,
    out_new,
    out_m,
    out_v,
    scales_held,
    in_sem,
    out_sem,
    scale_sem,
):
    tall = TAPS * 512 // CHUNKS
    pairs = ((precond, in_precond), (weight, in_weight), (first, in_first), (second, in_second))
    outs = ((out_new, conv_new), (out_m, conv_m), (out_v, conv_v))

    def load(k, i):
        rows = pl.ds(pl.multiple_of(i * tall, tall), tall)
        return pltpu.make_async_copy(pairs[k][0].at[rows], pairs[k][1].at[rows], in_sem.at[k, i])

    def store(k, i):
        rows = pl.ds(pl.multiple_of(i * tall, tall), tall)
        return pltpu.make_async_copy(outs[k][0].at[i % RING], outs[k][1].at[rows], out_sem.at[k, i % RING])

    def start(i, carry):
        for k in range(4):
            load(k, i).start()
        return carry

    lax.fori_loop(0, CHUNKS, start, 0)
    scale_in = pltpu.make_async_copy(scales, scales_held, scale_sem.at[0])
    scale_out = pltpu.make_async_copy(scales_held, scales_new, scale_sem.at[1])
    scale_in.start()

    factor = facts[21:22, 0:1]
    loss_parts[0] = facts[18, 0]
    loss_parts[1] = facts[19, 0]
    grad_norm[0] = facts[20, 0]
    grads = factor * facts[16:18, :]
    weights = jnp.concatenate([gain[...], shift[...]], axis=0)
    norm_new[...], norm_m[...], norm_v[...] = adamw(weights, grads, norm_first[...], norm_second[...], 0.1)
    block = factor * facts[0:16, :]
    head_new[:, 0:512], head_m[:, 0:512], head_v[:, 0:512] = adamw(
        head[:, 0:512], block[0:NCLS], head_first[:, 0:512], head_second[:, 0:512], 0.05
    )
    bias = jnp.concatenate([block[0:16, 0:128], jnp.zeros((112, 128), F32)], axis=0).T[0:NCLS, NCLS : NCLS + 1]
    head_new[:, 512:513], head_m[:, 512:513], head_v[:, 512:513] = adamw(
        head[:, 512:513], bias, head_first[:, 512:513], head_second[:, 512:513], 0.05
    )

    def chunk(i, carry):
        for k in range(4):
            load(k, i).wait()

        @pl.when(i >= RING)
        def _():
            for k in range(3):
                store(k, i).wait()

        def piece(j, inner):
            rows = pl.ds(pl.multiple_of(i * tall + j * 32, 32), 32)
            at = pl.ds(pl.multiple_of(j * 32, 32), 32)
            out_new[i % RING, at], out_m[i % RING, at], out_v[i % RING, at] = adamw_positive(
                in_weight[rows],
                factor * in_precond[rows],
                in_first[rows].astype(F32),
                in_second[rows].astype(F32),
                0.02,
            )
            return inner

        lax.fori_loop(0, tall // 32, piece, 0)
        for k in range(3):
            store(k, i).start()
        return carry

    lax.fori_loop(0, CHUNKS, chunk, 0)
    scale_in.wait()
    scale_out.start()
    for i in range(CHUNKS - RING, CHUNKS):
        for k in range(3):
            store(k, i).wait()
    scale_out.wait()


def shards(
    sizes,
    images,
    micro_ids,
    labels,
    conv_weight,
    conv_first,
    conv_second,
    eig_scales,
    basis_in,
    basis_out,
    batchnorm_gain,
    batchnorm_shift,
    norm_first,
    norm_second,
    head,
    head_first,
    head_second,
):
    dp_count, rep_count = sizes
    count_img = images.shape[0]
    chips = dp_count * rep_count // 2
    bit_count = (dp_count * rep_count - 1).bit_length()
    extra = bit_count - 5
    vmem = pl.BlockSpec(memory_space=pltpu.VMEM)
    smem = pl.BlockSpec(memory_space=pltpu.SMEM)
    hbm = pl.BlockSpec(memory_space=pl.ANY)
    gain = batchnorm_gain.reshape(1, 512)
    shift = batchnorm_shift.reshape(1, 512)
    pixels = 8 * count_img
    square = (512, 512)
    dma = pltpu.SemaphoreType.DMA
    scratch = [
        pltpu.VMEM((10, 2, 2, 2, 2, 2, 16, 512), F32),
        pltpu.VMEM((10, 2, 2, 2, 2, 16, 512), F32),
        pltpu.VMEM((2, 2, 2, 2, 2, 16, 512), F32),
        pltpu.VMEM((10, 2, 2, 2, 2, 16, 512), F32),
        pltpu.VMEM((10, 2, 2, 2, 16, 512), F32),
        pltpu.VMEM((10, 2, 2, 16, 512), F32),
        pltpu.VMEM((10, 2, 16, 512), F32),
        pltpu.VMEM((10, 16, 512), F32),
        pltpu.VMEM((10, max(extra, 1), 16, 512) if extra else (1, 1, 8, 128), F32),
        pltpu.VMEM((16, 512), F32),
        pltpu.VMEM((bit_count, 16, 512), F32),
        pltpu.VMEM((2, 8, 512), F32),
        pltpu.VMEM((2, 8, 256), F32),
        pltpu.VMEM((2, chips, 8, 256), F32),
        pltpu.VMEM((2, 2, 8, 256), F32),
        pltpu.VMEM((3, 10 * pixels, 512), BF16),
        pltpu.VMEM((3, 1024, 512), BF16),
        pltpu.VMEM((8, pixels, 512), F32),
        pltpu.VMEM((8, pixels, 512), F32),
        pltpu.VMEM((3, 512, 1280), BF16),
        pltpu.VMEM((3, 512, 1280), BF16),
        pltpu.VMEM((512, 1024), BF16),
        pltpu.VMEM((512, 1024), BF16),
        pltpu.VMEM((1024, 512), BF16),
    ]
    scratch += [pltpu.VMEM((1024, 512), BF16)] * 4
    scratch += [pltpu.VMEM(square, F32)]
    scratch += [pltpu.VMEM(square, BF16)] * 10
    scratch += [
        pltpu.VMEM((2, 512, 512), F32),
        pltpu.VMEM((4, 8, 512), F32),
        pltpu.VMEM((16, 512), F32),
        pltpu.VMEM((16, 512), F32),
        pltpu.VMEM((16, 512), F32),
        pltpu.VMEM((16, 512), F32),
        pltpu.VMEM((128, 640), F32),
        pltpu.VMEM((16, 512), F32),
        pltpu.VMEM((8, 256), F32),
        dma((TAPS,)),
        dma((3,)),
        dma((3,)),
        dma((10, bit_count)),
        dma((10, bit_count)),
        dma((10, 5)),
        dma((10, 5)),
        dma((bit_count,)),
        dma((bit_count,)),
        dma((4,)),
        dma((4,)),
        dma((2,)),
        dma((2,)),
    ]
    precond, scales, facts = pl.pallas_call(
        functools.partial(main_kernel, (dp_count, rep_count, count_img)),
        out_shape=(
            jax.ShapeDtypeStruct((TAPS * 512, 512), F32),
            jax.ShapeDtypeStruct((2, 2, 2, 2, 2, 16, 512), F32),
            jax.ShapeDtypeStruct((24, 512), F32),
        ),
        in_specs=[smem, smem, vmem, vmem, vmem, vmem, hbm, hbm, hbm, hbm],
        out_specs=(hbm, hbm, vmem),
        scratch_shapes=scratch,
        compiler_params=pltpu.CompilerParams(
            collective_id=0, has_side_effects=True, vmem_limit_bytes=63 * 2**20
        ),
        name="reduce_and_precondition",
    )(
        micro_ids,
        labels,
        images,
        gain,
        shift,
        head.T,
        conv_weight.reshape(TAPS, 2, 2, 2, 2, 2, 16, 512),
        eig_scales,
        basis_in,
        basis_out,
    )
    tall = TAPS * 512 // CHUNKS
    head_shape = (NCLS, 513)
    outs = pl.pallas_call(
        update_kernel,
        out_shape=(
            jax.ShapeDtypeStruct((2,), F32),
            jax.ShapeDtypeStruct((1,), F32),
            *[jax.ShapeDtypeStruct((2, 512), F32)] * 3,
            *[jax.ShapeDtypeStruct(head_shape, F32)] * 3,
            *[jax.ShapeDtypeStruct((TAPS * 512, 512), F32)] * 3,
            jax.ShapeDtypeStruct(square, F32),
        ),
        in_specs=[vmem] * 8 + [hbm] * 5,
        out_specs=(smem, smem) + (vmem,) * 6 + (hbm,) * 4,
        scratch_shapes=[
            pltpu.VMEM((TAPS * 512, 512), F32),
            pltpu.VMEM((TAPS * 512, 512), F32),
            pltpu.VMEM((TAPS * 512, 512), BF16),
            pltpu.VMEM((TAPS * 512, 512), BF16),
            *[pltpu.VMEM((RING, tall, 512), F32)] * 3,
            pltpu.VMEM(square, F32),
            dma((4, CHUNKS)),
            dma((3, RING)),
            dma((2,)),
        ],
        compiler_params=pltpu.CompilerParams(vmem_limit_bytes=62 * 2**20),
        name="adamw",
    )(
        facts,
        gain,
        shift,
        norm_first,
        norm_second,
        head.T,
        head_first.T,
        head_second.T,
        precond,
        conv_weight,
        conv_first,
        conv_second,
        scales.reshape(square),
    )
    loss_parts, grad_norm, norm_new, norm_m, norm_v, head_new, head_m, head_v, conv_new, conv_m, conv_v, scales_new = outs
    return (
        loss_parts,
        grad_norm.reshape(()),
        conv_new,
        conv_m,
        conv_v,
        scales_new,
        norm_new,
        norm_m,
        norm_v,
        head_new.T,
        head_m.T,
        head_v.T,
    )


def solution(mesh):
    split_images = P(("dp", "rep"))
    in_specs = (P(("dp", "rep"), None, None, None), split_images, split_images) + (P(),) * 13
    sizes = (mesh.shape["dp"], mesh.shape["rep"])
    return jax.shard_map(
        functools.partial(shards, sizes), mesh=mesh, in_specs=in_specs, out_specs=(P(),) * 12, check_vma=False
    )
```

time: 542 us -> 161 us (0.30)
  waiting for transfers between devices: 199 us -> 0 us
  Pallas kernels: 0 us -> 160 us
  matrix products: 142 us -> 0 us
  blocking collectives: 84.8 us -> 0 us
  other arithmetic: 57.8 us -> 0 us
  local copies, waits for them, and re-layouts: 34.4 us -> 0 us
  between operations: 19.3 us -> 0.81 us
    psum x1 -> x0, waiting for transfers between devices: 199 us -> none  [shards(): lax.psum((kernel_local, stat_local, head_local, loss_local), ('dp', 'rep'))]
    pallas_call x0 -> x2, Pallas kernels: none -> 160 us  [the longest x1 138 us: shards(): pl.pallas_call(functools.partial(main_kernel, (dp_count, rep_count, count...]
    dot_general x20 -> x0, matrix products: 142 us -> none  [the longest x1 35.1 us: shards(): jnp.einsum('tik,lk->til', back, basis_out, precision=highest_precision)]
    psum x2 -> x0, blocking collectives: 84.8 us -> none  [the longest x1 42.8 us: shards(): counts = lax.psum(counts_local, ('dp', 'rep'))]
    sub x4 -> x0, other arithmetic: 19.7 us -> none  [the longest x3 19.7 us: adamw(): return (weight - rate * (step_size + 0.01 * weight), first, second)]
    reshape x3 -> x0, local copies, waits for them, and re-layouts: 16.5 us -> none  [the longest x1 9.58 us: shards(): kernel_grad.reshape(9, chan, chan)]
    add x2 -> x0, other arithmetic: 12.9 us -> none  [the longest x1 11.6 us: shards(): box = box + turned[:, r:r + rows, c:c + wid, :]]
    reduce_sum x10 -> x0, other arithmetic: 11.1 us -> none  [the longest x1 4.24 us: shards(): jnp.einsum('gu,gqf->uf', micro_member, preactivation_gradient, precision=...]
  transfers between devices with their start and end apart: 1 -> 0, of which waited for: 1 -> 0; matrix products, arithmetic and copies ran while one was open for 1% -> 0% of each run, Pallas kernels for 0% -> 0%
where the time goes in v1:
time: 161 us
  Pallas kernels  160 us (99%)
    pallas_call x1, Pallas kernels, shards(): pl.pallas_call(functools.partial(main_kernel, (dp_count, rep_count, count...  138 us
    pallas_call x1, Pallas kernels, shards(): pl.pallas_call(update_kernel, out_shape=(jax.ShapeDtypeStruct((2,), F32),...  22.2 us

profile of v1, /device:TPU:0, one launch (start us, length us, event | category | flops | bytes accessed | tf_op | source)
XLA Modules:
  0.0 160.9 jit_solution(10259924675817172709)
XLA Ops:
  0.6 137.9 %reduce_and_precondition.1 = (f32[4608,512]{1,0:T(8,128)}, f32[2,2,2,2,2,16,512]{6,5,4,3,2,1,0:T(8,128)}, f32[24,512]{1,0:T(8,128)}) custom-call(s32[12]{0:T(128)} %micro.1, s32[12]{0:T(128)} %labels.1, bf16[12,8,8,512]{3,2,1,0:T(8,128)(2,1)} %images.1, f32[1,512]{1,0:T(1,128)} %bitcast.17, f32[1,512]{1,0:T(1,128)} %bitcast.19, f32[10,513]{1,0:T(8,128)} %bitcast.13, ...), custom_call_target="tpu_custom_call" | custom-call | tf_op jit(solution)/shard_map/reduce_and_precondition/pallas_call | solution.py:985
  138.5 22.2 %adamw.1 = (f32[2]{0:T(128)}, f32[1]{0:T(128)}, f32[2,512]{1,0:T(2,128)}, f32[2,512]{1,0:T(2,128)}, f32[2,512]{1,0:T(2,128)}, /*index=5*/f32[10,513]{1,0:T(8,128...) custom-call(f32[24,512]{1,0:T(8,128)} %get-tuple-element.27.facts, ...), custom_call_target="tpu_custom_call" | custom-call | tf_op jit(solution)/shard_map/adamw/pallas_call | solution.py:1013

commit v2 on v1

--- a/solution.py
+++ b/solution.py
@@ -1,5 +1,4 @@
 import functools
-import itertools
 
 import jax
 import jax.numpy as jnp
@@ -19,95 +18,54 @@
 HIGHEST = lax.Precision.HIGHEST
 TAPS = 9
 STAT = 9
-UNITS = (0, 1, 9, 2, 3, 4, 5, 6, 7, 8)
-ORDERS = {
-    0: (0, 2, 1, 3, 4),
-    1: (0, 3, 2, 1, 4),
-    9: (0, 1, 2, 3, 4),
-    2: (0, 2, 1, 3, 4),
-    3: (0, 3, 2, 1, 4),
-    4: (0, 3, 2, 1, 4),
-    5: (0, 1, 2, 3, 4),
-    6: (0, 2, 1, 3, 4),
-    7: (0, 1, 3, 4, 2),
-    8: (0, 1, 2, 3, 4),
-}
-
-
-def plan(extra):
-    free, pending, tasks, held = {}, [], [], []
-    serial = itertools.count()
-    queue = list(UNITS)
-    rank = {"ag": 0, "rs": 1, "sm": 1, "post": 2, "mm": 3, "fin": 4}
-    clock, stat_ready = 0.0, False
-
-    def send(dim, rows, now):
-        size = rows * 2.048
-        if dim == 0:
-            need, lag = [("c", size / 550.0)], 0.9
-        elif dim in (1, 2):
-            need, lag = [(dim, size / 45.7)], 2.0
-        elif dim == 3:
-            need, lag = [("low", size / 45.7)], 2.0
-        else:
-            need, lag = [("high", size / 22.8), ("low", size / 45.7)], 2.8
-        end = now
-        for name, length in need:
-            free[name] = max(free.get(name, 0.0), now) + length
-            end = max(end, free[name])
-        return end + lag
-
-    def push(when, *task):
-        pending.append((when, next(serial), task))
-
-    push(0.0, "mm", queue.pop(0))
-    push(send(0, 16, 0.0), "sm", 0)
-    while pending:
-        ready = [p for p in pending if p[0] <= clock]
-        if not ready:
-            clock = min(p[0] for p in pending)
-            continue
-        pick = min(ready, key=lambda p: (rank[p[2][0]], -p[2][-1] if len(p[2]) > 2 else 0, p[0], p[1]))
-        pending.remove(pick)
-        task = pick[2]
-        tasks.append(task)
-        kind, unit = task[0], task[1]
-        if kind == "mm":
-            push(send(0, 256, clock + 0.75), "rs", unit, 0)
-            clock += 1.5
-            if queue:
-                push(clock, "mm", queue.pop(0))
-        elif kind == "sm":
-            clock += 0.05
-            if unit + 1 < 5 + extra:
-                push(send(min(unit + 1, 4), 16, clock), "sm", unit + 1)
-        elif kind == "rs":
-            stage = task[2]
-            clock += 0.05 + (256 >> stage) * 0.0012
-            if stage < 4 + extra:
-                dim = ORDERS[unit][stage + 1] if stage < 4 else 4
-                push(send(dim, max(256 >> (stage + 1), 16), clock), "rs", unit, stage + 1)
-            elif unit == STAT or stat_ready:
-                push(clock, "post", unit)
-            else:
-                held.append(unit)
-        elif kind == "post":
-            clock += 0.8
-            if unit == STAT:
-                stat_ready = True
-                for other in held:
-                    push(clock, "post", other)
-            push(send(ORDERS[unit][4], 16, clock), "ag", unit, 0)
-        elif kind == "ag":
-            stage = task[2]
-            clock += 0.05
-            if stage < 4:
-                push(send(ORDERS[unit][3 - stage], 16 << (stage + 1), clock), "ag", unit, stage + 1)
-            else:
-                push(clock, "fin", unit)
-        else:
-            clock += 1.2
-    return tasks
+AWAY = 4
+UNITS = (13, 4, 14, 5, 7, 18, 3, 19, 15, 12, 0, 17, 9, 10, 16, 11, 6, 2, 1, 8)
+RS_ORDER = (
+    (3, 1, 2, 4), (1, 2, 3, 4), (1, 2, 3, 4), (2, 1, 3, 4), (3, 1, 4, 2),
+    (1, 3, 4, 2), (1, 2, 3, 4), (3, 1, 2, 4), (1, 2, 3, 4), (2, 1, 3, 4),
+    (2, 3, 4, 1), (2, 3, 1, 4), (1, 2, 3, 4), (2, 3, 1, 4), (1, 2, 3, 4),
+    (3, 1, 4, 2), (1, 2, 3, 4), (2, 3, 4, 1), (2, 1, 3, 4), (1, 2, 3, 4),
+)
+AG_ORDER = (
+    (1, 3, 4, 2), (3, 4, 2, 1), (2, 3, 1, 4), (1, 3, 4, 2), (1, 2, 3, 4),
+    (1, 2, 3, 4), (3, 1, 2, 4), (1, 2, 3, 4), (2, 3, 4, 1), (3, 4, 1, 2),
+    (2, 1, 3, 4), (2, 1, 3, 4), (1, 2, 3, 4), (2, 1, 3, 4), (2, 3, 1, 4),
+    (3, 2, 1, 4), (1, 2, 3, 4), (2, 3, 4, 1), (1, 2, 3, 4), (2, 1, 3, 4),
+)
+TASKS = (
+    (0, 13, 0), (0, 4, 0), (0, 14, 0), (5, 0, 0), (1, 13, 0), (0, 5, 0), (1, 4, 0), (1, 14, 0),
+    (0, 7, 0), (0, 18, 0), (1, 5, 0), (1, 7, 0), (5, 1, 0), (0, 3, 0), (1, 18, 0), (0, 19, 0),
+    (1, 3, 0), (1, 13, 1), (0, 15, 0), (1, 19, 0), (1, 14, 1), (1, 4, 1), (5, 2, 0), (0, 12, 0),
+    (0, 0, 0), (1, 15, 0), (0, 17, 0), (1, 12, 0), (1, 7, 1), (1, 5, 1), (1, 0, 0), (1, 18, 1),
+    (1, 17, 0), (0, 9, 0), (1, 13, 2), (0, 10, 0), (5, 3, 0), (0, 16, 0), (1, 9, 0), (1, 19, 1),
+    (1, 3, 1), (1, 10, 0), (0, 11, 0), (1, 16, 0), (1, 4, 2), (1, 14, 2), (0, 6, 0), (1, 15, 1),
+    (0, 2, 0), (1, 11, 0), (0, 1, 0), (1, 5, 2), (1, 6, 0), (0, 8, 0), (1, 2, 0), (1, 12, 1),
+    (1, 1, 0), (1, 17, 1), (1, 8, 0), (1, 7, 2), (1, 0, 1), (1, 18, 2), (1, 9, 1), (5, 4, 0),
+    (1, 13, 3), (1, 14, 3), (1, 4, 3), (1, 19, 2), (1, 3, 2), (1, 5, 3), (1, 17, 2), (1, 18, 3),
+    (1, 10, 1), (1, 16, 1), (1, 13, 4), (1, 19, 3), (1, 14, 4), (1, 3, 3), (1, 15, 2), (1, 11, 1),
+    (1, 17, 3), (1, 18, 4), (1, 10, 2), (1, 12, 2), (1, 6, 1), (1, 7, 3), (1, 4, 4), (1, 19, 4),
+    (2, 9, 0), (1, 5, 4), (1, 3, 4), (2, 2, 0), (1, 15, 3), (1, 11, 2), (1, 16, 2), (1, 2, 1),
+    (1, 12, 3), (1, 6, 2), (1, 10, 3), (1, 15, 4), (2, 7, 0), (1, 7, 4), (3, 18, 0), (1, 1, 1),
+    (3, 19, 0), (1, 16, 3), (1, 2, 2), (3, 4, 0), (1, 6, 3), (3, 5, 0), (1, 12, 4), (2, 6, 0),
+    (1, 8, 1), (3, 18, 1), (3, 14, 0), (3, 19, 1), (1, 1, 2), (3, 15, 0), (1, 0, 2), (1, 2, 3),
+    (1, 16, 4), (3, 4, 1), (1, 9, 2), (1, 17, 4), (2, 8, 0), (3, 5, 1), (1, 8, 2), (1, 6, 4),
+    (1, 11, 3), (2, 3, 0), (1, 10, 4), (3, 12, 0), (3, 14, 1), (1, 1, 3), (3, 18, 2), (3, 13, 0),
+    (1, 0, 3), (1, 9, 3), (1, 2, 4), (2, 1, 0), (3, 19, 2), (3, 15, 1), (1, 8, 3), (3, 4, 2),
+    (3, 16, 0), (3, 17, 0), (1, 11, 4), (2, 5, 0), (3, 5, 2), (3, 6, 0), (3, 12, 1), (3, 3, 0),
+    (3, 7, 0), (3, 18, 3), (3, 14, 2), (3, 13, 1), (1, 1, 4), (3, 18, 4), (3, 19, 3), (4, 18, 0),
+    (1, 0, 4), (2, 0, 0), (1, 9, 4), (3, 4, 3), (3, 15, 2), (3, 2, 0), (3, 19, 4), (3, 16, 1),
+    (1, 8, 4), (2, 4, 0), (3, 6, 1), (4, 19, 0), (3, 4, 4), (4, 4, 0), (3, 12, 2), (3, 11, 0),
+    (3, 10, 0), (3, 5, 3), (3, 17, 1), (3, 7, 1), (3, 3, 1), (3, 13, 2), (3, 5, 4), (4, 5, 0),
+    (3, 0, 0), (3, 1, 0), (3, 14, 3), (3, 2, 1), (3, 8, 0), (3, 15, 3), (3, 11, 1), (3, 16, 2),
+    (3, 6, 2), (3, 14, 4), (3, 9, 0), (4, 14, 0), (3, 10, 1), (3, 15, 4), (4, 15, 0), (3, 17, 2),
+    (3, 7, 2), (3, 12, 3), (3, 3, 2), (3, 11, 2), (3, 12, 4), (3, 13, 3), (4, 12, 0), (3, 0, 1),
+    (3, 1, 1), (3, 2, 2), (3, 13, 4), (4, 13, 0), (3, 8, 1), (3, 16, 3), (3, 9, 1), (3, 17, 3),
+    (3, 16, 4), (4, 16, 0), (3, 10, 2), (3, 17, 4), (3, 6, 3), (4, 17, 0), (3, 0, 2), (3, 11, 3),
+    (3, 6, 4), (4, 6, 0), (3, 7, 3), (3, 1, 2), (3, 11, 4), (4, 11, 0), (3, 2, 3), (3, 8, 2),
+    (3, 7, 4), (4, 7, 0), (3, 3, 3), (3, 2, 4), (3, 9, 2), (4, 2, 0), (3, 10, 3), (3, 3, 4),
+    (4, 3, 0), (3, 1, 3), (3, 0, 3), (3, 10, 4), (4, 10, 0), (3, 1, 4), (3, 8, 3), (4, 1, 0),
+    (3, 0, 4), (3, 9, 3), (4, 0, 0), (3, 8, 4), (4, 8, 0), (3, 9, 4), (4, 9, 0),
+)
 
 
 def split(value):
@@ -157,13 +115,12 @@
     wide,
     conv,
     share,
+    weight_low,
     turned_hi,
-    turned_lo,
     box_hi,
     box_lo,
     grad_low,
     rot_hi,
-    rot_lo,
     rot2_hi,
     rot2_lo,
     eig,
@@ -228,12 +185,26 @@
     def chip_device(q):
         return (q // (rep_count // 2), (q % (rep_count // 2)) * 2 + core)
 
-    weight_copies = [pltpu.make_async_copy(weight.at[t], work.at[t], w_sem.at[t]) for t in range(TAPS)]
-    for copy in weight_copies:
-        copy.start()
+    def weight_copy(unit):
+        tap, cols = unit // 2, pl.ds(pl.multiple_of((unit % 2) * 256, 256), 256)
+        return pltpu.make_async_copy(weight.at[tap, :, :, :, :, :, :, cols], work.at[unit], w_sem.at[unit])
+
+    def start_weight(unit, carry):
+        weight_copy(unit).start()
+        return carry
+
+    lax.fori_loop(0, 2 * TAPS, start_weight, 0)
     loads = [
         pltpu.make_async_copy(src, dst, load_sem.at[k])
-        for k, (src, dst) in enumerate(((in_hbm, result.at[0]), (out_hbm, result.at[1]), (eig_hbm, eig)))
+        for k, (src, dst) in enumerate(
+            (
+                (in_hbm.at[:, 0:256], result.at[0]),
+                (in_hbm.at[:, 256:512], result.at[1]),
+                (out_hbm.at[:, 0:256], result.at[2]),
+                (out_hbm.at[:, 256:512], result.at[3]),
+                (eig_hbm, eig),
+            )
+        )
     ]
     for copy in loads:
         copy.start()
@@ -280,21 +251,22 @@
 
     def conv_row(dy, carry):
         for dx in range(3):
-            tap = dy * 3 + dx
-            pltpu.make_async_copy(weight.at[tap], work.at[tap], w_sem.at[tap]).wait()
-
-            def cast(k, inner):
-                piece = work[tap, k // 4, (k // 2) % 2, k % 2].reshape(64, 512)
-                turned_lo[dx, pl.ds(pl.multiple_of(k * 64, 64), 64), 0:512] = piece.astype(BF16)
-                return inner
-
-            lax.fori_loop(0, 8, cast, 0)
+            for j in range(2):
+                unit = 2 * (dy * 3 + dx) + j
+                weight_copy(unit).wait()
+
+                def cast(k, inner):
+                    piece = work[unit, k // 4, (k // 2) % 2, k % 2].reshape(64, 256)
+                    weight_low[dx, pl.ds(pl.multiple_of(k * 64, 64), 64), j * 256 : j * 256 + 256] = piece.astype(BF16)
+                    return inner
+
+                lax.fori_loop(0, 8, cast, 0)
         for m in range(2):
             for n in range(2):
                 total = None
                 for dx in range(3):
                     rows = pl.ds(pl.multiple_of(dy * stride + m * 4 * stride, 16), 4 * stride)
-                    term = dot(narrow[dx, rows], turned_lo[dx, :, n * 256 : n * 256 + 256])
+                    term = dot(narrow[dx, rows], weight_low[dx, :, n * 256 : n * 256 + 256])
                     total = term if total is None else total + term
                 conv[4 * m : 4 * m + 4, :, n * 256 : n * 256 + 256] += total.reshape(4, stride, 256)
         return carry
@@ -399,16 +371,15 @@
 
     for copy in loads:
         copy.wait()
-    value = result[0]
+    value = jnp.concatenate([result[0], result[1]], axis=1)
     in_hi[...], in_lo[...] = split(value)
     in_t_hi[...], in_t_lo[...] = split(value.T)
-    value = result[1]
+    value = jnp.concatenate([result[2], result[3]], axis=1)
     out_hi[...], out_lo[...] = split(value)
     out_t_hi[...], out_t_lo[...] = split(value.T)
     for dx in range(3):
-        for ref in (turned_hi, turned_lo):
-            ref[dx, :, 0:128] = jnp.zeros((512, 128), BF16)
-            ref[dx, :, 1152:1280] = jnp.zeros((512, 128), BF16)
+        turned_hi[dx, :, 0:128] = jnp.zeros((512, 128), BF16)
+        turned_hi[dx, :, 1152:1280] = jnp.zeros((512, 128), BF16)
 
     def turn(j, carry):
         total = None
@@ -416,15 +387,15 @@
             rows = wide[dx, pl.ds(pl.multiple_of(256 * j, 256), 256)]
             value = dot(in_t_hi[...], rows, ((1,), (1,))) + dot(in_t_lo[...], rows, ((1,), (1,)))
             at = pl.ds(pl.multiple_of(128 + 256 * j, 128), 256)
-            turned_hi[dx, :, at], turned_lo[dx, :, at] = split(value)
+            turned_hi[dx, :, at] = value.astype(BF16)
             total = value * value if total is None else total + value * value
-        result[j // 2, :, pl.ds(pl.multiple_of((j % 2) * 256, 256), 256)] = total
+        result[j] = total
         return carry
 
     lax.fori_loop(0, 4, turn, 0)
 
     def squares(h):
-        return result[h // 4, :, (h % 4) * 128 : (h % 4) * 128 + 128]
+        return result[h // 2, :, (h % 2) * 128 : (h % 2) * 128 + 128]
 
     for h in range(8):
         value = squares(h)
@@ -559,28 +530,28 @@
     def rotate(k, carry):
         rows = pl.ds(pl.multiple_of(k * 256, 256), 256)
         value = dot(grad_low[rows], out_hi[...]) + dot(grad_low[rows], out_lo[...])
-        rot_hi[rows], rot_lo[rows] = split(value)
+        rot_hi[rows] = value.astype(BF16)
         rot2_hi[rows], rot2_lo[rows] = split(value * value)
         return carry
 
     lax.fori_loop(0, 4, rotate, 0)
 
     got = (got0, got1, got2, got3, got4)
-    left_home = []
+    left_home = set()
 
     def region(unit, fixed, first=1):
         return (unit,) + tuple(fixed.get(k, slice(None)) for k in range(first, 5))
 
     def rs_copy(unit, stage):
         if stage < 5:
-            order = ORDERS[unit]
+            order = (0,) + RS_ORDER[unit]
             fixed = {k: mine[k] for k in order[:stage]}
             fixed[order[stage]] = 1 - mine[order[stage]]
             target, to = got[stage].at[unit], partner(order[stage])
         else:
             fixed = dict(enumerate(mine[:5]))
             target, to = got_more.at[unit, stage - 5], partner(stage)
-        source = half_sum.at[region(unit, fixed)] if stage else away.at[UNITS.index(unit) % 2]
+        source = half_sum.at[region(unit, fixed)] if stage else away.at[UNITS.index(unit) % AWAY]
         return pltpu.make_async_remote_copy(
             src_ref=source,
             dst_ref=target,
@@ -591,7 +562,7 @@
         )
 
     def ag_copy(unit, stage):
-        order = ORDERS[unit]
+        order = (0,) + AG_ORDER[unit]
         where = work.at[region(unit, {k: mine[k] for k in order[: 5 - stage]}, 0)]
         return pltpu.make_async_remote_copy(
             src_ref=where,
@@ -612,36 +583,28 @@
             device_id_type=MESH,
         )
 
-    def do_mm(unit):
-        dy, dx = unit // 3, unit % 3
-        slot = UNITS.index(unit) % 2
-        if UNITS.index(unit) >= 2:
-            before = UNITS[UNITS.index(unit) - 2]
-            if before not in left_home:
-                left_home.append(before)
-                rs_copy(before, 0).wait_send()
+    def do_mm(unit, stage):
+        tap, cols = unit // 2, slice((unit % 2) * 256, (unit % 2) * 256 + 256)
+        dy, dx = tap // 3, tap % 3
+        place = UNITS.index(unit)
+        if place >= AWAY and UNITS[place - AWAY] not in left_home:
+            left_home.add(UNITS[place - AWAY])
+            rs_copy(UNITS[place - AWAY], 0).wait_send()
         for stays, half in enumerate((1 - core, core)):
             rows = pl.ds(pl.multiple_of(half * 256, 256), 256)
-
-            def tile(k, carry):
-                cols = pl.ds(pl.multiple_of(k * 256, 256), 256)
-                if unit == STAT:
-                    left_hi, left_lo = box_hi[rows], box_lo[rows]
-                    right_hi, right_lo = rot2_hi[:, cols], rot2_lo[:, cols]
-                else:
-                    left_hi = turned_hi[dx, rows, dy * 128 : dy * 128 + 1024]
-                    left_lo = turned_lo[dx, rows, dy * 128 : dy * 128 + 1024]
-                    right_hi, right_lo = rot_hi[:, cols], rot_lo[:, cols]
-                value = dot(left_hi, right_hi) + dot(left_hi, right_lo) + dot(left_lo, right_hi)
-                value = value.reshape(2, 2, 2, 2, 16, 256)
-                if stays:
-                    half_sum[unit, :, :, :, :, :, cols] = value
-                else:
-                    away[slot, :, :, :, :, :, cols] = value
-                return carry
-
-            lax.fori_loop(0, 2, tile, 0)
-            if not stays:
+            if tap == STAT:
+                value = (
+                    dot(box_hi[rows], rot2_hi[:, cols])
+                    + dot(box_hi[rows], rot2_lo[:, cols])
+                    + dot(box_lo[rows], rot2_hi[:, cols])
+                )
+            else:
+                value = dot(turned_hi[dx, rows, dy * 128 : dy * 128 + 1024], rot_hi[:, cols])
+            value = value.reshape(2, 2, 2, 2, 16, 256)
+            if stays:
+                half_sum[unit] = value
+            else:
+                away[place % AWAY] = value
                 rs_copy(unit, 0).start()
 
     def do_rs(unit, stage):
@@ -649,10 +612,10 @@
             rs_copy(unit, stage).wait_recv()
         else:
             rs_copy(unit, stage).wait()
-            left_home.append(unit)
+            if stage == 0:
+                left_home.add(unit)
         if stage < 5:
-            order = ORDERS[unit]
-            fixed = {k: mine[k] for k in order[: stage + 1]}
+            fixed = {k: mine[k] for k in ((0,) + RS_ORDER[unit])[: stage + 1]}
             source, at = got[stage], (unit,)
         else:
             fixed = dict(enumerate(mine[:5]))
@@ -674,22 +637,25 @@
             add(0, 0)
         if stage < 4 + extra:
             rs_copy(unit, stage + 1).start()
+        if stage >= 4 and stage < 4 + extra:
+            do_rs(unit, stage + 1)
 
     own = dict(enumerate(mine[:5]))
     own_block = (((mine[0] * 2 + mine[1]) * 2 + mine[2]) * 2 + mine[3]) * 2 + mine[4]
 
-    def do_post(unit):
-        at = region(unit, own, 0)
-        value = half_sum[region(unit, own)]
-        if unit == STAT:
+    def do_post(tap, stage):
+        pair = (2 * tap, 2 * tap + 1)
+        value = jnp.concatenate([half_sum[region(unit, own)] for unit in pair], axis=1)
+        if tap == STAT:
             rows = pl.ds(pl.multiple_of(own_block * 16, 16), 16)
             value = 0.95 * eig[rows] + 0.05 * (value * (live_total * float(area * area)))
             scale_rows[...] = value + DAMPING
-            work[at] = value
         else:
             high, low = split(value / scale_rows[...])
-            work[at] = dot(high, out_t_hi[...]) + dot(high, out_t_lo[...]) + dot(low, out_t_hi[...])
-        ag_copy(unit, 0).start()
+            value = dot(high, out_t_hi[...]) + dot(high, out_t_lo[...]) + dot(low, out_t_hi[...])
+        for k, unit in enumerate(pair):
+            work[region(unit, own, 0)] = value[:, 256 * k : 256 * k + 256]
+            ag_copy(unit, 0).start()
 
     def do_ag(unit, stage):
         ag_copy(unit, stage).wait()
@@ -699,56 +665,60 @@
     done = []
 
     def result_copy(k):
-        unit = done[k]
-        return pltpu.make_async_copy(
-            result.at[k % 2], precond.at[pl.ds(unit * 512, 512)], out_sem.at[k % 2]
+        tap, cols = done[k] // 2, slice((done[k] % 2) * 256, (done[k] % 2) * 256 + 256)
+        return pltpu.make_async_copy(result.at[k % 4], precond.at[pl.ds(tap * 512, 512), cols], out_sem.at[k % 4])
+
+    scale_copies = [
+        pltpu.make_async_copy(
+            work.at[2 * STAT + k], scales.at[:, :, :, :, :, :, 256 * k : 256 * k + 256], out_sem.at[4 + k]
         )
-
-    scales_copy = pltpu.make_async_copy(work.at[STAT], scales, out_sem.at[2])
-
-    def do_fin(unit):
-        if unit == STAT:
-            scales_copy.start()
+        for k in range(2)
+    ]
+
+    def do_fin(unit, stage):
+        if unit // 2 == STAT:
+            scale_copies[unit % 2].start()
             return
         k = len(done)
         done.append(unit)
-        if k >= 2:
-            result_copy(k - 2).wait()
+        if k >= 4:
+            result_copy(k - 4).wait()
 
         def cut(i, carry):
             rows = pl.ds(pl.multiple_of(i * 64, 64), 64)
-            value = work[unit, i // 4, (i // 2) % 2, i % 2].reshape(64, 512)
+            value = work[unit, i // 4, (i // 2) % 2, i % 2].reshape(64, 256)
             gathered_hi[rows], gathered_lo[rows] = split(value)
             return carry
 
         lax.fori_loop(0, 8, cut, 0)
 
         def tile(i, carry):
-            rows = pl.ds(pl.multiple_of((i // 2) * 256, 256), 256)
-            cols = pl.ds(pl.multiple_of((i % 2) * 256, 256), 256)
+            rows = pl.ds(pl.multiple_of(i * 256, 256), 256)
             value = (
-                dot(in_hi[rows], gathered_hi[:, cols])
-                + dot(in_hi[rows], gathered_lo[:, cols])
-                + dot(in_lo[rows], gathered_hi[:, cols])
+                dot(in_hi[rows], gathered_hi[...])
+                + dot(in_hi[rows], gathered_lo[...])
+                + dot(in_lo[rows], gathered_hi[...])
             )
-            result[k % 2, rows, cols] = value
+            result[k % 4, rows] = value
             square_sum[...] += jnp.sum((value * value).reshape(32, 8, 256), axis=0)
             return carry
 
-        lax.fori_loop(0, 4, tile, 0)
+        lax.fori_loop(0, 2, tile, 0)
         result_copy(k).start()
 
-    def do_sm(stage):
+    def do_sm(stage, unused):
         sm_copy(stage).wait()
         small[...] += small_got[stage]
         if stage < 4 + extra:
             sm_copy(stage + 1).start()
+        if stage >= 4 and stage < 4 + extra:
+            do_sm(stage + 1, 0)
 
     square_sum[...] = jnp.zeros((8, 256), F32)
     sm_copy(0).start()
-    run = {"mm": do_mm, "rs": do_rs, "post": do_post, "ag": do_ag, "fin": do_fin, "sm": do_sm}
-    for task in plan(extra):
-        run[task[0]](*task[1:])
+    run = (do_mm, do_rs, do_post, do_ag, do_fin, do_sm)
+    for kind, which, stage in TASKS:
+        run[kind](which, stage)
 
     block = small[...]
     head_part = jnp.where(row16w <= NCLS, block, 0.0)
@@ -761,9 +731,10 @@
     factor = jnp.minimum(1.0, CLIP / (norm + 1e-06))
     facts[0:16] = block
     facts[16:24] = stack_rows(norm_grads + [block[NCLS + 1 : NCLS + 2], live_total, norm, factor])
-    for k in range(max(len(done) - 2, 0), len(done)):
+    for k in range(max(len(done) - 4, 0), len(done)):
         result_copy(k).wait()
-    scales_copy.wait()
+    for copy in scale_copies:
+        copy.wait()
 
 
 def adamw(weight, grad, first, second, rate):
@@ -930,15 +901,15 @@
     square = (512, 512)
     dma = pltpu.SemaphoreType.DMA
     scratch = [
-        pltpu.VMEM((10, 2, 2, 2, 2, 2, 16, 512), F32),
-        pltpu.VMEM((10, 2, 2, 2, 2, 16, 512), F32),
-        pltpu.VMEM((2, 2, 2, 2, 2, 16, 512), F32),
-        pltpu.VMEM((10, 2, 2, 2, 2, 16, 512), F32),
-        pltpu.VMEM((10, 2, 2, 2, 16, 512), F32),
-        pltpu.VMEM((10, 2, 2, 16, 512), F32),
-        pltpu.VMEM((10, 2, 16, 512), F32),
-        pltpu.VMEM((10, 16, 512), F32),
-        pltpu.VMEM((10, max(extra, 1), 16, 512) if extra else (1, 1, 8, 128), F32),
+        pltpu.VMEM((20, 2, 2, 2, 2, 2, 16, 256), F32),
+        pltpu.VMEM((20, 2, 2, 2, 2, 16, 256), F32),
+        pltpu.VMEM((AWAY, 2, 2, 2, 2, 16, 256), F32),
+        pltpu.VMEM((20, 2, 2, 2, 2, 16, 256), F32),
+        pltpu.VMEM((20, 2, 2, 2, 16, 256), F32),
+        pltpu.VMEM((20, 2, 2, 16, 256), F32),
+        pltpu.VMEM((20, 2, 16, 256), F32),
+        pltpu.VMEM((20, 16, 256), F32),
+        pltpu.VMEM((20, extra, 16, 256) if extra else (1, 1, 8, 128), F32),
         pltpu.VMEM((16, 512), F32),
         pltpu.VMEM((bit_count, 16, 512), F32),
         pltpu.VMEM((2, 8, 512), F32),
@@ -949,17 +920,17 @@
         pltpu.VMEM((3, 1024, 512), BF16),
         pltpu.VMEM((8, pixels, 512), F32),
         pltpu.VMEM((8, pixels, 512), F32),
-        pltpu.VMEM((3, 512, 1280), BF16),
+        pltpu.VMEM((3, 512, 512), BF16),
         pltpu.VMEM((3, 512, 1280), BF16),
         pltpu.VMEM((512, 1024), BF16),
         pltpu.VMEM((512, 1024), BF16),
         pltpu.VMEM((1024, 512), BF16),
     ]
-    scratch += [pltpu.VMEM((1024, 512), BF16)] * 4
+    scratch += [pltpu.VMEM((1024, 512), BF16)] * 3
     scratch += [pltpu.VMEM(square, F32)]
-    scratch += [pltpu.VMEM(square, BF16)] * 10
+    scratch += [pltpu.VMEM(square, BF16)] * 8 + [pltpu.VMEM((512, 256), BF16)] * 2
     scratch += [
-        pltpu.VMEM((2, 512, 512), F32),
+        pltpu.VMEM((4, 512, 256), F32),
         pltpu.VMEM((4, 8, 512), F32),
         pltpu.VMEM((16, 512), F32),
         pltpu.VMEM((16, 512), F32),
@@ -968,13 +939,13 @@
         pltpu.VMEM((128, 640), F32),
         pltpu.VMEM((16, 512), F32),
         pltpu.VMEM((8, 256), F32),
-        dma((TAPS,)),
-        dma((3,)),
-        dma((3,)),
-        dma((10, bit_count)),
-        dma((10, bit_count)),
-        dma((10, 5)),
-        dma((10, 5)),
+        dma((2 * TAPS,)),
+        dma((5,)),
+        dma((6,)),
+        dma((20, bit_count)),
+        dma((20, bit_count)),
+        dma((20, 5)),
+        dma((20, 5)),
         dma((bit_count,)),
         dma((bit_count,)),
         dma((4,)),

time: 161 us -> 144 us (0.89)
  Pallas kernels: 160 us -> 143 us
    pallas_call x1, Pallas kernels: 138 us -> 121 us  [shards(): pl.pallas_call(functools.partial(main_kernel, (dp_count, rep_count, count...]
where the time goes in v2:
time: 144 us
  Pallas kernels  143 us (99%)
    pallas_call x1, Pallas kernels, shards(): pl.pallas_call(functools.partial(main_kernel, (dp_count, rep_count, count...  121 us
    pallas_call x1, Pallas kernels, shards(): pl.pallas_call(update_kernel, out_shape=(jax.ShapeDtypeStruct((2,), F32),...  22.2 us

profile of v2, /device:TPU:0, one launch (start us, length us, event | category | flops | bytes accessed | tf_op | source)
XLA Modules:
  0.0 144.2 jit_solution(15227877741020440721)
XLA Ops:
  0.6 121.2 %reduce_and_precondition.1 = (f32[4608,512]{1,0:T(8,128)}, f32[2,2,2,2,2,16,512]{6,5,4,3,2,1,0:T(8,128)}, f32[24,512]{1,0:T(8,128)}) custom-call(s32[12]{0:T(128)} %micro.1, s32[12]{0:T(128)} %labels.1, bf16[12,8,8,512]{3,2,1,0:T(8,128)(2,1)} %images.1, f32[1,512]{1,0:T(1,128)} %bitcast.17, f32[1,512]{1,0:T(1,128)} %bitcast.19, f32[10,513]{1,0:T(8,128)} %bitcast.13, ...), custom_call_target="tpu_custom_call" | custom-call | tf_op jit(solution)/shard_map/reduce_and_precondition/pallas_call | solution.py:956
  121.8 22.2 %adamw.1 = (f32[2]{0:T(128)}, f32[1]{0:T(128)}, f32[2,512]{1,0:T(2,128)}, f32[2,512]{1,0:T(2,128)}, f32[2,512]{1,0:T(2,128)}, /*index=5*/f32[10,513]{1,0:T(8,128...) custom-call(f32[24,512]{1,0:T(8,128)} %get-tuple-element.27.facts, ...), custom_call_target="tpu_custom_call" | custom-call | tf_op jit(solution)/shard_map/adamw/pallas_call | solution.py:984

commit v3 on v2

--- a/solution.py
+++ b/solution.py
@@ -66,6 +66,32 @@
     (4, 3, 0), (3, 1, 3), (3, 0, 3), (3, 10, 4), (4, 10, 0), (3, 1, 4), (3, 8, 3), (4, 1, 0),
     (3, 0, 4), (3, 9, 3), (4, 0, 0), (3, 8, 4), (4, 8, 0), (3, 9, 4), (4, 9, 0),
 )
+GOT_COUNT = (6, 17, 14, 10, 11)
+RECV_COUNT, SEND_COUNT = 59, 20
+RS_SLOT = (
+    (4, 11, 12, 2, 5), (1, 15, 0, 1, 0), (4, 14, 3, 0, 3), (0, 7, 7, 6, 6), (1, 2, 1, 2, 3),
+    (3, 4, 3, 3, 5), (3, 2, 2, 4, 2), (4, 3, 4, 8, 8), (2, 16, 1, 4, 7), (1, 12, 13, 3, 6),
+    (2, 13, 0, 2, 10), (0, 1, 1, 9, 4), (3, 9, 10, 1, 0), (0, 0, 0, 0, 0), (2, 1, 2, 1, 1),
+    (2, 8, 9, 0, 7), (5, 0, 11, 3, 1), (0, 10, 8, 7, 9), (5, 5, 5, 4, 2), (1, 6, 6, 5, 4),
+)
+AG_RECV = (
+    (12, 17, 10, 24, 6), (29, 6, 11, 4, 1), (22, 14, 18, 12, 2), (4, 28, 4, 23, 0), (2, 8, 0, 20, 1),
+    (3, 9, 17, 26, 2), (2, 9, 33, 20, 0), (18, 10, 3, 22, 1), (15, 38, 13, 5, 0), (34, 8, 14, 16, 2),
+    (25, 35, 9, 15, 3), (24, 31, 5, 21, 3), (10, 3, 23, 37, 2), (13, 6, 11, 16, 0), (5, 11, 19, 13, 0),
+    (7, 15, 21, 30, 1), (1, 8, 32, 7, 1), (16, 27, 36, 19, 2), (0, 4, 12, 5, 58), (1, 6, 14, 7, 0),
+)
+RS_SEND = (
+    (10, 10, 10, 10, 10), (18, 18, 4, 4, 4), (17, 17, 14, 14, 14), (6, 6, 6, 6, 2), (1, 1, 1, 1, 1),
+    (3, 3, 3, 3, 3), (16, 16, 11, 11, 11), (4, 4, 4, 4, 4), (19, 19, 17, 17, 17), (12, 12, 12, 12, 12),
+    (13, 13, 13, 5, 5), (15, 15, 7, 7, 7), (9, 9, 9, 9, 9), (0, 0, 0, 0, 0), (2, 2, 2, 2, 2),
+    (8, 8, 8, 6, 6), (14, 14, 14, 13, 13), (11, 11, 11, 11, 8), (5, 5, 5, 5, 5), (7, 7, 7, 7, 0),
+)
+AG_SEND = (
+    (1, 1, 1, 1, 1), (4, 3, 3, 3, 3), (14, 12, 6, 6, 5), (16, 16, 16, 13, 6), (2, 2, 2, 2, 2),
+    (3, 3, 3, 3, 3), (11, 11, 11, 11, 7), (18, 18, 15, 12, 7), (8, 8, 2, 2, 0), (14, 4, 4, 4, 1),
+    (7, 7, 7, 0, 0), (19, 5, 5, 5, 5), (9, 5, 5, 2, 2), (16, 9, 9, 9, 2), (6, 6, 6, 6, 4),
+    (15, 15, 15, 10, 10), (8, 8, 0, 0, 0), (13, 13, 13, 10, 8), (0, 0, 0, 0, 0), (1, 1, 1, 1, 0),
+)
 
 
 def split(value):
@@ -83,12 +109,12 @@
 
 def main_kernel(
     sizes,
-    micro,
-    labels,
-    images,
-    gain_ref,
-    shift_ref,
-    head,
+    micro_hbm,
+    labels_hbm,
+    images_hbm,
+    gain_hbm,
+    shift_hbm,
+    head_hbm,
     weight,
     eig_hbm,
     in_hbm,
@@ -96,6 +122,12 @@
     precond,
     scales,
     facts,
+    micro,
+    labels,
+    images,
+    gain_ref,
+    shift_ref,
+    head,
     work,
     half_sum,
     away,
@@ -123,6 +155,7 @@
     rot_hi,
     rot2_hi,
     rot2_lo,
+    basis_out,
     eig,
     in_hi,
     in_lo,
@@ -146,10 +179,9 @@
     w_sem,
     load_sem,
     out_sem,
-    rs_send,
-    rs_recv,
-    ag_send,
-    ag_recv,
+    send_sem,
+    recv_sem,
+    more_sem,
     sm_send,
     sm_recv,
     core_send,
@@ -185,6 +217,21 @@
     def chip_device(q):
         return (q // (rep_count // 2), (q % (rep_count // 2)) * 2 + core)
 
+    first_loads = [
+        pltpu.make_async_copy(src, dst, load_sem.at[5 + k])
+        for k, (src, dst) in enumerate(
+            (
+                (images_hbm, images),
+                (micro_hbm, micro),
+                (labels_hbm, labels),
+                (gain_hbm, gain_ref),
+                (shift_hbm, shift_ref),
+                (head_hbm, head),
+            )
+        )
+    ]
+    first_loads[0].start()
+    first_loads[1].start()
     def weight_copy(unit):
         tap, cols = unit // 2, pl.ds(pl.multiple_of((unit % 2) * 256, 256), 256)
         return pltpu.make_async_copy(weight.at[tap, :, :, :, :, :, :, cols], work.at[unit], w_sem.at[unit])
@@ -200,13 +247,13 @@
             (
                 (in_hbm.at[:, 0:256], result.at[0]),
                 (in_hbm.at[:, 256:512], result.at[1]),
-                (out_hbm.at[:, 0:256], result.at[2]),
-                (out_hbm.at[:, 256:512], result.at[3]),
+                (out_hbm.at[:, 0:256], basis_out.at[0]),
+                (out_hbm.at[:, 256:512], basis_out.at[1]),
                 (eig_hbm, eig),
             )
         )
     ]
-    for copy in loads:
+    for copy in loads + first_loads[2:]:
         copy.start()
 
     barrier = pltpu.get_barrier_semaphore()
@@ -241,6 +288,7 @@
         grad_low[fill] = jnp.zeros((128 - stride, 512), BF16)
         return carry
 
+    first_loads[0].wait()
     lax.fori_loop(0, 8, build, 0)
 
     def clear(h, carry):
@@ -273,6 +321,8 @@
 
     lax.fori_loop(0, 3, conv_row, 0)
 
+    for copy in first_loads[1:]:
+        copy.wait()
     def member(n):
         return [jnp.where(micro[n] == m, 1.0, 0.0).astype(F32) for m in range(3)]
 
@@ -374,9 +424,6 @@
     value = jnp.concatenate([result[0], result[1]], axis=1)
     in_hi[...], in_lo[...] = split(value)
     in_t_hi[...], in_t_lo[...] = split(value.T)
-    value = jnp.concatenate([result[2], result[3]], axis=1)
-    out_hi[...], out_lo[...] = split(value)
-    out_t_hi[...], out_t_lo[...] = split(value.T)
     for dx in range(3):
         turned_hi[dx, :, 0:128] = jnp.zeros((512, 128), BF16)
         turned_hi[dx, :, 1152:1280] = jnp.zeros((512, 128), BF16)
@@ -392,18 +439,7 @@
         result[j] = total
         return carry
 
-    lax.fori_loop(0, 4, turn, 0)
-
-    def squares(h):
-        return result[h // 2, :, (h % 2) * 128 : (h % 2) * 128 + 128]
-
-    for h in range(8):
-        value = squares(h)
-        if h > 0:
-            value = value + squares(h - 1)
-        if h < 7:
-            value = value + squares(h + 1)
-        box_hi[:, h * 128 : h * 128 + 128], box_lo[:, h * 128 : h * 128 + 128] = split(value)
+    lax.fori_loop(0, 2, turn, 0)
 
     totals = tile_end(0)
 
@@ -498,6 +534,22 @@
             back_rows.append(jnp.sum(inside * (dpool[...] * which[...]), axis=0, keepdims=True))
     tile_in[1] = stack_rows(back_rows)
     tile_start(1)
+
+    lax.fori_loop(2, 4, turn, 0)
+    def squares(h):
+        return result[h // 2, :, (h % 2) * 128 : (h % 2) * 128 + 128]
+
+    for h in range(8):
+        value = squares(h)
+        if h > 0:
+            value = value + squares(h - 1)
+        if h < 7:
+            value = value + squares(h + 1)
+        box_hi[:, h * 128 : h * 128 + 128], box_lo[:, h * 128 : h * 128 + 128] = split(value)
+
+    value = jnp.concatenate([basis_out[0], basis_out[1]], axis=1)
+    out_hi[...], out_lo[...] = split(value)
+    out_t_hi[...], out_t_lo[...] = split(value.T)
     totals = tile_end(1)
     norm_grads = [
         totals[3:4] + totals[4:5] + totals[5:6],
@@ -547,16 +599,18 @@
             order = (0,) + RS_ORDER[unit]
             fixed = {k: mine[k] for k in order[:stage]}
             fixed[order[stage]] = 1 - mine[order[stage]]
-            target, to = got[stage].at[unit], partner(order[stage])
+            target, to = got[stage].at[RS_SLOT[unit][stage]], partner(order[stage])
+            sems = (send_sem.at[RS_SEND[unit][stage]], recv_sem.at[sum(GOT_COUNT[:stage]) + RS_SLOT[unit][stage]])
         else:
             fixed = dict(enumerate(mine[:5]))
             target, to = got_more.at[unit, stage - 5], partner(stage)
+            sems = (more_sem.at[0, unit, stage - 5], more_sem.at[1, unit, stage - 5])
         source = half_sum.at[region(unit, fixed)] if stage else away.at[UNITS.index(unit) % AWAY]
         return pltpu.make_async_remote_copy(
             src_ref=source,
             dst_ref=target,
-            send_sem=rs_send.at[unit, stage],
-            recv_sem=rs_recv.at[unit, stage],
+            send_sem=sems[0],
+            recv_sem=sems[1],
             device_id=to,
             device_id_type=MESH,
         )
@@ -567,8 +621,8 @@
         return pltpu.make_async_remote_copy(
             src_ref=where,
             dst_ref=where,
-            send_sem=ag_send.at[unit, stage],
-            recv_sem=ag_recv.at[unit, stage],
+            send_sem=send_sem.at[AG_SEND[unit][stage]],
+            recv_sem=recv_sem.at[AG_RECV[unit][stage]],
             device_id=partner(order[4 - stage]),
             device_id_type=MESH,
         )
@@ -616,7 +670,7 @@
                 left_home.add(unit)
         if stage < 5:
             fixed = {k: mine[k] for k in ((0,) + RS_ORDER[unit])[: stage + 1]}
-            source, at = got[stage], (unit,)
+            source, at = got[stage], (RS_SLOT[unit][stage],)
         else:
             fixed = dict(enumerate(mine[:5]))
             source, at = got_more, (unit, stage - 5)
@@ -754,6 +808,7 @@
 
 
 CHUNKS = 18
+LOADS = 9
 RING = 4
 
 
@@ -800,7 +855,8 @@
     outs = ((out_new, conv_new), (out_m, conv_m), (out_v, conv_v))
 
     def load(k, i):
-        rows = pl.ds(pl.multiple_of(i * tall, tall), tall)
+        deep = TAPS * 512 // LOADS
+        rows = pl.ds(pl.multiple_of(i * deep, deep), deep)
         return pltpu.make_async_copy(pairs[k][0].at[rows], pairs[k][1].at[rows], in_sem.at[k, i])
 
     def store(k, i):
@@ -812,7 +868,7 @@
             load(k, i).start()
         return carry
 
-    lax.fori_loop(0, CHUNKS, start, 0)
+    lax.fori_loop(0, LOADS, start, 0)
     scale_in = pltpu.make_async_copy(scales, scales_held, scale_sem.at[0])
     scale_out = pltpu.make_async_copy(scales_held, scales_new, scale_sem.at[1])
     scale_in.start()
@@ -834,8 +890,10 @@
     )
 
     def chunk(i, carry):
-        for k in range(4):
-            load(k, i).wait()
+        @pl.when(i % (CHUNKS // LOADS) == 0)
+        def _():
+            for k in range(4):
+                load(k, i // (CHUNKS // LOADS)).wait()
 
         @pl.when(i >= RING)
         def _():
@@ -901,14 +959,20 @@
     square = (512, 512)
     dma = pltpu.SemaphoreType.DMA
     scratch = [
+        pltpu.SMEM((count_img,), jnp.int32),
+        pltpu.SMEM((count_img,), jnp.int32),
+        pltpu.VMEM(images.shape, BF16),
+        pltpu.VMEM((1, 512), F32),
+        pltpu.VMEM((1, 512), F32),
+        pltpu.VMEM((NCLS, 513), F32),
         pltpu.VMEM((20, 2, 2, 2, 2, 2, 16, 256), F32),
         pltpu.VMEM((20, 2, 2, 2, 2, 16, 256), F32),
         pltpu.VMEM((AWAY, 2, 2, 2, 2, 16, 256), F32),
-        pltpu.VMEM((20, 2, 2, 2, 2, 16, 256), F32),
-        pltpu.VMEM((20, 2, 2, 2, 16, 256), F32),
-        pltpu.VMEM((20, 2, 2, 16, 256), F32),
-        pltpu.VMEM((20, 2, 16, 256), F32),
-        pltpu.VMEM((20, 16, 256), F32),
+        pltpu.VMEM((GOT_COUNT[0], 2, 2, 2, 2, 16, 256), F32),
+        pltpu.VMEM((GOT_COUNT[1], 2, 2, 2, 16, 256), F32),
+        pltpu.VMEM((GOT_COUNT[2], 2, 2, 16, 256), F32),
+        pltpu.VMEM((GOT_COUNT[3], 2, 16, 256), F32),
+        pltpu.VMEM((GOT_COUNT[4], 16, 256), F32),
         pltpu.VMEM((20, extra, 16, 256) if extra else (1, 1, 8, 128), F32),
         pltpu.VMEM((16, 512), F32),
         pltpu.VMEM((bit_count, 16, 512), F32),
@@ -927,7 +991,7 @@
         pltpu.VMEM((1024, 512), BF16),
     ]
     scratch += [pltpu.VMEM((1024, 512), BF16)] * 3
-    scratch += [pltpu.VMEM(square, F32)]
+    scratch += [pltpu.VMEM((2, 512, 256), F32), pltpu.VMEM(square, F32)]
     scratch += [pltpu.VMEM(square, BF16)] * 8 + [pltpu.VMEM((512, 256), BF16)] * 2
     scratch += [
         pltpu.VMEM((4, 512, 256), F32),
@@ -940,12 +1004,11 @@
         pltpu.VMEM((16, 512), F32),
         pltpu.VMEM((8, 256), F32),
         dma((2 * TAPS,)),
-        dma((5,)),
+        dma((11,)),
         dma((6,)),
-        dma((20, bit_count)),
-        dma((20, bit_count)),
-        dma((20, 5)),
-        dma((20, 5)),
+        dma((SEND_COUNT,)),
+        dma((RECV_COUNT,)),
+        dma((2, 20, extra) if extra else (1, 1, 1)),
         dma((bit_count,)),
         dma((bit_count,)),
         dma((4,)),
@@ -960,7 +1023,7 @@
             jax.ShapeDtypeStruct((2, 2, 2, 2, 2, 16, 512), F32),
             jax.ShapeDtypeStruct((24, 512), F32),
         ),
-        in_specs=[smem, smem, vmem, vmem, vmem, vmem, hbm, hbm, hbm, hbm],
+        in_specs=[hbm] * 10,
         out_specs=(hbm, hbm, vmem),
         scratch_shapes=scratch,
         compiler_params=pltpu.CompilerParams(
@@ -1000,7 +1063,7 @@
             pltpu.VMEM((TAPS * 512, 512), BF16),
             *[pltpu.VMEM((RING, tall, 512), F32)] * 3,
             pltpu.VMEM(square, F32),
-            dma((4, CHUNKS)),
+            dma((4, LOADS)),
             dma((3, RING)),
             dma((2,)),
         ],

time: 144 us -> 139 us (0.965)
  Pallas kernels: 143 us -> 138 us
    pallas_call x1, Pallas kernels: 121 us -> 117 us  [shards(): pl.pallas_call(functools.partial(main_kernel, (dp_count, rep_count, count...]
where the time goes in v3:
time: 139 us
  Pallas kernels  138 us (99%)
    pallas_call x1, Pallas kernels, shards(): pl.pallas_call(functools.partial(main_kernel, (dp_count, rep_count, count...  117 us
    pallas_call x1, Pallas kernels, shards(): pl.pallas_call(update_kernel, out_shape=(jax.ShapeDtypeStruct((2,), F32),...  21.2 us

profile of v3, /device:TPU:0, one launch (start us, length us, event | category | flops | bytes accessed | tf_op | source)
XLA Modules:
  0.0 139.3 jit_solution(696243025535514863)
XLA Ops:
  0.6 117.3 %reduce_and_precondition.1 = (f32[4608,512]{1,0:T(8,128)}, f32[2,2,2,2,2,16,512]{6,5,4,3,2,1,0:T(8,128)}, f32[24,512]{1,0:T(8,128)}) custom-call(s32[12]{0:T(128)} %micro_hbm.1, s32[12]{0:T(128)} %labels_hbm.1, bf16[12,8,8,512]{3,2,1,0:T(8,128)(2,1)} %images_hbm.1, f32[1,512]{1,0:T(1,128)} %bitcast.17, f32[1,512]{1,0:T(1,128)} %bitcast.19, ...), custom_call_target="tpu_custom_call" | custom-call | tf_op jit(solution)/shard_map/reduce_and_precondition/pallas_call | solution.py:1019
  117.9 21.2 %adamw.1 = (f32[2]{0:T(128)}, f32[1]{0:T(128)}, f32[2,512]{1,0:T(2,128)}, f32[2,512]{1,0:T(2,128)}, f32[2,512]{1,0:T(2,128)}, /*index=5*/f32[10,513]{1,0:T(8,128...) custom-call(f32[24,512]{1,0:T(8,128)} %get-tuple-element.27.facts, ...), custom_call_target="tpu_custom_call" | custom-call | tf_op jit(solution)/shard_map/adamw/pallas_call | solution.py:1047

commit v4 on v3

--- a/solution.py
+++ b/solution.py
@@ -155,7 +155,6 @@
     rot_hi,
     rot2_hi,
     rot2_lo,
-    basis_out,
     eig,
     in_hi,
     in_lo,
@@ -167,7 +166,6 @@
     out_t_lo,
     gathered_hi,
     gathered_lo,
-    result,
     rows_stat,
     pooled,
     shares,
@@ -178,7 +176,6 @@
     square_sum,
     w_sem,
     load_sem,
-    out_sem,
     send_sem,
     recv_sem,
     more_sem,
@@ -209,6 +206,9 @@
     extra = len(bits) - 5
     mine = [((dp if name == "dp" else rep) // weight_of) % 2 for name, weight_of in bits]
 
+    own = dict(enumerate(mine[:5]))
+    own_block = (((mine[0] * 2 + mine[1]) * 2 + mine[2]) * 2 + mine[3]) * 2 + mine[4]
+
     def partner(k):
         name, weight_of = bits[k]
         change = (1 - 2 * mine[k]) * weight_of
@@ -240,20 +240,20 @@
         weight_copy(unit).start()
         return carry
 
-    lax.fori_loop(0, 2 * TAPS, start_weight, 0)
+    lax.fori_loop(0, 12, start_weight, 0)
     loads = [
         pltpu.make_async_copy(src, dst, load_sem.at[k])
         for k, (src, dst) in enumerate(
             (
-                (in_hbm.at[:, 0:256], result.at[0]),
-                (in_hbm.at[:, 256:512], result.at[1]),
-                (out_hbm.at[:, 0:256], basis_out.at[0]),
-                (out_hbm.at[:, 256:512], basis_out.at[1]),
-                (eig_hbm, eig),
+                (in_hbm.at[:, :, :, :, :, :, 0:256], work.at[4]),
+                (in_hbm.at[:, :, :, :, :, :, 256:512], work.at[5]),
+                (out_hbm.at[:, :, :, :, :, :, 0:256], work.at[6]),
+                (out_hbm.at[:, :, :, :, :, :, 256:512], work.at[7]),
+                (eig_hbm.at[pl.ds(pl.multiple_of(own_block * 16, 16), 16)], eig),
             )
         )
     ]
-    for copy in loads + first_loads[2:]:
+    for copy in first_loads[2:]:
         copy.start()
 
     barrier = pltpu.get_barrier_semaphore()
@@ -291,35 +291,39 @@
     first_loads[0].wait()
     lax.fori_loop(0, 8, build, 0)
 
-    def clear(h, carry):
-        conv[h] = jnp.zeros((stride, 512), F32)
-        return carry
-
-    lax.fori_loop(0, 8, clear, 0)
-
-    def conv_row(dy, carry):
-        for dx in range(3):
-            for j in range(2):
-                unit = 2 * (dy * 3 + dx) + j
-                weight_copy(unit).wait()
-
-                def cast(k, inner):
-                    piece = work[unit, k // 4, (k // 2) % 2, k % 2].reshape(64, 256)
-                    weight_low[dx, pl.ds(pl.multiple_of(k * 64, 64), 64), j * 256 : j * 256 + 256] = piece.astype(BF16)
-                    return inner
-
-                lax.fori_loop(0, 8, cast, 0)
+    def wait_row(dy):
+        for unit in range(6 * dy, 6 * dy + 6):
+            weight_copy(unit).wait()
+
+    def cast(dy, k):
+        dx, j, half = k // 4, (k // 2) % 2, k % 2
+        piece = work[2 * (3 * dy + dx) + j, half].reshape(256, 256)
+        weight_low[dy % 2, dx, 256 * half : 256 * half + 256, 256 * j : 256 * j + 256] = piece.astype(BF16)
+
+    wait_row(0)
+    lax.fori_loop(12, 2 * TAPS, start_weight, 0)
+    for k in range(12):
+        cast(0, k)
+    for dy in range(3):
+        if dy < 2:
+            wait_row(dy + 1)
+        if dy == 1:
+            for copy in loads:
+                copy.start()
         for m in range(2):
             for n in range(2):
                 total = None
                 for dx in range(3):
-                    rows = pl.ds(pl.multiple_of(dy * stride + m * 4 * stride, 16), 4 * stride)
-                    term = dot(narrow[dx, rows], weight_low[dx, :, n * 256 : n * 256 + 256])
+                    begin = (dy + 4 * m) * stride
+                    term = dot(
+                        narrow[dx, begin : begin + 4 * stride], weight_low[dy % 2, dx, :, n * 256 : n * 256 + 256]
+                    )
                     total = term if total is None else total + term
-                conv[4 * m : 4 * m + 4, :, n * 256 : n * 256 + 256] += total.reshape(4, stride, 256)
-        return carry
-
-    lax.fori_loop(0, 3, conv_row, 0)
+                    if dy < 2:
+                        cast(dy + 1, 6 * m + 3 * n + dx)
+                at = (slice(4 * m, 4 * m + 4), slice(None), slice(n * 256, n * 256 + 256))
+                total = total.reshape(4, stride, 256)
+                conv[at] = total if dy == 0 else conv[at] + total
 
     for copy in first_loads[1:]:
         copy.wait()
@@ -421,7 +425,7 @@
 
     for copy in loads:
         copy.wait()
-    value = jnp.concatenate([result[0], result[1]], axis=1)
+    value = jnp.concatenate([work[4].reshape(512, 256), work[5].reshape(512, 256)], axis=1)
     in_hi[...], in_lo[...] = split(value)
     in_t_hi[...], in_t_lo[...] = split(value.T)
     for dx in range(3):
@@ -436,7 +440,7 @@
             at = pl.ds(pl.multiple_of(128 + 256 * j, 128), 256)
             turned_hi[dx, :, at] = value.astype(BF16)
             total = value * value if total is None else total + value * value
-        result[j] = total
+        work[j] = total.reshape(2, 2, 2, 2, 2, 16, 256)
         return carry
 
     lax.fori_loop(0, 2, turn, 0)
@@ -537,7 +541,7 @@
 
     lax.fori_loop(2, 4, turn, 0)
     def squares(h):
-        return result[h // 2, :, (h % 2) * 128 : (h % 2) * 128 + 128]
+        return work[h // 2, :, :, :, :, :, :, (h % 2) * 128 : (h % 2) * 128 + 128].reshape(512, 128)
 
     for h in range(8):
         value = squares(h)
@@ -547,7 +551,7 @@
             value = value + squares(h + 1)
         box_hi[:, h * 128 : h * 128 + 128], box_lo[:, h * 128 : h * 128 + 128] = split(value)
 
-    value = jnp.concatenate([basis_out[0], basis_out[1]], axis=1)
+    value = jnp.concatenate([work[6].reshape(512, 256), work[7].reshape(512, 256)], axis=1)
     out_hi[...], out_lo[...] = split(value)
     out_t_hi[...], out_t_lo[...] = split(value.T)
     totals = tile_end(1)
@@ -694,15 +698,11 @@
         if stage >= 4 and stage < 4 + extra:
             do_rs(unit, stage + 1)
 
-    own = dict(enumerate(mine[:5]))
-    own_block = (((mine[0] * 2 + mine[1]) * 2 + mine[2]) * 2 + mine[3]) * 2 + mine[4]
-
     def do_post(tap, stage):
         pair = (2 * tap, 2 * tap + 1)
         value = jnp.concatenate([half_sum[region(unit, own)] for unit in pair], axis=1)
         if tap == STAT:
-            rows = pl.ds(pl.multiple_of(own_block * 16, 16), 16)
-            value = 0.95 * eig[rows] + 0.05 * (value * (live_total * float(area * area)))
+            value = 0.95 * eig[...] + 0.05 * (value * (live_total * float(area * area)))
             scale_rows[...] = value + DAMPING
         else:
             high, low = split(value / scale_rows[...])
@@ -716,27 +716,12 @@
         if stage < 4:
             ag_copy(unit, stage + 1).start()
 
-    done = []
-
-    def result_copy(k):
-        tap, cols = done[k] // 2, slice((done[k] % 2) * 256, (done[k] % 2) * 256 + 256)
-        return pltpu.make_async_copy(result.at[k % 4], precond.at[pl.ds(tap * 512, 512), cols], out_sem.at[k % 4])
-
-    scale_copies = [
-        pltpu.make_async_copy(
-            work.at[2 * STAT + k], scales.at[:, :, :, :, :, :, 256 * k : 256 * k + 256], out_sem.at[4 + k]
-        )
-        for k in range(2)
-    ]
 
     def do_fin(unit, stage):
-        if unit // 2 == STAT:
-            scale_copies[unit % 2].start()
+        tap, cols = unit // 2, slice((unit % 2) * 256, (unit % 2) * 256 + 256)
+        if tap == STAT:
+            scales[:, cols] = work[unit].reshape(512, 256)
             return
-        k = len(done)
-        done.append(unit)
-        if k >= 4:
-            result_copy(k - 4).wait()
 
         def cut(i, carry):
             rows = pl.ds(pl.multiple_of(i * 64, 64), 64)
@@ -753,12 +738,11 @@
                 + dot(in_hi[rows], gathered_lo[...])
                 + dot(in_lo[rows], gathered_hi[...])
             )
-            result[k % 4, rows] = value
+            precond[pl.ds(pl.multiple_of(tap * 512 + i * 256, 256), 256), cols] = value
             square_sum[...] += jnp.sum((value * value).reshape(32, 8, 256), axis=0)
             return carry
 
         lax.fori_loop(0, 2, tile, 0)
-        result_copy(k).start()
 
     def do_sm(stage, unused):
         sm_copy(stage).wait()
@@ -785,10 +769,6 @@
     factor = jnp.minimum(1.0, CLIP / (norm + 1e-06))
     facts[0:16] = block
     facts[16:24] = stack_rows(norm_grads + [block[NCLS + 1 : NCLS + 2], live_total, norm, factor])
-    for k in range(max(len(done) - 4, 0), len(done)):
-        result_copy(k).wait()
-    for copy in scale_copies:
-        copy.wait()
 
 
 def adamw(weight, grad, first, second, rate):
@@ -821,11 +801,11 @@
     head,
     head_first,
     head_second,
-    precond,
+    in_precond,
+    scales,
     weight,
     first,
     second,
-    scales,
     loss_parts,
     grad_norm,
     norm_new,
@@ -838,20 +818,18 @@
     conv_m,
     conv_v,
     scales_new,
-    in_precond,
     in_weight,
     in_first,
     in_second,
     out_new,
     out_m,
     out_v,
-    scales_held,
     in_sem,
     out_sem,
     scale_sem,
 ):
     tall = TAPS * 512 // CHUNKS
-    pairs = ((precond, in_precond), (weight, in_weight), (first, in_first), (second, in_second))
+    pairs = ((weight, in_weight), (first, in_first), (second, in_second))
     outs = ((out_new, conv_new), (out_m, conv_m), (out_v, conv_v))
 
     def load(k, i):
@@ -864,14 +842,13 @@
         return pltpu.make_async_copy(outs[k][0].at[i % RING], outs[k][1].at[rows], out_sem.at[k, i % RING])
 
     def start(i, carry):
-        for k in range(4):
+        for k in range(3):
             load(k, i).start()
         return carry
 
     lax.fori_loop(0, LOADS, start, 0)
-    scale_in = pltpu.make_async_copy(scales, scales_held, scale_sem.at[0])
-    scale_out = pltpu.make_async_copy(scales_held, scales_new, scale_sem.at[1])
-    scale_in.start()
+    scale_out = pltpu.make_async_copy(scales, scales_new, scale_sem)
+    scale_out.start()
 
     factor = facts[21:22, 0:1]
     loss_parts[0] = facts[18, 0]
@@ -892,7 +869,7 @@
     def chunk(i, carry):
         @pl.when(i % (CHUNKS // LOADS) == 0)
         def _():
-            for k in range(4):
+            for k in range(3):
                 load(k, i // (CHUNKS // LOADS)).wait()
 
         @pl.when(i >= RING)
@@ -918,8 +895,6 @@
         return carry
 
     lax.fori_loop(0, CHUNKS, chunk, 0)
-    scale_in.wait()
-    scale_out.start()
     for i in range(CHUNKS - RING, CHUNKS):
         for k in range(3):
             store(k, i).wait()
@@ -952,7 +927,7 @@
     extra = bit_count - 5
     vmem = pl.BlockSpec(memory_space=pltpu.VMEM)
     smem = pl.BlockSpec(memory_space=pltpu.SMEM)
-    hbm = pl.BlockSpec(memory_space=pl.ANY)
+    hbm = pl.BlockSpec(memory_space=pltpu.HBM)
     gain = batchnorm_gain.reshape(1, 512)
     shift = batchnorm_shift.reshape(1, 512)
     pixels = 8 * count_img
@@ -984,17 +959,16 @@
         pltpu.VMEM((3, 1024, 512), BF16),
         pltpu.VMEM((8, pixels, 512), F32),
         pltpu.VMEM((8, pixels, 512), F32),
-        pltpu.VMEM((3, 512, 512), BF16),
+        pltpu.VMEM((2, 3, 512, 512), BF16),
         pltpu.VMEM((3, 512, 1280), BF16),
         pltpu.VMEM((512, 1024), BF16),
         pltpu.VMEM((512, 1024), BF16),
         pltpu.VMEM((1024, 512), BF16),
     ]
     scratch += [pltpu.VMEM((1024, 512), BF16)] * 3
-    scratch += [pltpu.VMEM((2, 512, 256), F32), pltpu.VMEM(square, F32)]
+    scratch += [pltpu.VMEM((16, 512), F32)]
     scratch += [pltpu.VMEM(square, BF16)] * 8 + [pltpu.VMEM((512, 256), BF16)] * 2
     scratch += [
-        pltpu.VMEM((4, 512, 256), F32),
         pltpu.VMEM((4, 8, 512), F32),
         pltpu.VMEM((16, 512), F32),
         pltpu.VMEM((16, 512), F32),
@@ -1005,7 +979,6 @@
         pltpu.VMEM((8, 256), F32),
         dma((2 * TAPS,)),
         dma((11,)),
-        dma((6,)),
         dma((SEND_COUNT,)),
         dma((RECV_COUNT,)),
         dma((2, 20, extra) if extra else (1, 1, 1)),
@@ -1019,15 +992,15 @@
     precond, scales, facts = pl.pallas_call(
         functools.partial(main_kernel, (dp_count, rep_count, count_img)),
         out_shape=(
-            jax.ShapeDtypeStruct((TAPS * 512, 512), F32),
-            jax.ShapeDtypeStruct((2, 2, 2, 2, 2, 16, 512), F32),
-            jax.ShapeDtypeStruct((24, 512), F32),
+            pltpu.VMEM((TAPS * 512, 512), F32),
+            pltpu.VMEM(square, F32),
+            pltpu.VMEM((24, 512), F32),
         ),
         in_specs=[hbm] * 10,
-        out_specs=(hbm, hbm, vmem),
+        out_specs=(vmem, vmem, vmem),
         scratch_shapes=scratch,
         compiler_params=pltpu.CompilerParams(
-            collective_id=0, has_side_effects=True, vmem_limit_bytes=63 * 2**20
+            collective_id=0, has_side_effects=True, vmem_limit_bytes=53 * 2**20
         ),
         name="reduce_and_precondition",
     )(
@@ -1039,8 +1012,8 @@
         head.T,
         conv_weight.reshape(TAPS, 2, 2, 2, 2, 2, 16, 512),
         eig_scales,
-        basis_in,
-        basis_out,
+        basis_in.reshape(2, 2, 2, 2, 2, 16, 512),
+        basis_out.reshape(2, 2, 2, 2, 2, 16, 512),
     )
     tall = TAPS * 512 // CHUNKS
     head_shape = (NCLS, 513)
@@ -1054,20 +1027,18 @@
             *[jax.ShapeDtypeStruct((TAPS * 512, 512), F32)] * 3,
             jax.ShapeDtypeStruct(square, F32),
         ),
-        in_specs=[vmem] * 8 + [hbm] * 5,
+        in_specs=[vmem] * 10 + [hbm] * 3,
         out_specs=(smem, smem) + (vmem,) * 6 + (hbm,) * 4,
         scratch_shapes=[
-            pltpu.VMEM((TAPS * 512, 512), F32),
             pltpu.VMEM((TAPS * 512, 512), F32),
             pltpu.VMEM((TAPS * 512, 512), BF16),
             pltpu.VMEM((TAPS * 512, 512), BF16),
             *[pltpu.VMEM((RING, tall, 512), F32)] * 3,
-            pltpu.VMEM(square, F32),
-            dma((4, LOADS)),
+            dma((3, LOADS)),
             dma((3, RING)),
-            dma((2,)),
+            dma,
         ],
-        compiler_params=pltpu.CompilerParams(vmem_limit_bytes=62 * 2**20),
+        compiler_params=pltpu.CompilerParams(vmem_limit_bytes=30 * 2**20),
         name="adamw",
     )(
         facts,
@@ -1079,10 +1050,8 @@
         head_first.T,
         head_second.T,
         precond,
-        conv_weight,
-        conv_first,
-        conv_second,
-        scales.reshape(square),
+        scales,
+        *(pltpu.with_memory_space_constraint(x, pltpu.HBM) for x in (conv_weight, conv_first, conv_second)),
     )
     loss_parts, grad_norm, norm_new, norm_m, norm_v, head_new, head_m, head_v, conv_new, conv_m, conv_v, scales_new = outs
     return (

time: 139 us -> 133 us (0.957)
  Pallas kernels: 138 us -> 131 us
    pallas_call x1, Pallas kernels: 21.2 us -> 17.3 us  [shards(): pl.pallas_call(update_kernel, out_shape=(jax.ShapeDtypeStruct((2,), F32),...]
    pallas_call x1, Pallas kernels: 117 us -> 114 us  [shards(): pl.pallas_call(functools.partial(main_kernel, (dp_count, rep_count, count...]
where the time goes in v4:
time: 133 us; the launch traced here: 132 us
  Pallas kernels  131 us (98%)
    pallas_call x1, Pallas kernels, shards(): pl.pallas_call(functools.partial(main_kernel, (dp_count, rep_count, count...  114 us
    pallas_call x1, Pallas kernels, shards(): pl.pallas_call(update_kernel, out_shape=(jax.ShapeDtypeStruct((2,), F32),...  17.3 us

profile of v4, /device:TPU:0, one launch (start us, length us, event | category | flops | bytes accessed | tf_op | source)
XLA Modules:
  0.0 132.4 jit_solution(18311555278160395372)
XLA Ops:
  0.6 0.0 copy-start.2
  0.7 0.0 copy-start.1
  0.7 0.0 copy-start
  0.7 0.0 copy-start.6
  0.7 0.0 copy-start.5
  0.7 0.0 copy-start.4
  0.7 0.0 copy-start.3
  0.7 114.2 %reduce_and_precondition.1 = (f32[4608,512]{1,0:T(8,128)S(1)}, f32[512,512]{1,0:T(8,128)S(1)}, f32[24,512]{1,0:T(8,128)S(1)}) custom-call(s32[12]{0:T(128)} %micro_hbm.1, s32[12]{0:T(128)} %labels_hbm.1, bf16[12,8,8,512]{3,2,1,0:T(8,128)(2,1)} %images_hbm.1, f32[1,512]{1,0:T(1,128)} %bitcast.16, f32[1,512]{1,0:T(1,128)} %bitcast.18, f32[10,513]{1,0:T(8,128)} %bitcast.12, ...), custom_call_target="tpu_custom_call" | custom-call | tf_op jit(solution)/shard_map/reduce_and_precondition/pallas_call | solution.py:992
  114.9 0.0 copy-done.2
  114.9 0.0 copy-done.1
  115.0 0.0 copy-done
  115.0 0.0 copy-done.6
  115.0 0.0 copy-done.5
  115.0 0.0 copy-done.4
  115.0 0.0 copy-done.3
  115.0 17.3 %adamw.1 = (f32[2]{0:T(128)}, f32[1]{0:T(128)}, f32[2,512]{1,0:T(2,128)}, f32[2,512]{1,0:T(2,128)}, f32[2,512]{1,0:T(2,128)}, /*index=5*/f32[10,513]{1,0:T(8,128...) custom-call(f32[24,512]{1,0:T(8,128)S(1)} %get-tuple-element.27.fact, ...), custom_call_target="tpu_custom_call" | custom-call | tf_op jit(solution)/shard_map/adamw/pallas_call | solution.py:1020
Async XLA Ops:
  0.6 114.3 %copy-start.2 = (f32[513,10]{0,1:T(8,128)S(1)}, f32[513,10]{0,1:T(8,128)}, u32[]{:S(2)}) copy-start(f32[513,10]{0,1:T(8,128)} %param.31) | copy-start | bytes 61564
  0.7 114.3 %copy-start.1 = (f32[513,10]{0,1:T(8,128)S(1)}, f32[513,10]{0,1:T(8,128)}, u32[]{:S(2)}) copy-start(f32[513,10]{0,1:T(8,128)} %param.30) | copy-start | bytes 61564
  0.7 114.3 %copy-start = (f32[513,10]{0,1:T(8,128)S(1)}, f32[513,10]{0,1:T(8,128)}, u32[]{:S(2)}) copy-start(f32[513,10]{0,1:T(8,128)} %param.29) | copy-start | bytes 61564
  0.7 114.3 %copy-start.6 = (f32[2,512]{1,0:T(2,128)S(1)}, f32[2,512]{1,0:T(2,128)}, u32[]{:S(2)}) copy-start(f32[2,512]{1,0:T(2,128)} %norm_second.1) | copy-start | bytes 12292
  0.7 114.3 %copy-start.5 = (f32[2,512]{1,0:T(2,128)S(1)}, f32[2,512]{1,0:T(2,128)}, u32[]{:S(2)}) copy-start(f32[2,512]{1,0:T(2,128)} %norm_first.1) | copy-start | bytes 12292
  0.7 114.3 %copy-start.4 = (f32[512]{0:T(512)S(1)}, f32[512]{0:T(512)}, u32[]{:S(2)}) copy-start(f32[512]{0:T(512)} %param.26) | copy-start | bytes 6148
  0.7 114.3 %copy-start.3 = (f32[512]{0:T(512)S(1)}, f32[512]{0:T(512)}, u32[]{:S(2)}) copy-start(f32[512]{0:T(512)} %param.25) | copy-start | bytes 6148

commit v5 on v0

v5 whole, which is shorter than its diff:
```python
import functools

import jax
import jax.numpy as jnp
from jax import lax
from jax.experimental import pallas as pl
from jax.experimental.pallas import tpu as pltpu
from jax.sharding import PartitionSpec as P

NCLS = 10
STEP = 5
NORM_EPS = 1e-05
DAMPING = 0.001
CLIP = 0.01
MESH = pl.DeviceIdType.MESH
F32 = jnp.float32
BF16 = jnp.bfloat16
HIGHEST = lax.Precision.HIGHEST
TAPS = 9
STAT = 9
WEIGHT = 20
AWAY = 4
UNITS = (13, 4, 14, 5, 7, 18, 3, 19, 15, 12, 0, 17, 9, 10, 16, 11, 6, 2, 1, 8)
RS_ORDER = (
    (3, 1, 2, 4), (1, 2, 3, 4), (1, 2, 3, 4), (2, 1, 3, 4), (3, 1, 4, 2),
    (1, 3, 4, 2), (1, 2, 3, 4), (3, 1, 2, 4), (1, 2, 3, 4), (2, 1, 3, 4),
    (2, 3, 4, 1), (2, 3, 1, 4), (1, 2, 3, 4), (2, 3, 1, 4), (1, 2, 3, 4),
    (3, 1, 4, 2), (1, 2, 3, 4), (2, 3, 4, 1), (2, 1, 3, 4), (1, 2, 3, 4),
)
AG_ORDER = (
    (1, 3, 4, 2), (3, 4, 2, 1), (2, 3, 1, 4), (1, 3, 4, 2), (1, 2, 3, 4),
    (1, 2, 3, 4), (3, 1, 2, 4), (1, 2, 3, 4), (2, 3, 4, 1), (3, 4, 1, 2),
    (2, 1, 3, 4), (2, 1, 3, 4), (1, 2, 3, 4), (2, 1, 3, 4), (2, 3, 1, 4),
    (3, 2, 1, 4), (1, 2, 3, 4), (2, 3, 4, 1), (1, 2, 3, 4), (2, 1, 3, 4),
)
TASKS = (
    (0, 13, 0), (0, 4, 0), (0, 14, 0), (5, 0, 0), (1, 13, 0), (0, 5, 0), (1, 4, 0), (1, 14, 0),
    (0, 7, 0), (0, 18, 0), (1, 5, 0), (1, 7, 0), (5, 1, 0), (0, 3, 0), (1, 18, 0), (0, 19, 0),
    (1, 3, 0), (1, 13, 1), (0, 15, 0), (1, 19, 0), (1, 14, 1), (1, 4, 1), (5, 2, 0), (0, 12, 0),
    (0, 0, 0), (1, 15, 0), (0, 17, 0), (1, 12, 0), (1, 7, 1), (1, 5, 1), (1, 0, 0), (1, 18, 1),
    (1, 17, 0), (0, 9, 0), (1, 13, 2), (0, 10, 0), (5, 3, 0), (0, 16, 0), (1, 9, 0), (1, 19, 1),
    (1, 3, 1), (1, 10, 0), (0, 11, 0), (1, 16, 0), (1, 4, 2), (1, 14, 2), (0, 6, 0), (1, 15, 1),
    (0, 2, 0), (1, 11, 0), (0, 1, 0), (1, 5, 2), (1, 6, 0), (0, 8, 0), (1, 2, 0), (1, 12, 1),
    (1, 1, 0), (1, 17, 1), (1, 8, 0), (1, 7, 2), (1, 0, 1), (1, 18, 2), (1, 9, 1), (5, 4, 0),
    (1, 13, 3), (1, 14, 3), (1, 4, 3), (1, 19, 2), (1, 3, 2), (1, 5, 3), (1, 17, 2), (1, 18, 3),
    (1, 10, 1), (1, 16, 1), (1, 13, 4), (1, 19, 3), (1, 14, 4), (1, 3, 3), (1, 15, 2), (1, 11, 1),
    (1, 17, 3), (1, 18, 4), (1, 10, 2), (1, 12, 2), (1, 6, 1), (1, 7, 3), (1, 4, 4), (1, 19, 4),
    (2, 9, 0), (1, 5, 4), (1, 3, 4), (2, 2, 0), (1, 15, 3), (1, 11, 2), (1, 16, 2), (1, 2, 1),
    (1, 12, 3), (1, 6, 2), (1, 10, 3), (1, 15, 4), (2, 7, 0), (1, 7, 4), (3, 18, 0), (1, 1, 1),
    (3, 19, 0), (1, 16, 3), (1, 2, 2), (3, 4, 0), (1, 6, 3), (3, 5, 0), (1, 12, 4), (2, 6, 0),
    (1, 8, 1), (3, 18, 1), (3, 14, 0), (3, 19, 1), (1, 1, 2), (3, 15, 0), (1, 0, 2), (1, 2, 3),
    (1, 16, 4), (3, 4, 1), (1, 9, 2), (1, 17, 4), (2, 8, 0), (3, 5, 1), (1, 8, 2), (1, 6, 4),
    (1, 11, 3), (2, 3, 0), (1, 10, 4), (3, 12, 0), (3, 14, 1), (1, 1, 3), (3, 18, 2), (3, 13, 0),
    (1, 0, 3), (1, 9, 3), (1, 2, 4), (2, 1, 0), (3, 19, 2), (3, 15, 1), (1, 8, 3), (3, 4, 2),
    (3, 16, 0), (3, 17, 0), (1, 11, 4), (2, 5, 0), (3, 5, 2), (3, 6, 0), (3, 12, 1), (3, 3, 0),
    (3, 7, 0), (3, 18, 3), (3, 14, 2), (3, 13, 1), (1, 1, 4), (3, 18, 4), (3, 19, 3), (4, 18, 0),
    (1, 0, 4), (2, 0, 0), (1, 9, 4), (3, 4, 3), (3, 15, 2), (3, 2, 0), (3, 19, 4), (3, 16, 1),
    (1, 8, 4), (2, 4, 0), (3, 6, 1), (4, 19, 0), (3, 4, 4), (4, 4, 0), (3, 12, 2), (3, 11, 0),
    (3, 10, 0), (3, 5, 3), (3, 17, 1), (3, 7, 1), (3, 3, 1), (3, 13, 2), (3, 5, 4), (4, 5, 0),
    (3, 0, 0), (3, 1, 0), (3, 14, 3), (3, 2, 1), (3, 8, 0), (3, 15, 3), (3, 11, 1), (3, 16, 2),
    (3, 6, 2), (3, 14, 4), (3, 9, 0), (4, 14, 0), (3, 10, 1), (3, 15, 4), (4, 15, 0), (3, 17, 2),
    (3, 7, 2), (3, 12, 3), (3, 3, 2), (3, 11, 2), (3, 12, 4), (3, 13, 3), (4, 12, 0), (3, 0, 1),
    (3, 1, 1), (3, 2, 2), (3, 13, 4), (4, 13, 0), (3, 8, 1), (3, 16, 3), (3, 9, 1), (3, 17, 3),
    (3, 16, 4), (4, 16, 0), (3, 10, 2), (3, 17, 4), (3, 6, 3), (4, 17, 0), (3, 0, 2), (3, 11, 3),
    (3, 6, 4), (4, 6, 0), (3, 7, 3), (3, 1, 2), (3, 11, 4), (4, 11, 0), (3, 2, 3), (3, 8, 2),
    (3, 7, 4), (4, 7, 0), (3, 3, 3), (3, 2, 4), (3, 9, 2), (4, 2, 0), (3, 10, 3), (3, 3, 4),
    (4, 3, 0), (3, 1, 3), (3, 0, 3), (3, 10, 4), (4, 10, 0), (3, 1, 4), (3, 8, 3), (4, 1, 0),
    (3, 0, 4), (3, 9, 3), (4, 0, 0), (3, 8, 4), (4, 8, 0), (3, 9, 4), (4, 9, 0),
)
GOT_COUNT = (6, 17, 14, 10, 11)
RECV_COUNT, SEND_COUNT = 59, 20
RS_SLOT = (
    (4, 11, 12, 2, 5), (1, 15, 0, 1, 0), (4, 14, 3, 0, 3), (0, 7, 7, 6, 6), (1, 2, 1, 2, 3),
    (3, 4, 3, 3, 5), (3, 2, 2, 4, 2), (4, 3, 4, 8, 8), (2, 16, 1, 4, 7), (1, 12, 13, 3, 6),
    (2, 13, 0, 2, 10), (0, 1, 1, 9, 4), (3, 9, 10, 1, 0), (0, 0, 0, 0, 0), (2, 1, 2, 1, 1),
    (2, 8, 9, 0, 7), (5, 0, 11, 3, 1), (0, 10, 8, 7, 9), (5, 5, 5, 4, 2), (1, 6, 6, 5, 4),
)
AG_RECV = (
    (12, 17, 10, 24, 6), (29, 6, 11, 4, 1), (22, 14, 18, 12, 2), (4, 28, 4, 23, 0), (2, 8, 0, 20, 1),
    (3, 9, 17, 26, 2), (2, 9, 33, 20, 0), (18, 10, 3, 22, 1), (15, 38, 13, 5, 0), (34, 8, 14, 16, 2),
    (25, 35, 9, 15, 3), (24, 31, 5, 21, 3), (10, 3, 23, 37, 2), (13, 6, 11, 16, 0), (5, 11, 19, 13, 0),
    (7, 15, 21, 30, 1), (1, 8, 32, 7, 1), (16, 27, 36, 19, 2), (0, 4, 12, 5, 58), (1, 6, 14, 7, 0),
)
RS_SEND = (
    (10, 10, 10, 10, 10), (18, 18, 4, 4, 4), (17, 17, 14, 14, 14), (6, 6, 6, 6, 2), (1, 1, 1, 1, 1),
    (3, 3, 3, 3, 3), (16, 16, 11, 11, 11), (4, 4, 4, 4, 4), (19, 19, 17, 17, 17), (12, 12, 12, 12, 12),
    (13, 13, 13, 5, 5), (15, 15, 7, 7, 7), (9, 9, 9, 9, 9), (0, 0, 0, 0, 0), (2, 2, 2, 2, 2),
    (8, 8, 8, 6, 6), (14, 14, 14, 13, 13), (11, 11, 11, 11, 8), (5, 5, 5, 5, 5), (7, 7, 7, 7, 0),
)
AG_SEND = (
    (1, 1, 1, 1, 1), (4, 3, 3, 3, 3), (14, 12, 6, 6, 5), (16, 16, 16, 13, 6), (2, 2, 2, 2, 2),
    (3, 3, 3, 3, 3), (11, 11, 11, 11, 7), (18, 18, 15, 12, 7), (8, 8, 2, 2, 0), (14, 4, 4, 4, 1),
    (7, 7, 7, 0, 0), (19, 5, 5, 5, 5), (9, 5, 5, 2, 2), (16, 9, 9, 9, 2), (6, 6, 6, 6, 4),
    (15, 15, 15, 10, 10), (8, 8, 0, 0, 0), (13, 13, 13, 10, 8), (0, 0, 0, 0, 0), (1, 1, 1, 1, 0),
)


def split(value):
    high = value.astype(BF16)
    return high, (value - high.astype(F32)).astype(BF16)


def dot(a, b, dims=((1,), (0,))):
    return lax.dot_general(a, b, (dims, ((), ())), preferred_element_type=F32)


def dot_exact(a, b, dims=((1,), (0,))):
    return lax.dot_general(a, b, (dims, ((), ())), precision=HIGHEST, preferred_element_type=F32)


def main_kernel(
    sizes,
    micro_hbm,
    labels_hbm,
    images_hbm,
    gain_hbm,
    shift_hbm,
    head_hbm,
    weight,
    eig_hbm,
    in_hbm,
    out_hbm,
    work,
    facts,
    micro,
    labels,
    gain_ref,
    shift_ref,
    head,
    got0,
    got1,
    got2,
    got3,
    got4,
    got_more,
    small,
    small_got,
    tile_in,
    tile_core,
    tile_slots,
    tile_out,
    turned_hi,
    box_hi,
    box_lo,
    rot_hi,
    rot2_hi,
    rot2_lo,
    eig,
    in_hi,
    in_lo,
    out_t_hi,
    out_t_lo,
    rows_stat,
    pooled,
    shares,
    shares_x,
    dpool,
    head_pad,
    scale_rows,
    square_sum,
    w_sem,
    load_sem,
    send_sem,
    recv_sem,
    more_sem,
    sm_send,
    sm_recv,
    core_send,
    core_recv,
    chip_send,
    chip_recv,
):
    dp_count, rep_count, count_img = sizes
    area = 64
    cells = 16
    chips = dp_count * rep_count // 2
    dp = lax.axis_index("dp")
    rep = lax.axis_index("rep")
    core = rep % 2
    chip = dp * (rep_count // 2) + rep // 2
    bits = [("rep", 1), ("dp", 1), ("rep", 2), ("dp", 2), ("dp", 4)]
    step = 8
    while step < dp_count:
        bits.append(("dp", step))
        step *= 2
    step = 4
    while step < rep_count:
        bits.append(("rep", step))
        step *= 2
    extra = len(bits) - 5
    stride = count_img * 8
    mine = [((dp if name == "dp" else rep) // weight_of) % 2 for name, weight_of in bits]

    own = dict(enumerate(mine[:5]))
    own_block = (((mine[0] * 2 + mine[1]) * 2 + mine[2]) * 2 + mine[3]) * 2 + mine[4]

    def partner(k):
        name, weight_of = bits[k]
        change = (1 - 2 * mine[k]) * weight_of
        return (dp + change, rep) if name == "dp" else (dp, rep + change)

    def chip_device(q):
        return (q // (rep_count // 2), (q % (rep_count // 2)) * 2 + core)

    def weight_copy(unit):
        cols = pl.ds(pl.multiple_of((unit % 2) * 256, 256), 256)
        return pltpu.make_async_copy(
            weight.at[unit // 2, :, :, :, :, :, :, cols], work.at[WEIGHT + unit], w_sem.at[unit]
        )

    def start_weight(unit, carry):
        weight_copy(unit).start()
        return carry

    loads = [
        pltpu.make_async_copy(src, dst, load_sem.at[k])
        for k, (src, dst) in enumerate(
            (
                (in_hbm.at[:, :, :, :, :, :, 0:256], work.at[4]),
                (in_hbm.at[:, :, :, :, :, :, 256:512], work.at[5]),
                (out_hbm.at[:, :, :, :, :, :, 0:256], work.at[6]),
                (out_hbm.at[:, :, :, :, :, :, 256:512], work.at[7]),
                (eig_hbm.at[pl.ds(pl.multiple_of(own_block * 16, 16), 16)], eig),
            )
        )
    ]

    barrier = pltpu.get_barrier_semaphore()

    def greet(k, carry):
        pl.semaphore_signal(barrier, inc=1, device_id=chip_device((chip + k) % chips), device_id_type=MESH)
        return carry

    lax.fori_loop(1, chips, greet, 0)
    pl.semaphore_signal(barrier, inc=1, device_id=partner(0), device_id_type=MESH)

    row8 = lax.broadcasted_iota(jnp.int32, (8, 512), 0)
    row16w = lax.broadcasted_iota(jnp.int32, (16, 512), 0)
    zero_tile = jnp.zeros((8, 512), F32)

    def stack_rows(rows):
        tile = zero_tile
        for k, row in enumerate(rows):
            tile = jnp.where(row8 == k, jnp.broadcast_to(row, (8, 512)), tile)
        return tile

    def prepare(
        narrow, wide, weight_low, conv, share, images, in_t_hi, in_t_lo, out_hi, out_lo, grad_low
    ):
        first_loads = [
            pltpu.make_async_copy(src, dst, load_sem.at[5 + k])
            for k, (src, dst) in enumerate(
                (
                    (images_hbm, images),
                    (micro_hbm, micro),
                    (labels_hbm, labels),
                    (gain_hbm, gain_ref),
                    (shift_hbm, shift_ref),
                    (head_hbm, head),
                )
            )
        ]
        first_loads[0].start()
        first_loads[1].start()
        lax.fori_loop(0, 12, start_weight, 0)
        for copy in first_loads[2:]:
            copy.start()

        column = lax.broadcasted_iota(jnp.int32, (2, 8, 512), 1)
        for k in range(3):
            narrow[k, 0:stride] = jnp.zeros((stride, 512), BF16)
            narrow[k, 9 * stride : 10 * stride] = jnp.zeros((stride, 512), BF16)

        def build(h, carry):
            for pair in range(count_img // 2):
                block = images[2 * pair : 2 * pair + 2, h].astype(F32)
                left = jnp.where(column == 0, 0.0, pltpu.roll(block, 1, 1))
                right = jnp.where(column == 7, 0.0, pltpu.roll(block, 7, 1))
                at = pl.ds(pl.multiple_of((h + 1) * stride + 16 * pair, 16), 16)
                for k, value in enumerate((left, block, right)):
                    narrow[k, at] = value.reshape(16, 512).astype(BF16)
            return carry

        first_loads[0].wait()
        lax.fori_loop(0, 8, build, 0)

        def wait_row(dy):
            for unit in range(6 * dy, 6 * dy + 6):
                weight_copy(unit).wait()

        def cast(dy, k):
            dx, j, half = k // 4, (k // 2) % 2, k % 2
            piece = work[WEIGHT + 2 * (3 * dy + dx) + j, half].reshape(256, 256)
            weight_low[dy % 2, dx, 256 * half : 256 * half + 256, 256 * j : 256 * j + 256] = piece.astype(BF16)

        wait_row(0)
        lax.fori_loop(12, 2 * TAPS, start_weight, 0)
        for k in range(12):
            cast(0, k)
        for dy in range(3):
            if dy < 2:
                wait_row(dy + 1)
            if dy == 1:
                for copy in loads:
                    copy.start()
            for m in range(2):
                for n in range(2):
                    total = None
                    for dx in range(3):
                        begin = (dy + 4 * m) * stride
                        term = dot(
                            narrow[dx, begin : begin + 4 * stride], weight_low[dy % 2, dx, :, n * 256 : n * 256 + 256]
                        )
                        total = term if total is None else total + term
                        if dy < 2:
                            cast(dy + 1, 6 * m + 3 * n + dx)
                    at = (slice(4 * m, 4 * m + 4), slice(None), slice(n * 256, n * 256 + 256))
                    total = total.reshape(4, stride, 256)
                    conv[at] = total if dy == 0 else conv[at] + total

        for copy in first_loads[1:]:
            copy.wait()
        def member(n):
            return [jnp.where(micro[n] == m, 1.0, 0.0).astype(F32) for m in range(3)]

        def gather_sums(n, carry):
            at = pl.ds(pl.multiple_of(n * 8, 8), 8)
            first = jnp.zeros((8, 512), F32)
            second = jnp.zeros((8, 512), F32)
            for h in range(8):
                value = conv[h, at]
                first = first + value
                second = second + value * value
            kinds = member(n)
            return tuple(c + k * first for c, k in zip(carry[:3], kinds)) + tuple(
                c + k * second for c, k in zip(carry[3:6], kinds)
            )

        sums = lax.fori_loop(0, count_img, gather_sums, (zero_tile,) * 6)
        counts = [jnp.zeros((), F32)] * 3
        for n in range(count_img):
            counts = [c + k for c, k in zip(counts, member(n))]
        lane8 = lax.broadcasted_iota(jnp.int32, (8, 512), 1)

        count_row = zero_tile
        for m in range(3):
            count_row = jnp.where(lane8 % 256 == m, counts[m], count_row)
        tile_in[0] = jnp.where(row8 == 6, count_row, stack_rows([jnp.sum(s, axis=0, keepdims=True) for s in sums]))

        def core_half(which):
            return pl.ds(pl.multiple_of(which * 256, 256), 256)

        def tile_copy(i):
            return pltpu.make_async_remote_copy(
                src_ref=tile_in.at[i, :, core_half(1 - core)],
                dst_ref=tile_core.at[i],
                send_sem=core_send.at[2 * i],
                recv_sem=core_recv.at[2 * i],
                device_id=partner(0),
                device_id_type=MESH,
            )

        def tile_start(i):
            tile_copy(i).start()
            tile_copy(i).wait()
            tile_slots[i, 0] = tile_in[i, :, core_half(core)] + tile_core[i]

            def give(k, carry):
                pltpu.make_async_remote_copy(
                    src_ref=tile_slots.at[i, 0],
                    dst_ref=tile_slots.at[i, k],
                    send_sem=chip_send.at[i],
                    recv_sem=chip_recv.at[i],
                    device_id=chip_device((chip + k) % chips),
                    device_id_type=MESH,
                ).start()
                return carry

            lax.fori_loop(1, chips, give, 0)

        def tile_end(i):
            others = tile_slots.at[i, pl.ds(1, chips - 1)]
            pltpu.make_async_remote_copy(
                src_ref=others,
                dst_ref=others,
                send_sem=chip_send.at[i],
                recv_sem=chip_recv.at[i],
                device_id=partner(0),
                device_id_type=MESH,
            ).wait()

            def add(k, total):
                return total + tile_slots[i, (chip - k + chips) % chips]

            tile_out[i, core] = lax.fori_loop(0, chips, add, jnp.zeros((8, 256), F32))
            back = pltpu.make_async_remote_copy(
                src_ref=tile_out.at[i, core],
                dst_ref=tile_out.at[i, core],
                send_sem=core_send.at[2 * i + 1],
                recv_sem=core_recv.at[2 * i + 1],
                device_id=partner(0),
                device_id_type=MESH,
            )
            back.start()
            back.wait()
            return jnp.concatenate([tile_out[i, 0], tile_out[i, 1]], axis=1)

        pl.semaphore_wait(barrier, chips)
        tile_start(0)

        def widen(h, carry):
            source = pl.ds(pl.multiple_of((h + 1) * stride, 16), stride)
            target = pl.ds(pl.multiple_of(h * 128, 128), stride)
            fill = pl.ds(pl.multiple_of(h * 128 + stride, 16), 128 - stride)
            for k in range(3):
                wide[k, target] = narrow[k, source]
                wide[k, fill] = jnp.zeros((128 - stride, 512), BF16)
            grad_low[fill] = jnp.zeros((128 - stride, 512), BF16)
            return carry

        lax.fori_loop(0, 8, widen, 0)
        for copy in loads:
            copy.wait()
        value = jnp.concatenate([work[4].reshape(512, 256), work[5].reshape(512, 256)], axis=1)
        in_hi[...], in_lo[...] = split(value)
        in_t_hi[...], in_t_lo[...] = split(value.T)
        for dx in range(3):
            turned_hi[dx, :, 0:128] = jnp.zeros((512, 128), BF16)
            turned_hi[dx, :, 1152:1280] = jnp.zeros((512, 128), BF16)

        def turn(j, carry):
            total = None
            for dx in range(3):
                rows = wide[dx, pl.ds(pl.multiple_of(256 * j, 256), 256)]
                value = dot(in_t_hi[...], rows, ((1,), (1,))) + dot(in_t_lo[...], rows, ((1,), (1,)))
                at = pl.ds(pl.multiple_of(128 + 256 * j, 128), 256)
                turned_hi[dx, :, at] = value.astype(BF16)
                total = value * value if total is None else total + value * value
            work[j] = total.reshape(2, 2, 2, 2, 2, 16, 256)
            return carry

        lax.fori_loop(0, 2, turn, 0)

        totals = tile_end(0)

        gain = gain_ref[...]
        shift = shift_ref[...]
        live_total = totals[6:7, 0:1] + totals[6:7, 1:2] + totals[6:7, 2:3]
        pixels = [totals[6:7, m : m + 1] * float(area) for m in range(3)]
        mean_rows, rstd_rows = [], []
        for m in range(3):
            mean = totals[m : m + 1] / pixels[m]
            var = totals[3 + m : 4 + m] / pixels[m] - mean * mean
            mean_rows.append(mean)
            rstd_rows.append(lax.rsqrt(var + NORM_EPS))
        rows_stat[0] = stack_rows(mean_rows)
        rows_stat[1] = stack_rows(rstd_rows)

        def image_rows(n, k):
            kinds = member(n)
            row = sum(kinds[m] * rows_stat[k, m : m + 1] for m in range(3))
            return row, 1.0 - (kinds[0] + kinds[1] + kinds[2])

        even = lax.broadcasted_iota(jnp.int32, (8, 512), 0) % 2 == 0
        pooled[...] = jnp.zeros((16, 512), F32)
        shares[...] = jnp.zeros((16, 512), F32)
        shares_x[...] = jnp.zeros((16, 512), F32)

        def forward(n, carry):
            mean, dead = image_rows(n, 0)
            rstd, _ = image_rows(n, 1)
            rstd = rstd + dead
            at = pl.ds(pl.multiple_of(n * 8, 8), 8)
            cell_sum, share_sum, share_x_sum = zero_tile, zero_tile, zero_tile
            for a in range(4):
                xs = [(conv[2 * a + k, at] - mean) * rstd for k in range(2)]
                exps = [jnp.exp(gain * x + shift) for x in xs]
                both = exps[0] + exps[1]
                both = both + jnp.where(even, pltpu.roll(both, 7, 0), pltpu.roll(both, 1, 0))
                both = both + 4.0
                cell_sum = cell_sum + jnp.log(both)
                inverse = 1.0 / both
                for k in range(2):
                    part = exps[k] * inverse
                    share[2 * a + k, at] = part
                    share_sum = share_sum + part
                    share_x_sum = share_x_sum + part * xs[k]
            row = pl.ds(n, 1)
            pooled[row] = jnp.sum(cell_sum, axis=0, keepdims=True) * (0.5 / cells)
            shares[row] = jnp.sum(share_sum, axis=0, keepdims=True)
            shares_x[row] = jnp.sum(share_x_sum, axis=0, keepdims=True)
            return carry

        lax.fori_loop(0, count_img, forward, 0)

        head_pad[...] = jnp.zeros((128, 640), F32)
        head_pad[0:NCLS, 0:513] = head[...]
        head_rows = head_pad[:, 0:512].astype(BF16)
        pooled_low = pooled[...].astype(BF16)
        logits = dot(pooled_low, head_rows, ((1,), (1,))) + head_pad[:, 512:640].T[0:1, :]
        row16 = lax.broadcasted_iota(jnp.int32, (16, 128), 0)
        lane16 = lax.broadcasted_iota(jnp.int32, (16, 128), 1)
        label_of = jnp.zeros((16, 128), jnp.int32)
        micro_of = jnp.full((16, 128), 3, jnp.int32)
        for n in range(count_img):
            label_of = jnp.where(row16 == n, labels[n], label_of)
            micro_of = jnp.where(row16 == n, micro[n], micro_of)
        is_class = lane16 < NCLS
        live = jnp.where(micro_of < 3, 1.0, 0.0)
        onehot = jnp.where(lane16 == label_of, 1.0, 0.0)
        top = jnp.max(jnp.where(is_class, logits, -3e38), axis=1, keepdims=True)
        shifted = jnp.where(is_class, logits - top, 0.0)
        log_sum = jnp.log(jnp.sum(jnp.where(is_class, jnp.exp(shifted), 0.0), axis=1, keepdims=True))
        logp = jnp.where(is_class, shifted - log_sum, 0.0)
        per_img = -(
            0.9 * jnp.sum(onehot * logp, axis=1, keepdims=True) + 0.1 / NCLS * jnp.sum(logp, axis=1, keepdims=True)
        )
        loss = jnp.sum(live[:, 0:1] * per_img, axis=0, keepdims=True)
        dlogits = jnp.where(is_class, jnp.exp(logp) - 0.9 * onehot - 0.1 / NCLS, 0.0) * (live / live_total)
        dpool[...] = dot_exact(dlogits, head_rows.astype(F32)) * (1.0 / cells)
        head_grad = dot_exact(dlogits, pooled_low.astype(F32), ((0,), (0,)))
        bias_grad = jnp.concatenate(
            [jnp.sum(dlogits, axis=0, keepdims=True), jnp.zeros((1, 384), F32)], axis=1
        )
        block = jnp.where(row16w < NCLS, head_grad[0:16], 0.0)
        block = jnp.where(row16w == NCLS, bias_grad, block)
        small[...] = jnp.where(row16w == NCLS + 1, loss, block)

        back_rows = []
        for which in (shares, shares_x):
            for m in range(3):
                inside = jnp.where(micro_of[:, 0:1] == m, 1.0, 0.0)
                back_rows.append(jnp.sum(inside * (dpool[...] * which[...]), axis=0, keepdims=True))
        tile_in[1] = stack_rows(back_rows)
        tile_start(1)

        lax.fori_loop(2, 4, turn, 0)
        def squares(h):
            return work[h // 2, :, :, :, :, :, :, (h % 2) * 128 : (h % 2) * 128 + 128].reshape(512, 128)

        for h in range(8):
            value = squares(h)
            if h > 0:
                value = value + squares(h - 1)
            if h < 7:
                value = value + squares(h + 1)
            box_hi[:, h * 128 : h * 128 + 128], box_lo[:, h * 128 : h * 128 + 128] = split(value)

        value = jnp.concatenate([work[6].reshape(512, 256), work[7].reshape(512, 256)], axis=1)
        out_hi[...], out_lo[...] = split(value)
        out_t_hi[...], out_t_lo[...] = split(value.T)
        totals = tile_end(1)
        norm_grads = [
            totals[3:4] + totals[4:5] + totals[5:6],
            totals[0:1] + totals[1:2] + totals[2:3],
        ]
        rows_stat[4] = stack_rows(norm_grads + [jnp.broadcast_to(live_total, (1, 512))])
        rows_stat[2] = stack_rows([gain * totals[m : m + 1] / pixels[m] for m in range(3)])
        rows_stat[3] = stack_rows([gain * totals[3 + m : 4 + m] / pixels[m] for m in range(3)])

        def backward(pair, carry):
            parts = []
            for k in range(2):
                n = 2 * pair + k
                mean, dead = image_rows(n, 0)
                rstd, _ = image_rows(n, 1)
                rstd = rstd + dead
                offset, _ = image_rows(n, 2)
                slope, _ = image_rows(n, 3)
                parts.append((mean, rstd, offset, slope, gain * dpool[pl.ds(n, 1)], pl.ds(pl.multiple_of(n * 8, 8), 8)))
            for h in range(8):
                values = []
                for mean, rstd, offset, slope, factor, at in parts:
                    xhat = (conv[h, at] - mean) * rstd
                    values.append(rstd * (factor * share[h, at] - offset - xhat * slope))
                rows = pl.ds(pl.multiple_of(h * 128 + 16 * pair, 16), 16)
                grad_low[rows] = jnp.concatenate(values, axis=0).astype(BF16)
            return carry

        lax.fori_loop(0, count_img // 2, backward, 0)

        def rotate(k, carry):
            rows = pl.ds(pl.multiple_of(k * 256, 256), 256)
            value = dot(grad_low[rows], out_hi[...]) + dot(grad_low[rows], out_lo[...])
            rot_hi[rows] = value.astype(BF16)
            rot2_hi[rows], rot2_lo[rows] = split(value * value)
            return carry

        lax.fori_loop(0, 4, rotate, 0)

    def exchange(half_sum, away, gathered_hi, gathered_lo):
        got = (got0, got1, got2, got3, got4)
        left_home = set()
        live_total = rows_stat[4, 2:3, 0:1]
        norm_grads = [rows_stat[4, 0:1], rows_stat[4, 1:2]]
        moments = [
        ]
        for copy in moments:
            copy.start()

        def region(unit, fixed, first=1):
            return (unit,) + tuple(fixed.get(k, slice(None)) for k in range(first, 5))

        def rs_copy(unit, stage):
            if stage < 5:
                order = (0,) + RS_ORDER[unit]
                fixed = {k: mine[k] for k in order[:stage]}
                fixed[order[stage]] = 1 - mine[order[stage]]
                target, to = got[stage].at[RS_SLOT[unit][stage]], partner(order[stage])
                sems = (send_sem.at[RS_SEND[unit][stage]], recv_sem.at[sum(GOT_COUNT[:stage]) + RS_SLOT[unit][stage]])
            else:
                fixed = dict(enumerate(mine[:5]))
                target, to = got_more.at[unit, stage - 5], partner(stage)
                sems = (more_sem.at[0, unit, stage - 5], more_sem.at[1, unit, stage - 5])
            source = half_sum.at[region(unit, fixed)] if stage else away.at[UNITS.index(unit) % AWAY]
            return pltpu.make_async_remote_copy(
                src_ref=source,
                dst_ref=target,
                send_sem=sems[0],
                recv_sem=sems[1],
                device_id=to,
                device_id_type=MESH,
            )

        def ag_copy(unit, stage):
            order = (0,) + AG_ORDER[unit]
            where = work.at[region(unit, {k: mine[k] for k in order[: 5 - stage]}, 0)]
            return pltpu.make_async_remote_copy(
                src_ref=where,
                dst_ref=where,
                send_sem=send_sem.at[AG_SEND[unit][stage]],
                recv_sem=recv_sem.at[AG_RECV[unit][stage]],
                device_id=partner(order[4 - stage]),
                device_id_type=MESH,
            )

        def sm_copy(stage):
            return pltpu.make_async_remote_copy(
                src_ref=small,
                dst_ref=small_got.at[stage],
                send_sem=sm_send.at[stage],
                recv_sem=sm_recv.at[stage],
                device_id=partner(stage),
                device_id_type=MESH,
            )

        def do_mm(unit, stage):
            tap, cols = unit // 2, slice((unit % 2) * 256, (unit % 2) * 256 + 256)
            dy, dx = tap // 3, tap % 3
            place = UNITS.index(unit)
            if place >= AWAY and UNITS[place - AWAY] not in left_home:
                left_home.add(UNITS[place - AWAY])
                rs_copy(UNITS[place - AWAY], 0).wait_send()
            for stays, half in enumerate((1 - core, core)):
                rows = pl.ds(pl.multiple_of(half * 256, 256), 256)
                if tap == STAT:
                    value = (
                        dot(box_hi[rows], rot2_hi[:, cols])
                        + dot(box_hi[rows], rot2_lo[:, cols])
                        + dot(box_lo[rows], rot2_hi[:, cols])
                    )
                else:
                    value = dot(turned_hi[dx, rows, dy * 128 : dy * 128 + 1024], rot_hi[:, cols])
                value = value.reshape(2, 2, 2, 2, 16, 256)
                if stays:
                    half_sum[unit] = value
                else:
                    away[place % AWAY] = value
                    rs_copy(unit, 0).start()

        def do_rs(unit, stage):
            if stage == 0 and unit in left_home:
                rs_copy(unit, stage).wait_recv()
            else:
                rs_copy(unit, stage).wait()
                if stage == 0:
                    left_home.add(unit)
            if stage < 5:
                fixed = {k: mine[k] for k in ((0,) + RS_ORDER[unit])[: stage + 1]}
                source, at = got[stage], (RS_SLOT[unit][stage],)
            else:
                fixed = dict(enumerate(mine[:5]))
                source, at = got_more, (unit, stage - 5)
            left = [k for k in range(1, 5) if k not in fixed]

            def add(i, carry):
                inner = dict(fixed)
                where = at
                if len(left) >= 3:
                    inner[left[0]], inner[left[1]] = i // 2, i % 2
                    where = at + (i // 2, i % 2)
                half_sum[region(unit, inner)] += source[where]
                return carry

            if len(left) >= 3:
                lax.fori_loop(0, 4, add, 0)
            else:
                add(0, 0)
            if stage < 4 + extra:
                rs_copy(unit, stage + 1).start()
            if stage >= 4 and stage < 4 + extra:
                do_rs(unit, stage + 1)

        def do_post(tap, stage):
            pair = (2 * tap, 2 * tap + 1)
            value = jnp.concatenate([half_sum[region(unit, own)] for unit in pair], axis=1)
            if tap == STAT:
                value = 0.95 * eig[...] + 0.05 * (value * (live_total * float(area * area)))
                scale_rows[...] = value + DAMPING
            else:
                high, low = split(value / scale_rows[...])
                value = dot(high, out_t_hi[...]) + dot(high, out_t_lo[...]) + dot(low, out_t_hi[...])
            for k, unit in enumerate(pair):
                work[region(unit, own, 0)] = value[:, 256 * k : 256 * k + 256]
                ag_copy(unit, 0).start()

        def do_ag(unit, stage):
            ag_copy(unit, stage).wait()
            if stage < 4:
                ag_copy(unit, stage + 1).start()


        def do_fin(unit, stage):
            if unit // 2 == STAT:
                return

            def cut(i, carry):
                rows = pl.ds(pl.multiple_of(i * 64, 64), 64)
                value = work[unit, i // 4, (i // 2) % 2, i % 2].reshape(64, 256)
                gathered_hi[rows], gathered_lo[rows] = split(value)
                return carry

            lax.fori_loop(0, 8, cut, 0)

            def tile(i, carry):
                rows = pl.ds(pl.multiple_of(i * 256, 256), 256)
                value = (
                    dot(in_hi[rows], gathered_hi[...])
                    + dot(in_hi[rows], gathered_lo[...])
                    + dot(in_lo[rows], gathered_hi[...])
                )
                work[unit, i] = value.reshape(2, 2, 2, 2, 16, 256)
                square_sum[...] += jnp.sum((value * value).reshape(32, 8, 256), axis=0)
                return carry

            lax.fori_loop(0, 2, tile, 0)

        def do_sm(stage, unused):
            sm_copy(stage).wait()
            small[...] += small_got[stage]
            if stage < 4 + extra:
                sm_copy(stage + 1).start()
            if stage >= 4 and stage < 4 + extra:
                do_sm(stage + 1, 0)

        square_sum[...] = jnp.zeros((8, 256), F32)
        sm_copy(0).start()
        run = (do_mm, do_rs, do_post, do_ag, do_fin, do_sm)
        for kind, which, stage in TASKS:
            run[kind](which, stage)

        block = small[...]
        head_part = jnp.where(row16w <= NCLS, block, 0.0)
        squared = (
            jnp.sum(jnp.sum(square_sum[...], axis=0, keepdims=True), axis=1, keepdims=True)
            + jnp.sum(norm_grads[0] * norm_grads[0] + norm_grads[1] * norm_grads[1], axis=1, keepdims=True)
            + jnp.sum(jnp.sum(head_part * head_part, axis=0, keepdims=True), axis=1, keepdims=True)
        )
        norm = jnp.sqrt(squared)
        factor = jnp.minimum(1.0, CLIP / (norm + 1e-06))
        facts[0:16] = block
        facts[16:24] = stack_rows(norm_grads + [block[NCLS + 1 : NCLS + 2], live_total, norm, factor])
        for copy in moments:
            copy.wait()

    square = (512, 512)
    pl.run_scoped(
        prepare,
        pltpu.VMEM((3, 10 * stride, 512), BF16),
        pltpu.VMEM((3, 1024, 512), BF16),
        pltpu.VMEM((2, 3, 512, 512), BF16),
        pltpu.VMEM((8, stride, 512), F32),
        pltpu.VMEM((8, stride, 512), F32),
        pltpu.VMEM((count_img, 8, 8, 512), BF16),
        *[pltpu.VMEM(square, BF16)] * 4,
        pltpu.VMEM((1024, 512), BF16),
    )
    pl.run_scoped(
        exchange,
        pltpu.VMEM((20, 2, 2, 2, 2, 16, 256), F32),
        pltpu.VMEM((AWAY, 2, 2, 2, 2, 16, 256), F32),
        pltpu.VMEM((512, 256), BF16),
        pltpu.VMEM((512, 256), BF16),
    )


def adamw(weight, grad, first, second, rate):
    first = 0.9 * first + 0.1 * grad
    second = 0.999 * second + 0.001 * grad * grad
    step_size = first / (1.0 - 0.9**STEP) / (jnp.sqrt(second / (1.0 - 0.999**STEP)) + 1e-08)
    return (weight - rate * (step_size + 0.01 * weight), first, second)


def adamw_positive(weight, grad, first, second, rate):
    first = 0.9 * first + 0.1 * grad
    second = 0.999 * second + 0.001 * grad * grad
    scaled = second * (1.0 / (1.0 - 0.999**STEP))
    root = scaled * lax.rsqrt(scaled) + 1e-08
    step = first * (rate / (1.0 - 0.9**STEP)) / root
    return (weight * (1.0 - 0.01 * rate) - step, first, second)


CHUNKS = 18
LOADS = 6
RING = 4


def update_kernel(
    facts,
    gain,
    shift,
    norm_first,
    norm_second,
    head,
    head_first,
    head_second,
    gradients,
    first_hbm,
    second_hbm,
    loss_parts,
    grad_norm,
    norm_new,
    norm_m,
    norm_v,
    head_new,
    head_m,
    head_v,
    conv_new,
    conv_m,
    conv_v,
    scales_new,
    out_new,
    out_m,
    out_v,
    first,
    second,
    in_sem,
    out_sem,
    scale_sem,
):
    tall = TAPS * 512 // CHUNKS
    outs = ((out_new, conv_new), (out_m, conv_m), (out_v, conv_v))

    def store(k, i):
        rows = pl.ds(pl.multiple_of(i * tall, tall), tall)
        return pltpu.make_async_copy(outs[k][0].at[i % RING], outs[k][1].at[rows], out_sem.at[k, i % RING])

    pairs = ((first_hbm, first), (second_hbm, second))

    def load(k, i):
        deep = TAPS * 512 // LOADS
        rows = pl.ds(pl.multiple_of(i * deep, deep), deep)
        return pltpu.make_async_copy(pairs[k][0].at[rows], pairs[k][1].at[rows], in_sem.at[k, i])

    def start(i, carry):
        for k in range(len(pairs)):
            load(k, i).start()
        return carry

    lax.fori_loop(0, LOADS, start, 0)
    factor = facts[21:22, 0:1]

    def chunk(i, carry):
        @pl.when(i % (CHUNKS // LOADS) == 0)
        def _():
            for k in range(len(pairs)):
                load(k, i // (CHUNKS // LOADS)).wait()

        @pl.when(i >= RING)
        def _():
            for k in range(3):
                store(k, i).wait()

        def piece(j, inner):
            rows = pl.ds(pl.multiple_of(i * tall + j * 128, 128), 128)
            at = pl.ds(pl.multiple_of(j * 128, 128), 128)
            for half in range(2):
                cols = slice(256 * half, 256 * half + 256)
                where = (i % 2, j)
                grad = gradients[(2 * (i // 2) + half,) + where].reshape(128, 256)
                weight = gradients[(WEIGHT + 2 * (i // 2) + half,) + where].reshape(128, 256)
                out_new[i % RING, at, cols], out_m[i % RING, at, cols], out_v[i % RING, at, cols] = adamw_positive(
                    weight, factor * grad, first[rows, cols].astype(F32), second[rows, cols].astype(F32), 0.02
                )
            return inner

        lax.fori_loop(0, tall // 128, piece, 0)
        for k in range(3):
            store(k, i).start()
        return carry

    lax.fori_loop(0, CHUNKS, chunk, 0)
    scale_copies = [
        pltpu.make_async_copy(
            gradients.at[2 * STAT + k], scales_new.at[:, :, :, :, :, :, 256 * k : 256 * k + 256], scale_sem.at[k]
        )
        for k in range(2)
    ]
    for copy in scale_copies:
        copy.start()

    loss_parts[0] = facts[18, 0]
    loss_parts[1] = facts[19, 0]
    grad_norm[0] = facts[20, 0]
    grads = factor * facts[16:18, :]
    weights = jnp.concatenate([gain[...], shift[...]], axis=0)
    norm_new[...], norm_m[...], norm_v[...] = adamw(weights, grads, norm_first[...], norm_second[...], 0.1)
    block = factor * facts[0:16, :]
    head_new[:, 0:512], head_m[:, 0:512], head_v[:, 0:512] = adamw(
        head[:, 0:512], block[0:NCLS], head_first[:, 0:512], head_second[:, 0:512], 0.05
    )
    bias = jnp.concatenate([block[0:16, 0:128], jnp.zeros((112, 128), F32)], axis=0).T[0:NCLS, NCLS : NCLS + 1]
    head_new[:, 512:513], head_m[:, 512:513], head_v[:, 512:513] = adamw(
        head[:, 512:513], bias, head_first[:, 512:513], head_second[:, 512:513], 0.05
    )
    for i in range(CHUNKS - RING, CHUNKS):
        for k in range(3):
            store(k, i).wait()
    for copy in scale_copies:
        copy.wait()


def shards(
    sizes,
    images,
    micro_ids,
    labels,
    conv_weight,
    conv_first,
    conv_second,
    eig_scales,
    basis_in,
    basis_out,
    batchnorm_gain,
    batchnorm_shift,
    norm_first,
    norm_second,
    head,
    head_first,
    head_second,
):
    dp_count, rep_count = sizes
    count_img = images.shape[0]
    chips = dp_count * rep_count // 2
    bit_count = (dp_count * rep_count - 1).bit_length()
    extra = bit_count - 5
    vmem = pl.BlockSpec(memory_space=pltpu.VMEM)
    smem = pl.BlockSpec(memory_space=pltpu.SMEM)
    hbm = pl.BlockSpec(memory_space=pltpu.HBM)
    gain = batchnorm_gain.reshape(1, 512)
    shift = batchnorm_shift.reshape(1, 512)
    pixels = 8 * count_img
    square = (512, 512)
    dma = pltpu.SemaphoreType.DMA
    scratch = [
        pltpu.SMEM((count_img,), jnp.int32),
        pltpu.SMEM((count_img,), jnp.int32),
        pltpu.VMEM((1, 512), F32),
        pltpu.VMEM((1, 512), F32),
        pltpu.VMEM((NCLS, 513), F32),
        pltpu.VMEM((GOT_COUNT[0], 2, 2, 2, 2, 16, 256), F32),
        pltpu.VMEM((GOT_COUNT[1], 2, 2, 2, 16, 256), F32),
        pltpu.VMEM((GOT_COUNT[2], 2, 2, 16, 256), F32),
        pltpu.VMEM((GOT_COUNT[3], 2, 16, 256), F32),
        pltpu.VMEM((GOT_COUNT[4], 16, 256), F32),
        pltpu.VMEM((20, extra, 16, 256) if extra else (1, 1, 8, 128), F32),
        pltpu.VMEM((16, 512), F32),
        pltpu.VMEM((bit_count, 16, 512), F32),
        pltpu.VMEM((2, 8, 512), F32),
        pltpu.VMEM((2, 8, 256), F32),
        pltpu.VMEM((2, chips, 8, 256), F32),
        pltpu.VMEM((2, 2, 8, 256), F32),
        pltpu.VMEM((3, 512, 1280), BF16),
        pltpu.VMEM((512, 1024), BF16),
        pltpu.VMEM((512, 1024), BF16),
        *[pltpu.VMEM((1024, 512), BF16)] * 3,
        pltpu.VMEM((16, 512), F32),
        *[pltpu.VMEM(square, BF16)] * 4,
        pltpu.VMEM((5, 8, 512), F32),
        *[pltpu.VMEM((16, 512), F32)] * 4,
        pltpu.VMEM((128, 640), F32),
        pltpu.VMEM((16, 512), F32),
        pltpu.VMEM((8, 256), F32),
        dma((2 * TAPS,)),
        dma((11,)),
        dma((SEND_COUNT,)),
        dma((RECV_COUNT,)),
        dma((2, 20, extra) if extra else (1, 1, 1)),
        dma((bit_count,)),
        dma((bit_count,)),
        dma((4,)),
        dma((4,)),
        dma((2,)),
        dma((2,)),
    ]
    turned_basis = [x.reshape(2, 2, 2, 2, 2, 16, 512) for x in (basis_in, basis_out)]
    gradients, facts = pl.pallas_call(
        functools.partial(main_kernel, (dp_count, rep_count, count_img)),
        out_shape=(
            pltpu.VMEM((WEIGHT + 2 * TAPS, 2, 2, 2, 2, 2, 16, 256), F32),
            pltpu.VMEM((24, 512), F32),
        ),
        in_specs=[hbm] * 10,
        out_specs=(vmem,) * 2,
        scratch_shapes=scratch,
        compiler_params=pltpu.CompilerParams(
            collective_id=0, has_side_effects=True, vmem_limit_bytes=40 * 2**20
        ),
        name="reduce_and_precondition",
    )(
        micro_ids,
        labels,
        images,
        gain,
        shift,
        head.T,
        conv_weight.reshape(TAPS, 2, 2, 2, 2, 2, 16, 512),
        eig_scales,
        *turned_basis,
    )
    tall = TAPS * 512 // CHUNKS
    head_shape = (NCLS, 513)
    outs = pl.pallas_call(
        update_kernel,
        out_shape=(
            jax.ShapeDtypeStruct((2,), F32),
            jax.ShapeDtypeStruct((1,), F32),
            *[jax.ShapeDtypeStruct((2, 512), F32)] * 3,
            *[jax.ShapeDtypeStruct(head_shape, F32)] * 3,
            *[jax.ShapeDtypeStruct((TAPS * 512, 512), F32)] * 3,
            jax.ShapeDtypeStruct((2, 2, 2, 2, 2, 16, 512), F32),
        ),
        in_specs=[vmem] * 9 + [hbm] * 2,
        out_specs=(smem, smem) + (vmem,) * 6 + (hbm,) * 4,
        scratch_shapes=[
            *[pltpu.VMEM((RING, tall, 512), F32)] * 3,
            *[pltpu.VMEM((TAPS * 512, 512), BF16)] * 2,
            dma((2, LOADS)),
            dma((3, RING)),
            dma((2,)),
        ],
        compiler_params=pltpu.CompilerParams(vmem_limit_bytes=17 * 2**20),
        name="adamw",
    )(
        facts,
        gain,
        shift,
        norm_first,
        norm_second,
        head.T,
        head_first.T,
        head_second.T,
        gradients,
        *(pltpu.with_memory_space_constraint(x, pltpu.HBM) for x in (conv_first, conv_second)),
    )
    loss_parts, grad_norm, norm_new, norm_m, norm_v, head_new, head_m, head_v, conv_new, conv_m, conv_v, scales_new = outs
    return (
        loss_parts,
        grad_norm.reshape(()),
        conv_new,
        conv_m,
        conv_v,
        scales_new.reshape(square),
        norm_new,
        norm_m,
        norm_v,
        head_new.T,
        head_m.T,
        head_v.T,
    )


def solution(mesh):
    split_images = P(("dp", "rep"))
    in_specs = (P(("dp", "rep"), None, None, None), split_images, split_images) + (P(),) * 13
    sizes = (mesh.shape["dp"], mesh.shape["rep"])
    return jax.shard_map(
        functools.partial(shards, sizes), mesh=mesh, in_specs=in_specs, out_specs=(P(),) * 12, check_vma=False
    )
```

time: 542 us -> 129 us (0.24)
  waiting for transfers between devices: 199 us -> 0 us
  matrix products: 142 us -> 0 us
  Pallas kernels: 0 us -> 128 us
  blocking collectives: 84.8 us -> 0 us
  other arithmetic: 57.8 us -> 0 us
  local copies, waits for them, and re-layouts: 34.4 us -> 0.03 us
  between operations: 19.3 us -> 0.93 us
    psum x1 -> x0, waiting for transfers between devices: 199 us -> none  [shards(): lax.psum((kernel_local, stat_local, head_local, loss_local), ('dp', 'rep'))]
    dot_general x20 -> x0, matrix products: 142 us -> none  [the longest x1 35.1 us: shards(): jnp.einsum('tik,lk->til', back, basis_out, precision=highest_precision)]
    pallas_call x0 -> x2, Pallas kernels: none -> 128 us  [the longest x1 115 us: shards(): pl.pallas_call(functools.partial(main_kernel, (dp_count, rep_count, count...]
    psum x2 -> x0, blocking collectives: 84.8 us -> none  [the longest x1 42.8 us: shards(): counts = lax.psum(counts_local, ('dp', 'rep'))]
    sub x4 -> x0, other arithmetic: 19.7 us -> none  [the longest x3 19.7 us: adamw(): return (weight - rate * (step_size + 0.01 * weight), first, second)]
    reshape x3 -> x0, local copies, waits for them, and re-layouts: 16.5 us -> none  [the longest x1 9.58 us: shards(): kernel_grad.reshape(9, chan, chan)]
    add x2 -> x0, other arithmetic: 12.9 us -> none  [the longest x1 11.6 us: shards(): box = box + turned[:, r:r + rows, c:c + wid, :]]
    reduce_sum x10 -> x0, other arithmetic: 11.1 us -> none  [the longest x1 4.24 us: shards(): jnp.einsum('gu,gqf->uf', micro_member, preactivation_gradient, precision=...]
  transfers between devices with their start and end apart: 1 -> 0, of which waited for: 1 -> 0; matrix products, arithmetic and copies ran while one was open for 1% -> 0% of each run, Pallas kernels for 0% -> 0%
where the time goes in v5:
time: 129 us
  Pallas kernels  128 us (99%)
    pallas_call x1, Pallas kernels, shards(): pl.pallas_call(functools.partial(main_kernel, (dp_count, rep_count, count...  115 us
    pallas_call x1, Pallas kernels, shards(): pl.pallas_call(update_kernel, out_shape=(jax.ShapeDtypeStruct((2,), F32),...  13.3 us

profile of v5, /device:TPU:0, one launch (start us, length us, event | category | flops | bytes accessed | tf_op | source)
XLA Modules:
  0.0 128.8 jit_solution(978682258406320580)
XLA Ops:
  0.6 0.0 copy-start.2
  0.7 0.0 copy-start.1
  0.7 0.0 copy-start
  0.7 0.0 copy-start.6
  0.7 0.0 copy-start.5
  0.7 0.0 copy-start.4
  0.7 0.0 copy-start.3
  0.7 114.5 %reduce_and_precondition.1 = (f32[38,2,2,2,2,2,16,256]{7,6,5,4,3,2,1,0:T(8,128)S(1)}, f32[24,512]{1,0:T(8,128)S(1)}) custom-call(s32[12]{0:T(128)} %micro_hbm.1, s32[12]{0:T(128)} %labels_hbm.1, bf16[12,8,8,512]{3,2,1,0:T(8,128)(2,1)} %images_hbm.1, f32[1,512]{1,0:T(1,128)} %bitcast.17, f32[1,512]{1,0:T(1,128)} %bitcast.19, f32[10,513]{1,0:T(8,128)} %bitcast.13, ...), custom_call_target="tpu_custom_call" | custom-call | tf_op jit(solution)/shard_map/reduce_and_precondition/pallas_call | solution.py:1007
  115.2 0.0 copy-done.2
  115.3 0.0 copy-done.1
  115.3 0.0 copy-done
  115.3 0.0 copy-done.6
  115.3 0.0 copy-done.5
  115.3 0.0 copy-done.4
  115.3 0.0 copy-done.3
  115.3 13.3 %adamw.1 = (f32[2]{0:T(128)}, f32[1]{0:T(128)}, f32[2,512]{1,0:T(2,128)}, f32[2,512]{1,0:T(2,128)}, f32[2,512]{1,0:T(2,128)}, /*index=5*/f32[10,513]{1,0:T(8,128...) custom-call(f32[24,512]{1,0:T(8,128)S(1)} %get-tuple-element.26.fact, ...), custom_call_target="tpu_custom_call" | custom-call | tf_op jit(solution)/shard_map/adamw/pallas_call | solution.py:1033
Async XLA Ops:
  0.6 114.6 %copy-start.2 = (f32[513,10]{0,1:T(8,128)S(1)}, f32[513,10]{0,1:T(8,128)}, u32[]{:S(2)}) copy-start(f32[513,10]{0,1:T(8,128)} %param.31) | copy-start | bytes 61564
  0.7 114.6 %copy-start.1 = (f32[513,10]{0,1:T(8,128)S(1)}, f32[513,10]{0,1:T(8,128)}, u32[]{:S(2)}) copy-start(f32[513,10]{0,1:T(8,128)} %param.30) | copy-start | bytes 61564
  0.7 114.6 %copy-start = (f32[513,10]{0,1:T(8,128)S(1)}, f32[513,10]{0,1:T(8,128)}, u32[]{:S(2)}) copy-start(f32[513,10]{0,1:T(8,128)} %param.29) | copy-start | bytes 61564
  0.7 114.6 %copy-start.6 = (f32[2,512]{1,0:T(2,128)S(1)}, f32[2,512]{1,0:T(2,128)}, u32[]{:S(2)}) copy-start(f32[2,512]{1,0:T(2,128)} %norm_second.1) | copy-start | bytes 12292
  0.7 114.6 %copy-start.5 = (f32[2,512]{1,0:T(2,128)S(1)}, f32[2,512]{1,0:T(2,128)}, u32[]{:S(2)}) copy-start(f32[2,512]{1,0:T(2,128)} %norm_first.1) | copy-start | bytes 12292
  0.7 114.6 %copy-start.4 = (f32[512]{0:T(512)S(1)}, f32[512]{0:T(512)}, u32[]{:S(2)}) copy-start(f32[512]{0:T(512)} %param.26) | copy-start | bytes 6148
  0.7 114.6 %copy-start.3 = (f32[512]{0:T(512)S(1)}, f32[512]{0:T(512)}, u32[]{:S(2)}) copy-start(f32[512]{0:T(512)} %param.25) | copy-start | bytes 6148

commit v6 on v5

--- a/solution.py
+++ b/solution.py
@@ -117,11 +117,14 @@
     shift_hbm,
     head_hbm,
     weight,
+    first_hbm,
+    second_hbm,
     eig_hbm,
     in_hbm,
     out_hbm,
     work,
     facts,
+    moments_held,
     micro,
     labels,
     gain_ref,
@@ -134,6 +137,8 @@
     got4,
     got_more,
     small,
+    small_half,
+    small_back,
     small_got,
     tile_in,
     tile_core,
@@ -205,7 +210,7 @@
     def weight_copy(unit):
         cols = pl.ds(pl.multiple_of((unit % 2) * 256, 256), 256)
         return pltpu.make_async_copy(
-            weight.at[unit // 2, :, :, :, :, :, :, cols], work.at[WEIGHT + unit], w_sem.at[unit]
+            weight.at[unit // 2, :, :, :, :, :, :, cols], work.at[WEIGHT + unit], w_sem.at[unit // 6]
         )
 
     def start_weight(unit, carry):
@@ -243,6 +248,9 @@
         for k, row in enumerate(rows):
             tile = jnp.where(row8 == k, jnp.broadcast_to(row, (8, 512)), tile)
         return tile
+
+    def core_half(which):
+        return pl.ds(pl.multiple_of(which * 256, 256), 256)
 
     def prepare(
         narrow, wide, weight_low, conv, share, images, in_t_hi, in_t_lo, out_hi, out_lo, grad_low
@@ -285,8 +293,8 @@
         lax.fori_loop(0, 8, build, 0)
 
         def wait_row(dy):
-            for unit in range(6 * dy, 6 * dy + 6):
-                weight_copy(unit).wait()
+            held = work.at[pl.ds(WEIGHT + 6 * dy, 6)]
+            pltpu.make_async_copy(held, held, w_sem.at[dy]).wait()
 
         def cast(dy, k):
             dx, j, half = k // 4, (k // 2) % 2, k % 2
@@ -347,9 +355,6 @@
             count_row = jnp.where(lane8 % 256 == m, counts[m], count_row)
         tile_in[0] = jnp.where(row8 == 6, count_row, stack_rows([jnp.sum(s, axis=0, keepdims=True) for s in sums]))
 
-        def core_half(which):
-            return pl.ds(pl.multiple_of(which * 256, 256), 256)
-
         def tile_copy(i):
             return pltpu.make_async_remote_copy(
                 src_ref=tile_in.at[i, :, core_half(1 - core)],
@@ -441,6 +446,19 @@
 
         lax.fori_loop(0, 2, turn, 0)
 
+        head_pad[...] = jnp.zeros((128, 640), F32)
+        head_pad[0:NCLS, 0:513] = head[...]
+        head_rows = head_pad[:, 0:512].astype(BF16)
+        row16 = lax.broadcasted_iota(jnp.int32, (16, 128), 0)
+        lane16 = lax.broadcasted_iota(jnp.int32, (16, 128), 1)
+        label_of = jnp.zeros((16, 128), jnp.int32)
+        micro_of = jnp.full((16, 128), 3, jnp.int32)
+        for n in range(count_img):
+            label_of = jnp.where(row16 == n, labels[n], label_of)
+            micro_of = jnp.where(row16 == n, micro[n], micro_of)
+        is_class = lane16 < NCLS
+        live = jnp.where(micro_of < 3, 1.0, 0.0)
+        onehot = jnp.where(lane16 == label_of, 1.0, 0.0)
         totals = tile_end(0)
 
         gain = gain_ref[...]
@@ -493,21 +511,8 @@
 
         lax.fori_loop(0, count_img, forward, 0)
 
-        head_pad[...] = jnp.zeros((128, 640), F32)
-        head_pad[0:NCLS, 0:513] = head[...]
-        head_rows = head_pad[:, 0:512].astype(BF16)
         pooled_low = pooled[...].astype(BF16)
         logits = dot(pooled_low, head_rows, ((1,), (1,))) + head_pad[:, 512:640].T[0:1, :]
-        row16 = lax.broadcasted_iota(jnp.int32, (16, 128), 0)
-        lane16 = lax.broadcasted_iota(jnp.int32, (16, 128), 1)
-        label_of = jnp.zeros((16, 128), jnp.int32)
-        micro_of = jnp.full((16, 128), 3, jnp.int32)
-        for n in range(count_img):
-            label_of = jnp.where(row16 == n, labels[n], label_of)
-            micro_of = jnp.where(row16 == n, micro[n], micro_of)
-        is_class = lane16 < NCLS
-        live = jnp.where(micro_of < 3, 1.0, 0.0)
-        onehot = jnp.where(lane16 == label_of, 1.0, 0.0)
         top = jnp.max(jnp.where(is_class, logits, -3e38), axis=1, keepdims=True)
         shifted = jnp.where(is_class, logits - top, 0.0)
         log_sum = jnp.log(jnp.sum(jnp.where(is_class, jnp.exp(shifted), 0.0), axis=1, keepdims=True))
@@ -518,6 +523,14 @@
         loss = jnp.sum(live[:, 0:1] * per_img, axis=0, keepdims=True)
         dlogits = jnp.where(is_class, jnp.exp(logp) - 0.9 * onehot - 0.1 / NCLS, 0.0) * (live / live_total)
         dpool[...] = dot_exact(dlogits, head_rows.astype(F32)) * (1.0 / cells)
+        back_rows = []
+        for which in (shares, shares_x):
+            for m in range(3):
+                inside = jnp.where(micro_of[:, 0:1] == m, 1.0, 0.0)
+                back_rows.append(jnp.sum(inside * (dpool[...] * which[...]), axis=0, keepdims=True))
+        tile_in[1] = stack_rows(back_rows)
+        tile_start(1)
+
         head_grad = dot_exact(dlogits, pooled_low.astype(F32), ((0,), (0,)))
         bias_grad = jnp.concatenate(
             [jnp.sum(dlogits, axis=0, keepdims=True), jnp.zeros((1, 384), F32)], axis=1
@@ -526,13 +539,18 @@
         block = jnp.where(row16w == NCLS, bias_grad, block)
         small[...] = jnp.where(row16w == NCLS + 1, loss, block)
 
-        back_rows = []
-        for which in (shares, shares_x):
-            for m in range(3):
-                inside = jnp.where(micro_of[:, 0:1] == m, 1.0, 0.0)
-                back_rows.append(jnp.sum(inside * (dpool[...] * which[...]), axis=0, keepdims=True))
-        tile_in[1] = stack_rows(back_rows)
-        tile_start(1)
+        def scale(n, carry):
+            mean, dead = image_rows(n, 0)
+            rstd, _ = image_rows(n, 1)
+            rstd = rstd + dead
+            factor = rstd * gain * dpool[pl.ds(n, 1)]
+            at = pl.ds(pl.multiple_of(n * 8, 8), 8)
+            for h in range(8):
+                share[h, at] = factor * share[h, at]
+                conv[h, at] = (conv[h, at] - mean) * rstd * rstd
+            return carry
+
+        lax.fori_loop(0, count_img, scale, 0)
 
         lax.fori_loop(2, 4, turn, 0)
         def squares(h):
@@ -562,17 +580,12 @@
             parts = []
             for k in range(2):
                 n = 2 * pair + k
-                mean, dead = image_rows(n, 0)
-                rstd, _ = image_rows(n, 1)
-                rstd = rstd + dead
+                rstd, dead = image_rows(n, 1)
                 offset, _ = image_rows(n, 2)
                 slope, _ = image_rows(n, 3)
-                parts.append((mean, rstd, offset, slope, gain * dpool[pl.ds(n, 1)], pl.ds(pl.multiple_of(n * 8, 8), 8)))
+                parts.append(((rstd + dead) * offset, slope, pl.ds(pl.multiple_of(n * 8, 8), 8)))
             for h in range(8):
-                values = []
-                for mean, rstd, offset, slope, factor, at in parts:
-                    xhat = (conv[h, at] - mean) * rstd
-                    values.append(rstd * (factor * share[h, at] - offset - xhat * slope))
+                values = [share[h, at] - offset - conv[h, at] * slope for offset, slope, at in parts]
                 rows = pl.ds(pl.multiple_of(h * 128 + 16 * pair, 16), 16)
                 grad_low[rows] = jnp.concatenate(values, axis=0).astype(BF16)
             return carry
@@ -594,6 +607,8 @@
         live_total = rows_stat[4, 2:3, 0:1]
         norm_grads = [rows_stat[4, 0:1], rows_stat[4, 1:2]]
         moments = [
+            pltpu.make_async_copy(src, moments_held.at[pl.ds(k * TAPS * 512, TAPS * 512)], load_sem.at[k])
+            for k, src in enumerate((first_hbm, second_hbm))
         ]
         for copy in moments:
             copy.start()
@@ -635,12 +650,18 @@
             )
 
         def sm_copy(stage):
+            if stage == 0:
+                source, target, to = small.at[:, core_half(1 - core)], small_got.at[0], partner(0)
+            elif stage < len(bits):
+                source, target, to = small_half, small_got.at[stage], partner(stage)
+            else:
+                source, target, to = small_half, small_back, partner(0)
             return pltpu.make_async_remote_copy(
-                src_ref=small,
-                dst_ref=small_got.at[stage],
+                src_ref=source,
+                dst_ref=target,
                 send_sem=sm_send.at[stage],
                 recv_sem=sm_recv.at[stage],
-                device_id=partner(stage),
+                device_id=to,
                 device_id_type=MESH,
             )
 
@@ -747,9 +768,9 @@
 
         def do_sm(stage, unused):
             sm_copy(stage).wait()
-            small[...] += small_got[stage]
-            if stage < 4 + extra:
-                sm_copy(stage + 1).start()
+            before = small[:, core_half(core)] if stage == 0 else small_half[...]
+            small_half[...] = before + small_got[stage]
+            sm_copy(stage + 1).start()
             if stage >= 4 and stage < 4 + extra:
                 do_sm(stage + 1, 0)
 
@@ -759,7 +780,10 @@
         for kind, which, stage in TASKS:
             run[kind](which, stage)
 
-        block = small[...]
+        sm_copy(len(bits)).wait()
+        kept, came = small_half[...], small_back[...]
+        low_half, high_half = jnp.where(core == 0, kept, came), jnp.where(core == 0, came, kept)
+        block = jnp.concatenate([low_half, high_half], axis=1)
         head_part = jnp.where(row16w <= NCLS, block, 0.0)
         squared = (
             jnp.sum(jnp.sum(square_sum[...], axis=0, keepdims=True), axis=1, keepdims=True)
@@ -810,9 +834,8 @@
     return (weight * (1.0 - 0.01 * rate) - step, first, second)
 
 
-CHUNKS = 18
-LOADS = 6
-RING = 4
+CHUNKS = 36
+RING = 8
 
 
 def update_kernel(
@@ -825,8 +848,7 @@
     head_first,
     head_second,
     gradients,
-    first_hbm,
-    second_hbm,
+    moments,
     loss_parts,
     grad_norm,
     norm_new,
@@ -842,9 +864,6 @@
     out_new,
     out_m,
     out_v,
-    first,
-    second,
-    in_sem,
     out_sem,
     scale_sem,
 ):
@@ -855,46 +874,24 @@
         rows = pl.ds(pl.multiple_of(i * tall, tall), tall)
         return pltpu.make_async_copy(outs[k][0].at[i % RING], outs[k][1].at[rows], out_sem.at[k, i % RING])
 
-    pairs = ((first_hbm, first), (second_hbm, second))
-
-    def load(k, i):
-        deep = TAPS * 512 // LOADS
-        rows = pl.ds(pl.multiple_of(i * deep, deep), deep)
-        return pltpu.make_async_copy(pairs[k][0].at[rows], pairs[k][1].at[rows], in_sem.at[k, i])
-
-    def start(i, carry):
-        for k in range(len(pairs)):
-            load(k, i).start()
-        return carry
-
-    lax.fori_loop(0, LOADS, start, 0)
     factor = facts[21:22, 0:1]
 
     def chunk(i, carry):
-        @pl.when(i % (CHUNKS // LOADS) == 0)
-        def _():
-            for k in range(len(pairs)):
-                load(k, i // (CHUNKS // LOADS)).wait()
-
         @pl.when(i >= RING)
         def _():
             for k in range(3):
                 store(k, i).wait()
 
-        def piece(j, inner):
-            rows = pl.ds(pl.multiple_of(i * tall + j * 128, 128), 128)
-            at = pl.ds(pl.multiple_of(j * 128, 128), 128)
-            for half in range(2):
-                cols = slice(256 * half, 256 * half + 256)
-                where = (i % 2, j)
-                grad = gradients[(2 * (i // 2) + half,) + where].reshape(128, 256)
-                weight = gradients[(WEIGHT + 2 * (i // 2) + half,) + where].reshape(128, 256)
-                out_new[i % RING, at, cols], out_m[i % RING, at, cols], out_v[i % RING, at, cols] = adamw_positive(
-                    weight, factor * grad, first[rows, cols].astype(F32), second[rows, cols].astype(F32), 0.02
-                )
-            return inner
-
-        lax.fori_loop(0, tall // 128, piece, 0)
+        rows = pl.ds(pl.multiple_of(i * tall, tall), tall)
+        more = pl.ds(pl.multiple_of(TAPS * 512 + i * tall, tall), tall)
+        for half in range(2):
+            cols = slice(256 * half, 256 * half + 256)
+            where = (2 * (i // 4) + half, (i // 2) % 2, i % 2)
+            grad = gradients[where].reshape(tall, 256)
+            weight = gradients[(WEIGHT + where[0],) + where[1:]].reshape(tall, 256)
+            out_new[i % RING, :, cols], out_m[i % RING, :, cols], out_v[i % RING, :, cols] = adamw_positive(
+                weight, factor * grad, moments[rows, cols].astype(F32), moments[more, cols].astype(F32), 0.02
+            )
         for k in range(3):
             store(k, i).start()
         return carry
@@ -975,7 +972,9 @@
         pltpu.VMEM((GOT_COUNT[4], 16, 256), F32),
         pltpu.VMEM((20, extra, 16, 256) if extra else (1, 1, 8, 128), F32),
         pltpu.VMEM((16, 512), F32),
-        pltpu.VMEM((bit_count, 16, 512), F32),
+        pltpu.VMEM((16, 256), F32),
+        pltpu.VMEM((16, 256), F32),
+        pltpu.VMEM((bit_count, 16, 256), F32),
         pltpu.VMEM((2, 8, 512), F32),
         pltpu.VMEM((2, 8, 256), F32),
         pltpu.VMEM((2, chips, 8, 256), F32),
@@ -991,30 +990,31 @@
         pltpu.VMEM((128, 640), F32),
         pltpu.VMEM((16, 512), F32),
         pltpu.VMEM((8, 256), F32),
-        dma((2 * TAPS,)),
+        dma((3,)),
         dma((11,)),
         dma((SEND_COUNT,)),
         dma((RECV_COUNT,)),
         dma((2, 20, extra) if extra else (1, 1, 1)),
-        dma((bit_count,)),
-        dma((bit_count,)),
+        dma((bit_count + 1,)),
+        dma((bit_count + 1,)),
         dma((4,)),
         dma((4,)),
         dma((2,)),
         dma((2,)),
     ]
     turned_basis = [x.reshape(2, 2, 2, 2, 2, 16, 512) for x in (basis_in, basis_out)]
-    gradients, facts = pl.pallas_call(
+    gradients, facts, moments = pl.pallas_call(
         functools.partial(main_kernel, (dp_count, rep_count, count_img)),
         out_shape=(
             pltpu.VMEM((WEIGHT + 2 * TAPS, 2, 2, 2, 2, 2, 16, 256), F32),
             pltpu.VMEM((24, 512), F32),
+            pltpu.VMEM((2 * TAPS * 512, 512), BF16),
         ),
-        in_specs=[hbm] * 10,
-        out_specs=(vmem,) * 2,
+        in_specs=[hbm] * 12,
+        out_specs=(vmem,) * 3,
         scratch_shapes=scratch,
         compiler_params=pltpu.CompilerParams(
-            collective_id=0, has_side_effects=True, vmem_limit_bytes=40 * 2**20
+            collective_id=0, has_side_effects=True, vmem_limit_bytes=71 * 2**19
         ),
         name="reduce_and_precondition",
     )(
@@ -1025,6 +1025,8 @@
         shift,
         head.T,
         conv_weight.reshape(TAPS, 2, 2, 2, 2, 2, 16, 512),
+        conv_first,
+        conv_second,
         eig_scales,
         *turned_basis,
     )
@@ -1040,16 +1042,14 @@
             *[jax.ShapeDtypeStruct((TAPS * 512, 512), F32)] * 3,
             jax.ShapeDtypeStruct((2, 2, 2, 2, 2, 16, 512), F32),
         ),
-        in_specs=[vmem] * 9 + [hbm] * 2,
+        in_specs=[vmem] * 10,
         out_specs=(smem, smem) + (vmem,) * 6 + (hbm,) * 4,
         scratch_shapes=[
             *[pltpu.VMEM((RING, tall, 512), F32)] * 3,
-            *[pltpu.VMEM((TAPS * 512, 512), BF16)] * 2,
-            dma((2, LOADS)),
             dma((3, RING)),
             dma((2,)),
         ],
-        compiler_params=pltpu.CompilerParams(vmem_limit_bytes=17 * 2**20),
+        compiler_params=pltpu.CompilerParams(vmem_limit_bytes=27 * 2**18),
         name="adamw",
     )(
         facts,
@@ -1061,7 +1061,7 @@
         head_first.T,
         head_second.T,
         gradients,
-        *(pltpu.with_memory_space_constraint(x, pltpu.HBM) for x in (conv_first, conv_second)),
+        moments,
     )
     loss_parts, grad_norm, norm_new, norm_m, norm_v, head_new, head_m, head_v, conv_new, conv_m, conv_v, scales_new = outs
     return (

time: 129 us -> 127 us (0.984)
  Pallas kernels: 128 us -> 126 us
    pallas_call x1, Pallas kernels: 13.3 us -> 11.4 us  [shards(): pl.pallas_call(update_kernel, out_shape=(jax.ShapeDtypeStruct((2,), F32),...]
where the time goes in v6:
time: 127 us
  Pallas kernels  126 us (99%)
    pallas_call x1, Pallas kernels, shards(): pl.pallas_call(functools.partial(main_kernel, (dp_count, rep_count, count...  115 us
    pallas_call x1, Pallas kernels, shards(): pl.pallas_call(update_kernel, out_shape=(jax.ShapeDtypeStruct((2,), F32),...  11.4 us

profile of v6, /device:TPU:0, one launch (start us, length us, event | category | flops | bytes accessed | tf_op | source)
XLA Modules:
  0.0 127.3 jit_solution(3126378767238072086)
XLA Ops:
  0.7 0.0 copy-start
  0.7 0.0 copy-start.1
  0.7 0.0 copy-start.2
  0.7 0.0 copy-start.3
  0.7 0.0 copy-start.4
  0.7 0.0 copy-start.5
  0.7 0.0 copy-start.6
  0.7 114.8 %reduce_and_precondition.1 = (f32[38,2,2,2,2,2,16,256]{7,6,5,4,3,2,1,0:T(8,128)S(1)}, f32[24,512]{1,0:T(8,128)S(1)}, bf16[9216,512]{1,0:T(8,128)(2,1)S(1)}) custom-call(s32[12]{0:T(128)} %micro_hbm.1, s32[12]{0:T(128)} %labels_hbm.1, bf16[12,8,8,512]{3,2,1,0:T(8,128)(2,1)} %images_hbm.1, f32[1,512]{1,0:T(1,128)} %bitcast.17, f32[1,512]{1,0:T(1,128)} %bitcast.19, ...), custom_call_target="tpu_custom_call" | custom-call | tf_op jit(solution)/shard_map/reduce_and_precondition/pallas_call | solution.py:1006
  115.6 0.0 copy-done
  115.6 0.0 copy-done.1
  115.6 0.0 copy-done.2
  115.6 0.0 copy-done.3
  115.6 0.0 copy-done.4
  115.6 0.0 copy-done.5
  115.6 0.0 copy-done.6
  115.6 11.4 %adamw.1 = (f32[2]{0:T(128)}, f32[1]{0:T(128)}, f32[2,512]{1,0:T(2,128)}, f32[2,512]{1,0:T(2,128)}, f32[2,512]{1,0:T(2,128)}, /*index=5*/f32[10,513]{1,0:T(8,128...) custom-call(f32[24,512]{1,0:T(8,128)S(1)} %get-tuple-element.27.fact, ...), custom_call_target="tpu_custom_call" | custom-call | tf_op jit(solution)/shard_map/adamw/pallas_call | solution.py:1035
Async XLA Ops:
  0.7 114.9 %copy-start = (f32[513,10]{0,1:T(8,128)S(1)}, f32[513,10]{0,1:T(8,128)}, u32[]{:S(2)}) copy-start(f32[513,10]{0,1:T(8,128)} %param.29) | copy-start | bytes 61564
  0.7 114.9 %copy-start.1 = (f32[513,10]{0,1:T(8,128)S(1)}, f32[513,10]{0,1:T(8,128)}, u32[]{:S(2)}) copy-start(f32[513,10]{0,1:T(8,128)} %param.30) | copy-start | bytes 61564
  0.7 114.9 %copy-start.2 = (f32[513,10]{0,1:T(8,128)S(1)}, f32[513,10]{0,1:T(8,128)}, u32[]{:S(2)}) copy-start(f32[513,10]{0,1:T(8,128)} %param.31) | copy-start | bytes 61564
  0.7 114.9 %copy-start.3 = (f32[512]{0:T(512)S(1)}, f32[512]{0:T(512)}, u32[]{:S(2)}) copy-start(f32[512]{0:T(512)} %param.25) | copy-start | bytes 6148
  0.7 114.9 %copy-start.4 = (f32[512]{0:T(512)S(1)}, f32[512]{0:T(512)}, u32[]{:S(2)}) copy-start(f32[512]{0:T(512)} %param.26) | copy-start | bytes 6148
  0.7 114.9 %copy-start.5 = (f32[2,512]{1,0:T(2,128)S(1)}, f32[2,512]{1,0:T(2,128)}, u32[]{:S(2)}) copy-start(f32[2,512]{1,0:T(2,128)} %norm_first.1) | copy-start | bytes 12292
  0.7 114.9 %copy-start.6 = (f32[2,512]{1,0:T(2,128)S(1)}, f32[2,512]{1,0:T(2,128)}, u32[]{:S(2)}) copy-start(f32[2,512]{1,0:T(2,128)} %norm_second.1) | copy-start | bytes 12292

commit v7 on v6

--- a/solution.py
+++ b/solution.py
@@ -20,78 +20,78 @@
 STAT = 9
 WEIGHT = 20
 AWAY = 4
-UNITS = (13, 4, 14, 5, 7, 18, 3, 19, 15, 12, 0, 17, 9, 10, 16, 11, 6, 2, 1, 8)
+UNITS = (1, 7, 16, 8, 9, 19, 3, 18, 2, 12, 4, 11, 5, 14, 6, 10, 13, 17, 0, 15)
 RS_ORDER = (
-    (3, 1, 2, 4), (1, 2, 3, 4), (1, 2, 3, 4), (2, 1, 3, 4), (3, 1, 4, 2),
-    (1, 3, 4, 2), (1, 2, 3, 4), (3, 1, 2, 4), (1, 2, 3, 4), (2, 1, 3, 4),
-    (2, 3, 4, 1), (2, 3, 1, 4), (1, 2, 3, 4), (2, 3, 1, 4), (1, 2, 3, 4),
-    (3, 1, 4, 2), (1, 2, 3, 4), (2, 3, 4, 1), (2, 1, 3, 4), (1, 2, 3, 4),
+    (1, 2, 3, 4), (3, 1, 2, 4), (1, 2, 3, 4), (2, 1, 3, 4), (2, 1, 3, 4),
+    (3, 2, 4, 1), (2, 3, 4, 1), (1, 3, 2, 4), (1, 3, 2, 4), (3, 2, 1, 4),
+    (1, 3, 2, 4), (1, 3, 4, 2), (3, 2, 1, 4), (2, 1, 3, 4), (1, 2, 3, 4),
+    (2, 1, 3, 4), (2, 3, 4, 1), (1, 2, 3, 4), (1, 2, 3, 4), (2, 1, 3, 4),
 )
 AG_ORDER = (
-    (1, 3, 4, 2), (3, 4, 2, 1), (2, 3, 1, 4), (1, 3, 4, 2), (1, 2, 3, 4),
-    (1, 2, 3, 4), (3, 1, 2, 4), (1, 2, 3, 4), (2, 3, 4, 1), (3, 4, 1, 2),
-    (2, 1, 3, 4), (2, 1, 3, 4), (1, 2, 3, 4), (2, 1, 3, 4), (2, 3, 1, 4),
-    (3, 2, 1, 4), (1, 2, 3, 4), (2, 3, 4, 1), (1, 2, 3, 4), (2, 1, 3, 4),
+    (3, 2, 1, 4), (1, 3, 4, 2), (1, 2, 3, 4), (2, 3, 4, 1), (1, 2, 3, 4),
+    (1, 3, 4, 2), (2, 1, 3, 4), (1, 2, 3, 4), (1, 2, 3, 4), (1, 2, 3, 4),
+    (3, 1, 2, 4), (2, 3, 4, 1), (2, 3, 1, 4), (2, 3, 4, 1), (2, 3, 4, 1),
+    (1, 3, 4, 2), (2, 3, 4, 1), (1, 2, 3, 4), (1, 2, 3, 4), (2, 1, 3, 4),
 )
 TASKS = (
-    (0, 13, 0), (0, 4, 0), (0, 14, 0), (5, 0, 0), (1, 13, 0), (0, 5, 0), (1, 4, 0), (1, 14, 0),
-    (0, 7, 0), (0, 18, 0), (1, 5, 0), (1, 7, 0), (5, 1, 0), (0, 3, 0), (1, 18, 0), (0, 19, 0),
-    (1, 3, 0), (1, 13, 1), (0, 15, 0), (1, 19, 0), (1, 14, 1), (1, 4, 1), (5, 2, 0), (0, 12, 0),
-    (0, 0, 0), (1, 15, 0), (0, 17, 0), (1, 12, 0), (1, 7, 1), (1, 5, 1), (1, 0, 0), (1, 18, 1),
-    (1, 17, 0), (0, 9, 0), (1, 13, 2), (0, 10, 0), (5, 3, 0), (0, 16, 0), (1, 9, 0), (1, 19, 1),
-    (1, 3, 1), (1, 10, 0), (0, 11, 0), (1, 16, 0), (1, 4, 2), (1, 14, 2), (0, 6, 0), (1, 15, 1),
-    (0, 2, 0), (1, 11, 0), (0, 1, 0), (1, 5, 2), (1, 6, 0), (0, 8, 0), (1, 2, 0), (1, 12, 1),
-    (1, 1, 0), (1, 17, 1), (1, 8, 0), (1, 7, 2), (1, 0, 1), (1, 18, 2), (1, 9, 1), (5, 4, 0),
-    (1, 13, 3), (1, 14, 3), (1, 4, 3), (1, 19, 2), (1, 3, 2), (1, 5, 3), (1, 17, 2), (1, 18, 3),
-    (1, 10, 1), (1, 16, 1), (1, 13, 4), (1, 19, 3), (1, 14, 4), (1, 3, 3), (1, 15, 2), (1, 11, 1),
-    (1, 17, 3), (1, 18, 4), (1, 10, 2), (1, 12, 2), (1, 6, 1), (1, 7, 3), (1, 4, 4), (1, 19, 4),
-    (2, 9, 0), (1, 5, 4), (1, 3, 4), (2, 2, 0), (1, 15, 3), (1, 11, 2), (1, 16, 2), (1, 2, 1),
-    (1, 12, 3), (1, 6, 2), (1, 10, 3), (1, 15, 4), (2, 7, 0), (1, 7, 4), (3, 18, 0), (1, 1, 1),
-    (3, 19, 0), (1, 16, 3), (1, 2, 2), (3, 4, 0), (1, 6, 3), (3, 5, 0), (1, 12, 4), (2, 6, 0),
-    (1, 8, 1), (3, 18, 1), (3, 14, 0), (3, 19, 1), (1, 1, 2), (3, 15, 0), (1, 0, 2), (1, 2, 3),
-    (1, 16, 4), (3, 4, 1), (1, 9, 2), (1, 17, 4), (2, 8, 0), (3, 5, 1), (1, 8, 2), (1, 6, 4),
-    (1, 11, 3), (2, 3, 0), (1, 10, 4), (3, 12, 0), (3, 14, 1), (1, 1, 3), (3, 18, 2), (3, 13, 0),
-    (1, 0, 3), (1, 9, 3), (1, 2, 4), (2, 1, 0), (3, 19, 2), (3, 15, 1), (1, 8, 3), (3, 4, 2),
-    (3, 16, 0), (3, 17, 0), (1, 11, 4), (2, 5, 0), (3, 5, 2), (3, 6, 0), (3, 12, 1), (3, 3, 0),
-    (3, 7, 0), (3, 18, 3), (3, 14, 2), (3, 13, 1), (1, 1, 4), (3, 18, 4), (3, 19, 3), (4, 18, 0),
-    (1, 0, 4), (2, 0, 0), (1, 9, 4), (3, 4, 3), (3, 15, 2), (3, 2, 0), (3, 19, 4), (3, 16, 1),
-    (1, 8, 4), (2, 4, 0), (3, 6, 1), (4, 19, 0), (3, 4, 4), (4, 4, 0), (3, 12, 2), (3, 11, 0),
-    (3, 10, 0), (3, 5, 3), (3, 17, 1), (3, 7, 1), (3, 3, 1), (3, 13, 2), (3, 5, 4), (4, 5, 0),
-    (3, 0, 0), (3, 1, 0), (3, 14, 3), (3, 2, 1), (3, 8, 0), (3, 15, 3), (3, 11, 1), (3, 16, 2),
-    (3, 6, 2), (3, 14, 4), (3, 9, 0), (4, 14, 0), (3, 10, 1), (3, 15, 4), (4, 15, 0), (3, 17, 2),
-    (3, 7, 2), (3, 12, 3), (3, 3, 2), (3, 11, 2), (3, 12, 4), (3, 13, 3), (4, 12, 0), (3, 0, 1),
-    (3, 1, 1), (3, 2, 2), (3, 13, 4), (4, 13, 0), (3, 8, 1), (3, 16, 3), (3, 9, 1), (3, 17, 3),
-    (3, 16, 4), (4, 16, 0), (3, 10, 2), (3, 17, 4), (3, 6, 3), (4, 17, 0), (3, 0, 2), (3, 11, 3),
-    (3, 6, 4), (4, 6, 0), (3, 7, 3), (3, 1, 2), (3, 11, 4), (4, 11, 0), (3, 2, 3), (3, 8, 2),
-    (3, 7, 4), (4, 7, 0), (3, 3, 3), (3, 2, 4), (3, 9, 2), (4, 2, 0), (3, 10, 3), (3, 3, 4),
-    (4, 3, 0), (3, 1, 3), (3, 0, 3), (3, 10, 4), (4, 10, 0), (3, 1, 4), (3, 8, 3), (4, 1, 0),
-    (3, 0, 4), (3, 9, 3), (4, 0, 0), (3, 8, 4), (4, 8, 0), (3, 9, 4), (4, 9, 0),
+    (0, 1, 0), (0, 7, 0), (0, 16, 0), (5, 0, 0), (1, 1, 0), (0, 8, 0), (1, 7, 0), (1, 16, 0),
+    (0, 9, 0), (0, 19, 0), (1, 8, 0), (1, 9, 0), (5, 1, 0), (0, 3, 0), (1, 19, 0), (0, 18, 0),
+    (1, 3, 0), (1, 1, 1), (1, 7, 1), (1, 16, 1), (1, 18, 0), (0, 2, 0), (5, 2, 0), (0, 12, 0),
+    (0, 4, 0), (1, 9, 1), (1, 2, 0), (1, 8, 1), (1, 12, 0), (0, 11, 0), (1, 19, 1), (1, 7, 2),
+    (1, 4, 0), (1, 1, 2), (0, 5, 0), (1, 11, 0), (1, 16, 2), (0, 14, 0), (5, 3, 0), (0, 6, 0),
+    (1, 3, 1), (1, 5, 0), (1, 18, 1), (1, 14, 0), (1, 8, 2), (0, 10, 0), (1, 6, 0), (1, 9, 2),
+    (0, 13, 0), (1, 7, 3), (0, 17, 0), (1, 10, 0), (1, 2, 1), (0, 0, 0), (1, 12, 1), (1, 13, 0),
+    (1, 17, 0), (1, 19, 2), (1, 4, 1), (1, 16, 3), (1, 0, 0), (0, 15, 0), (1, 1, 3), (5, 4, 0),
+    (1, 18, 2), (1, 15, 0), (1, 11, 1), (1, 8, 3), (1, 5, 1), (1, 3, 2), (1, 19, 3), (1, 7, 4),
+    (1, 18, 3), (1, 1, 4), (1, 6, 1), (1, 11, 2), (1, 14, 1), (1, 2, 2), (1, 9, 3), (1, 3, 3),
+    (1, 8, 4), (1, 12, 2), (1, 19, 4), (1, 18, 4), (2, 9, 0), (1, 6, 2), (1, 10, 1), (1, 2, 3),
+    (1, 11, 3), (1, 13, 1), (1, 9, 4), (2, 4, 0), (1, 3, 4), (3, 18, 0), (1, 17, 1), (3, 19, 0),
+    (1, 15, 1), (1, 4, 2), (1, 10, 2), (1, 16, 4), (1, 6, 3), (1, 5, 2), (1, 2, 4), (2, 1, 0),
+    (3, 18, 1), (3, 8, 0), (1, 14, 2), (3, 19, 1), (3, 9, 0), (1, 11, 4), (1, 0, 1), (1, 4, 3),
+    (1, 12, 3), (1, 17, 2), (1, 10, 3), (3, 8, 1), (1, 13, 2), (1, 5, 3), (1, 14, 3), (3, 2, 0),
+    (3, 18, 2), (3, 9, 1), (1, 15, 2), (1, 6, 4), (2, 3, 0), (3, 3, 0), (1, 4, 4), (1, 0, 2),
+    (1, 17, 3), (1, 12, 4), (3, 19, 2), (1, 13, 3), (1, 10, 4), (1, 5, 4), (3, 8, 2), (2, 5, 0),
+    (2, 2, 0), (3, 2, 1), (1, 14, 4), (3, 9, 2), (1, 15, 3), (3, 6, 0), (3, 18, 3), (3, 7, 0),
+    (1, 0, 3), (3, 3, 1), (3, 18, 4), (4, 18, 0), (3, 19, 3), (1, 17, 4), (2, 8, 0), (3, 5, 0),
+    (1, 13, 4), (2, 6, 0), (3, 8, 3), (3, 11, 0), (3, 10, 0), (3, 19, 4), (3, 6, 1), (3, 2, 2),
+    (4, 19, 0), (3, 4, 0), (3, 7, 1), (3, 8, 4), (4, 8, 0), (1, 0, 4), (1, 15, 4), (3, 3, 2),
+    (2, 0, 0), (3, 9, 3), (3, 10, 1), (3, 16, 0), (2, 7, 0), (3, 13, 0), (3, 17, 0), (3, 5, 1),
+    (3, 7, 2), (3, 9, 4), (4, 9, 0), (3, 12, 0), (3, 6, 2), (3, 4, 1), (3, 11, 1), (3, 0, 0),
+    (3, 3, 3), (3, 2, 3), (3, 17, 1), (3, 1, 0), (3, 15, 0), (3, 16, 1), (3, 10, 2), (3, 3, 4),
+    (3, 5, 2), (4, 3, 0), (3, 13, 1), (3, 14, 0), (3, 11, 2), (3, 2, 4), (4, 2, 0), (3, 6, 3),
+    (3, 7, 3), (3, 1, 1), (3, 4, 2), (3, 12, 1), (3, 16, 2), (3, 6, 4), (4, 6, 0), (3, 17, 2),
+    (3, 0, 1), (3, 7, 4), (3, 15, 1), (4, 7, 0), (3, 10, 3), (3, 5, 3), (3, 11, 3), (3, 13, 2),
+    (3, 10, 4), (4, 10, 0), (3, 11, 4), (3, 5, 4), (4, 11, 0), (3, 16, 3), (3, 14, 1), (3, 4, 3),
+    (3, 1, 2), (4, 5, 0), (3, 12, 2), (3, 16, 4), (3, 0, 2), (4, 16, 0), (3, 17, 3), (3, 15, 2),
+    (3, 4, 4), (4, 4, 0), (3, 13, 3), (3, 14, 2), (3, 17, 4), (4, 17, 0), (3, 1, 3), (3, 13, 4),
+    (4, 13, 0), (3, 12, 3), (3, 0, 3), (3, 1, 4), (4, 1, 0), (3, 15, 3), (3, 12, 4), (4, 12, 0),
+    (3, 0, 4), (3, 14, 3), (4, 0, 0), (3, 15, 4), (4, 15, 0), (3, 14, 4), (4, 14, 0),
 )
-GOT_COUNT = (6, 17, 14, 10, 11)
-RECV_COUNT, SEND_COUNT = 59, 20
+GOT_COUNT = (6, 14, 14, 10, 10)
+RECV_COUNT, SEND_COUNT = 54, 20
 RS_SLOT = (
-    (4, 11, 12, 2, 5), (1, 15, 0, 1, 0), (4, 14, 3, 0, 3), (0, 7, 7, 6, 6), (1, 2, 1, 2, 3),
-    (3, 4, 3, 3, 5), (3, 2, 2, 4, 2), (4, 3, 4, 8, 8), (2, 16, 1, 4, 7), (1, 12, 13, 3, 6),
-    (2, 13, 0, 2, 10), (0, 1, 1, 9, 4), (3, 9, 10, 1, 0), (0, 0, 0, 0, 0), (2, 1, 2, 1, 1),
-    (2, 8, 9, 0, 7), (5, 0, 11, 3, 1), (0, 10, 8, 7, 9), (5, 5, 5, 4, 2), (1, 6, 6, 5, 4),
+    (1, 5, 0, 6, 7), (0, 0, 1, 2, 1), (2, 8, 0, 0, 0), (0, 6, 7, 7, 6), (4, 10, 10, 3, 1),
+    (1, 1, 3, 4, 4), (3, 11, 1, 2, 9), (1, 1, 0, 0, 0), (3, 4, 3, 3, 2), (4, 3, 4, 6, 5),
+    (0, 12, 2, 9, 3), (0, 0, 8, 1, 8), (3, 9, 9, 8, 2), (4, 3, 12, 2, 6), (2, 2, 11, 0, 5),
+    (0, 4, 13, 5, 8), (2, 2, 2, 1, 7), (5, 13, 4, 1, 0), (1, 7, 6, 5, 4), (5, 5, 5, 4, 3),
 )
 AG_RECV = (
-    (12, 17, 10, 24, 6), (29, 6, 11, 4, 1), (22, 14, 18, 12, 2), (4, 28, 4, 23, 0), (2, 8, 0, 20, 1),
-    (3, 9, 17, 26, 2), (2, 9, 33, 20, 0), (18, 10, 3, 22, 1), (15, 38, 13, 5, 0), (34, 8, 14, 16, 2),
-    (25, 35, 9, 15, 3), (24, 31, 5, 21, 3), (10, 3, 23, 37, 2), (13, 6, 11, 16, 0), (5, 11, 19, 13, 0),
-    (7, 15, 21, 30, 1), (1, 8, 32, 7, 1), (16, 27, 36, 19, 2), (0, 4, 12, 5, 58), (1, 6, 14, 7, 0),
+    (10, 35, 10, 7, 4), (30, 6, 23, 5, 0), (6, 2, 17, 29, 2), (12, 16, 12, 28, 1), (18, 9, 7, 22, 4),
+    (0, 23, 16, 18, 3), (10, 6, 26, 5, 0), (15, 7, 13, 33, 9), (3, 0, 8, 4, 2), (5, 1, 9, 19, 0),
+    (11, 8, 31, 17, 1), (5, 27, 4, 19, 2), (24, 34, 24, 6, 3), (22, 32, 20, 15, 2), (25, 21, 16, 9, 2),
+    (3, 12, 14, 8, 1), (21, 15, 8, 13, 0), (20, 14, 11, 36, 1), (0, 2, 7, 14, 25), (1, 4, 13, 3, 1),
 )
 RS_SEND = (
-    (10, 10, 10, 10, 10), (18, 18, 4, 4, 4), (17, 17, 14, 14, 14), (6, 6, 6, 6, 2), (1, 1, 1, 1, 1),
-    (3, 3, 3, 3, 3), (16, 16, 11, 11, 11), (4, 4, 4, 4, 4), (19, 19, 17, 17, 17), (12, 12, 12, 12, 12),
-    (13, 13, 13, 5, 5), (15, 15, 7, 7, 7), (9, 9, 9, 9, 9), (0, 0, 0, 0, 0), (2, 2, 2, 2, 2),
-    (8, 8, 8, 6, 6), (14, 14, 14, 13, 13), (11, 11, 11, 11, 8), (5, 5, 5, 5, 5), (7, 7, 7, 7, 0),
+    (18, 18, 7, 7, 7), (0, 0, 0, 0, 0), (8, 8, 8, 8, 8), (6, 6, 6, 6, 6), (10, 10, 10, 10, 10),
+    (12, 12, 12, 2, 2), (14, 14, 0, 0, 0), (1, 1, 1, 1, 1), (3, 3, 3, 3, 3), (4, 4, 4, 4, 4),
+    (15, 15, 9, 9, 9), (11, 11, 11, 7, 7), (9, 9, 9, 3, 3), (16, 16, 13, 13, 5), (13, 13, 11, 11, 11),
+    (19, 19, 15, 15, 14), (2, 2, 2, 2, 2), (17, 17, 6, 6, 6), (7, 7, 7, 7, 1), (5, 5, 5, 5, 5),
 )
 AG_SEND = (
-    (1, 1, 1, 1, 1), (4, 3, 3, 3, 3), (14, 12, 6, 6, 5), (16, 16, 16, 13, 6), (2, 2, 2, 2, 2),
-    (3, 3, 3, 3, 3), (11, 11, 11, 11, 7), (18, 18, 15, 12, 7), (8, 8, 2, 2, 0), (14, 4, 4, 4, 1),
-    (7, 7, 7, 0, 0), (19, 5, 5, 5, 5), (9, 5, 5, 2, 2), (16, 9, 9, 9, 2), (6, 6, 6, 6, 4),
-    (15, 15, 15, 10, 10), (8, 8, 0, 0, 0), (13, 13, 13, 10, 8), (0, 0, 0, 0, 0), (1, 1, 1, 1, 0),
+    (7, 7, 6, 2, 2), (12, 11, 10, 7, 0), (8, 8, 8, 1, 1), (12, 12, 12, 2, 2), (10, 8, 8, 8, 4),
+    (13, 13, 13, 2, 2), (0, 0, 0, 0, 0), (16, 15, 10, 10, 1), (4, 4, 4, 2, 2), (14, 14, 14, 11, 11),
+    (4, 4, 4, 4, 4), (9, 9, 9, 9, 7), (5, 5, 5, 5, 4), (16, 16, 13, 9, 4), (14, 14, 3, 3, 1),
+    (15, 12, 1, 1, 0), (3, 3, 3, 3, 2), (6, 6, 6, 0, 0), (1, 1, 1, 1, 1), (5, 5, 5, 3, 1),
 )
 
 

time: 127 us -> 126 us (level)
  no operation moved by 1% of the time
where the time goes in v7:
time: 126 us
  Pallas kernels  125 us (99%)
    pallas_call x1, Pallas kernels, shards(): pl.pallas_call(functools.partial(main_kernel, (dp_count, rep_count, count...  114 us
    pallas_call x1, Pallas kernels, shards(): pl.pallas_call(update_kernel, out_shape=(jax.ShapeDtypeStruct((2,), F32),...  11.4 us

profile of v7, /device:TPU:0, one launch (start us, length us, event | category | flops | bytes accessed | tf_op | source)
XLA Modules:
  0.0 126.0 jit_solution(17459476324814049622)
XLA Ops:
  0.7 0.0 copy-start
  0.7 0.0 copy-start.1
  0.7 0.0 copy-start.2
  0.7 0.0 copy-start.3
  0.7 0.0 copy-start.4
  0.7 0.0 copy-start.5
  0.7 0.0 copy-start.6
  0.7 113.6 %reduce_and_precondition.1 = (f32[38,2,2,2,2,2,16,256]{7,6,5,4,3,2,1,0:T(8,128)S(1)}, f32[24,512]{1,0:T(8,128)S(1)}, bf16[9216,512]{1,0:T(8,128)(2,1)S(1)}) custom-call(s32[12]{0:T(128)} %micro_hbm.1, s32[12]{0:T(128)} %labels_hbm.1, bf16[12,8,8,512]{3,2,1,0:T(8,128)(2,1)} %images_hbm.1, f32[1,512]{1,0:T(1,128)} %bitcast.17, f32[1,512]{1,0:T(1,128)} %bitcast.19, ...), custom_call_target="tpu_custom_call" | custom-call | tf_op jit(solution)/shard_map/reduce_and_precondition/pallas_call | solution.py:1006
  114.3 0.0 copy-done
  114.3 0.0 copy-done.1
  114.3 0.0 copy-done.2
  114.3 0.0 copy-done.3
  114.4 0.0 copy-done.4
  114.4 0.0 copy-done.5
  114.4 0.0 copy-done.6
  114.4 11.4 %adamw.1 = (f32[2]{0:T(128)}, f32[1]{0:T(128)}, f32[2,512]{1,0:T(2,128)}, f32[2,512]{1,0:T(2,128)}, f32[2,512]{1,0:T(2,128)}, /*index=5*/f32[10,513]{1,0:T(8,128...) custom-call(f32[24,512]{1,0:T(8,128)S(1)} %get-tuple-element.27.fact, ...), custom_call_target="tpu_custom_call" | custom-call | tf_op jit(solution)/shard_map/adamw/pallas_call | solution.py:1035
Async XLA Ops:
  0.7 113.7 %copy-start = (f32[513,10]{0,1:T(8,128)S(1)}, f32[513,10]{0,1:T(8,128)}, u32[]{:S(2)}) copy-start(f32[513,10]{0,1:T(8,128)} %param.29) | copy-start | bytes 61564
  0.7 113.7 %copy-start.1 = (f32[513,10]{0,1:T(8,128)S(1)}, f32[513,10]{0,1:T(8,128)}, u32[]{:S(2)}) copy-start(f32[513,10]{0,1:T(8,128)} %param.30) | copy-start | bytes 61564
  0.7 113.7 %copy-start.2 = (f32[513,10]{0,1:T(8,128)S(1)}, f32[513,10]{0,1:T(8,128)}, u32[]{:S(2)}) copy-start(f32[513,10]{0,1:T(8,128)} %param.31) | copy-start | bytes 61564
  0.7 113.7 %copy-start.3 = (f32[512]{0:T(512)S(1)}, f32[512]{0:T(512)}, u32[]{:S(2)}) copy-start(f32[512]{0:T(512)} %param.25) | copy-start | bytes 6148
  0.7 113.7 %copy-start.4 = (f32[512]{0:T(512)S(1)}, f32[512]{0:T(512)}, u32[]{:S(2)}) copy-start(f32[512]{0:T(512)} %param.26) | copy-start | bytes 6148
  0.7 113.7 %copy-start.5 = (f32[2,512]{1,0:T(2,128)S(1)}, f32[2,512]{1,0:T(2,128)}, u32[]{:S(2)}) copy-start(f32[2,512]{1,0:T(2,128)} %norm_first.1) | copy-start | bytes 12292
  0.7 113.7 %copy-start.6 = (f32[2,512]{1,0:T(2,128)S(1)}, f32[2,512]{1,0:T(2,128)}, u32[]{:S(2)}) copy-start(f32[2,512]{1,0:T(2,128)} %norm_second.1) | copy-start | bytes 12292

commit v8 on v7

--- a/solution.py
+++ b/solution.py
@@ -601,7 +601,7 @@
 
         lax.fori_loop(0, 4, rotate, 0)
 
-    def exchange(half_sum, away, gathered_hi, gathered_lo):
+    def exchange(half_sum, away, gathered_hi, gathered_lo, partial):
         got = (got0, got1, got2, got3, got4)
         left_home = set()
         live_total = rows_stat[4, 2:3, 0:1]
@@ -739,10 +739,49 @@
             ag_copy(unit, stage).wait()
             if stage < 4:
                 ag_copy(unit, stage + 1).start()
+            if stage == 3 and unit in early:
+                early_half(unit)
+
+        early = [unit for kind, unit, _ in TASKS if kind == 4 and unit // 2 != STAT][-1:]
+
+        def half_product(unit, half, finish):
+            def cut(i, carry):
+                rows = pl.ds(pl.multiple_of(i * 64, 64), 64)
+                gathered_hi[rows], gathered_lo[rows] = split(work[unit, half, i // 2, i % 2].reshape(64, 256))
+                return carry
+
+            lax.fori_loop(0, 4, cut, 0)
+            cols = core_half(half)
+            high, low = gathered_hi[0:256], gathered_lo[0:256]
+
+            def tile(i, carry):
+                rows = pl.ds(pl.multiple_of(i * 256, 256), 256)
+                left = in_hi[rows, cols]
+                finish(i, rows, dot(left, high) + dot(left, low) + dot(in_lo[rows, cols], high))
+                return carry
+
+            lax.fori_loop(0, 2, tile, 0)
+
+        def early_half(unit):
+            def keep(i, rows, value):
+                partial[early.index(unit), rows] = value
+
+            half_product(unit, core, keep)
+
+        def late_half(unit):
+            def keep(i, rows, value):
+                value = value + partial[early.index(unit), rows]
+                work[unit, i] = value.reshape(2, 2, 2, 2, 16, 256)
+                square_sum[...] += jnp.sum((value * value).reshape(32, 8, 256), axis=0)
+
+            half_product(unit, 1 - core, keep)
 
 
         def do_fin(unit, stage):
             if unit // 2 == STAT:
+                return
+            if unit in early:
+                late_half(unit)
                 return
 
             def cut(i, carry):
@@ -815,6 +854,7 @@
         pltpu.VMEM((AWAY, 2, 2, 2, 2, 16, 256), F32),
         pltpu.VMEM((512, 256), BF16),
         pltpu.VMEM((512, 256), BF16),
+        pltpu.VMEM((2, 512, 256), F32),
     )
 
 

time: 126 us -> 126 us (level)
  no operation moved by 1% of the time
where the time goes in v8:
time: 126 us
  Pallas kernels  125 us (99%)
    pallas_call x1, Pallas kernels, shards(): pl.pallas_call(functools.partial(main_kernel, (dp_count, rep_count, count...  114 us
    pallas_call x1, Pallas kernels, shards(): pl.pallas_call(update_kernel, out_shape=(jax.ShapeDtypeStruct((2,), F32),...  11.4 us

profile of v8, /device:TPU:0, one launch (start us, length us, event | category | flops | bytes accessed | tf_op | source)
XLA Modules:
  0.0 126.3 jit_solution(16487120233780098739)
XLA Ops:
  0.7 0.0 copy-start
  0.7 0.0 copy-start.1
  0.7 0.0 copy-start.2
  0.7 0.0 copy-start.3
  0.7 0.0 copy-start.4
  0.7 0.0 copy-start.5
  0.7 0.0 copy-start.6
  0.7 113.9 %reduce_and_precondition.1 = (f32[38,2,2,2,2,2,16,256]{7,6,5,4,3,2,1,0:T(8,128)S(1)}, f32[24,512]{1,0:T(8,128)S(1)}, bf16[9216,512]{1,0:T(8,128)(2,1)S(1)}) custom-call(s32[12]{0:T(128)} %micro_hbm.1, s32[12]{0:T(128)} %labels_hbm.1, bf16[12,8,8,512]{3,2,1,0:T(8,128)(2,1)} %images_hbm.1, f32[1,512]{1,0:T(1,128)} %bitcast.17, f32[1,512]{1,0:T(1,128)} %bitcast.19, ...), custom_call_target="tpu_custom_call" | custom-call | tf_op jit(solution)/shard_map/reduce_and_precondition/pallas_call | solution.py:1046
  114.6 0.0 copy-done
  114.6 0.0 copy-done.1
  114.7 0.0 copy-done.2
  114.7 0.0 copy-done.3
  114.7 0.0 copy-done.4
  114.7 0.0 copy-done.5
  114.7 0.0 copy-done.6
  114.7 11.4 %adamw.1 = (f32[2]{0:T(128)}, f32[1]{0:T(128)}, f32[2,512]{1,0:T(2,128)}, f32[2,512]{1,0:T(2,128)}, f32[2,512]{1,0:T(2,128)}, /*index=5*/f32[10,513]{1,0:T(8,128...) custom-call(f32[24,512]{1,0:T(8,128)S(1)} %get-tuple-element.27.fact, ...), custom_call_target="tpu_custom_call" | custom-call | tf_op jit(solution)/shard_map/adamw/pallas_call | solution.py:1075
Async XLA Ops:
  0.7 114.0 %copy-start = (f32[513,10]{0,1:T(8,128)S(1)}, f32[513,10]{0,1:T(8,128)}, u32[]{:S(2)}) copy-start(f32[513,10]{0,1:T(8,128)} %param.29) | copy-start | bytes 61564
  0.7 114.0 %copy-start.1 = (f32[513,10]{0,1:T(8,128)S(1)}, f32[513,10]{0,1:T(8,128)}, u32[]{:S(2)}) copy-start(f32[513,10]{0,1:T(8,128)} %param.30) | copy-start | bytes 61564
  0.7 114.0 %copy-start.2 = (f32[513,10]{0,1:T(8,128)S(1)}, f32[513,10]{0,1:T(8,128)}, u32[]{:S(2)}) copy-start(f32[513,10]{0,1:T(8,128)} %param.31) | copy-start | bytes 61564
  0.7 114.0 %copy-start.3 = (f32[512]{0:T(512)S(1)}, f32[512]{0:T(512)}, u32[]{:S(2)}) copy-start(f32[512]{0:T(512)} %param.25) | copy-start | bytes 6148
  0.7 114.0 %copy-start.4 = (f32[512]{0:T(512)S(1)}, f32[512]{0:T(512)}, u32[]{:S(2)}) copy-start(f32[512]{0:T(512)} %param.26) | copy-start | bytes 6148
  0.7 114.0 %copy-start.5 = (f32[2,512]{1,0:T(2,128)S(1)}, f32[2,512]{1,0:T(2,128)}, u32[]{:S(2)}) copy-start(f32[2,512]{1,0:T(2,128)} %norm_first.1) | copy-start | bytes 12292
  0.7 114.0 %copy-start.6 = (f32[2,512]{1,0:T(2,128)S(1)}, f32[2,512]{1,0:T(2,128)}, u32[]{:S(2)}) copy-start(f32[2,512]{1,0:T(2,128)} %norm_second.1) | copy-start | bytes 12292
